TPU v7x, 32 devices: a whole 2x2x4 slice. The times are simulated.
32 devices in a mesh: seq: 8 (over z, x), tp: 4 (over y, core).
Axes of the slice: x: 2, y: 2, z: 4, core: 2. Of those that a mesh axis runs over, the one named last changes fastest.
Arguments:
- layer_in: bfloat16 [2, 2048, 2, 512], P(None, 'seq'), may hold values from -6 to 6
- cotangent: bfloat16 [2, 2048, 2, 512], P(None, 'seq'), may hold values from -6 to 6
- clip_of_frame: int32 [2, 2], replicated, may hold values from 0 to 1, as said below
- w_query: bfloat16 [2, 512, 512], P(None, None, 'tp'), may hold values from -0.375 to 0.375
- w_key: bfloat16 [2, 512, 512], P(None, None, 'tp'), may hold values from -0.375 to 0.375
- w_value: bfloat16 [2, 512, 512], P(None, None, 'tp'), may hold values from -0.25 to 0.25
- w_out: bfloat16 [2, 512, 512], P(None, 'tp'), may hold values from -1.796875 to 1.796875
- w_up: bfloat16 [2, 512, 2048], P(None, None, 'tp'), may hold values from -0.25 to 0.25
- w_down: bfloat16 [2, 2048, 512], P(None, 'tp'), may hold values from -0.125 to 0.125
- norm1_gain: float32 [2, 512], replicated, may hold values from 0.5 to 1.5
- norm1_bias: float32 [2, 512], replicated, may hold values from -3 to 3
- norm2_gain: float32 [2, 512], replicated, may hold values from 0.5 to 1.5
- norm2_bias: float32 [2, 512], replicated, may hold values from -3 to 3
Outputs:
- layer_out: bfloat16 [2, 2048, 2, 512], P(None, 'seq')
- input_grad: bfloat16 [2, 2048, 2, 512], P(None, 'seq')
- grad_query: float32 [2, 512, 512], P(None, None, 'tp')
- grad_key: float32 [2, 512, 512], P(None, None, 'tp')
- grad_value: float32 [2, 512, 512], P(None, None, 'tp')
- grad_out: float32 [2, 512, 512], P(None, 'tp')
- grad_up: float32 [2, 512, 2048], P(None, None, 'tp')
- grad_down: float32 [2, 2048, 512], P(None, 'tp')
- grad_gain1: float32 [2, 512], replicated
- grad_bias1: float32 [2, 512], replicated
- grad_gain2: float32 [2, 512], replicated
- grad_bias2: float32 [2, 512], replicated
Inputs may be any that keep to these rules, and one draw needn't show every extreme that they name: `clip_of_frame`: in each stream clip numbers never fall; frames with equal numbers form one clip, and a clip's number is the index of its first frame. The last frame of one stream always starts a clip of its own; in the other stream, chosen from the seed, all 2 frames form a single clip.
All inputs are finite; a program needn't handle non-finite values.
Results may differ from a plain program's by a relative error of at most 0.024.
Values may be sent and summed in bfloat16 or wider, within the bound.
No kernel may reach another device: no remote copies, remote signals or barrier semaphores. Data moves between devices by JAX's collectives and lax.ppermute only.
A program may use at most 256 MiB of HBM per device.

v0:
```python
from functools import partial
import math

import jax
import jax.numpy as jnp
from jax import lax
from jax.sharding import PartitionSpec as P

HEAD_DIM = 64
FRAME = 1024


def layer_norm(inputs, gain, bias):
    center = inputs - jnp.mean(inputs, axis=-1, keepdims=True)
    spread = jnp.mean(center * center, axis=-1, keepdims=True)
    return center * lax.rsqrt(spread + 1e-05) * gain + bias


def clip_lookup(clip_table, positions):
    frames = positions // FRAME
    marks = frames[:, None] == jnp.arange(clip_table.shape[1], dtype=jnp.int32)[None, :]
    return jnp.sum(jnp.where(marks[None, :, :], clip_table[:, None, :], 0), axis=-1)


def clip_mask(query_ids, key_ids):
    return (query_ids[:, :, None] == key_ids[:, None, :])[:, None, :, :]


def raw_scores(query_four, key_four, score_scale):
    return (
        jnp.einsum("qshe,kshe->shqk", query_four, key_four, preferred_element_type=jnp.float32)
        * score_scale
    )


def score_grads(
    query_four, key_four, value_four, dout_four, lse_heads, delta_heads, same_clip, score_scale
):
    scores = raw_scores(query_four, key_four, score_scale)
    probs = jnp.where(same_clip, jnp.exp(scores - lse_heads[..., None]), 0.0)
    dprobs = jnp.einsum(
        "qshe,kshe->shqk", dout_four, value_four, preferred_element_type=jnp.float32
    )
    dscores = (probs * (dprobs - delta_heads[..., None])).astype(jnp.bfloat16)
    return (probs.astype(jnp.bfloat16), dscores)


def outer_sum(left, right):
    return lax.dot_general(
        left, right, (((0,), (0,)), ((), ())), preferred_element_type=jnp.float32
    )


def back_matmul(grads, weight):
    return lax.dot_general(
        grads, weight, (((1,), (1,)), ((), ())), preferred_element_type=jnp.float32
    )


def net_pass(
    net_input,
    net_cot,
    clip_table,
    wq_in,
    wk_in,
    wv_in,
    wo_in,
    wu_in,
    wd_in,
    gain_one,
    bias_one,
    gain_two,
    bias_two,
):
    segment, streams, features = net_input.shape
    row_count = segment * streams
    local_width = wq_in.shape[1]
    local_heads = local_width // HEAD_DIM
    score_scale = 1.0 / math.sqrt(HEAD_DIM)
    four_shape = (segment, streams, local_heads, HEAD_DIM)
    inputs = net_input.astype(jnp.float32).reshape(row_count, features)
    cot_low = net_cot.reshape(row_count, features)
    first_pos = lax.axis_index("seq") * segment
    local_ids = clip_lookup(clip_table, first_pos + jnp.arange(segment, dtype=jnp.int32))
    normed = layer_norm(inputs, gain_one, bias_one)
    normed_low = normed.astype(jnp.bfloat16)
    query_low = jnp.dot(normed_low, wq_in, preferred_element_type=jnp.float32).astype(jnp.bfloat16)
    key_low = jnp.dot(normed_low, wk_in, preferred_element_type=jnp.float32).astype(jnp.bfloat16)
    value_low = jnp.dot(normed_low, wv_in, preferred_element_type=jnp.float32).astype(jnp.bfloat16)
    query_four = query_low.reshape(four_shape)
    key_local = key_low.reshape(segment, streams, local_width)
    value_local = value_low.reshape(segment, streams, local_width)
    run_max = jnp.full((streams, local_heads, segment), -1e30, jnp.float32)
    key_part = lax.all_gather(key_local, "seq", axis=0, tiled=True)
    value_part = lax.all_gather(value_local, "seq", axis=0, tiled=True)
    amount = key_part.shape[0]
    key_part4 = key_part.reshape(amount, streams, local_heads, HEAD_DIM)
    value_part4 = value_part.reshape(amount, streams, local_heads, HEAD_DIM)
    same_clip = clip_mask(local_ids, clip_lookup(clip_table, jnp.arange(amount, dtype=jnp.int32)))
    scores = raw_scores(query_four, key_part4, score_scale)
    new_max = jnp.maximum(run_max, jnp.max(jnp.where(same_clip, scores, -1e30), axis=-1))
    weights = jnp.where(same_clip, jnp.exp(scores - new_max[..., None]), 0.0)
    run_sum = jnp.sum(weights, axis=-1)
    accum = jnp.einsum(
        "shqk,kshe->qshe",
        weights.astype(jnp.bfloat16),
        value_part4,
        preferred_element_type=jnp.float32,
    )
    run_max, run_sum, accum = (new_max, run_sum, accum)
    attended = accum / jnp.transpose(run_sum, (2, 0, 1))[..., None]
    lse_heads = run_max + jnp.log(run_sum)
    attended_low = attended.astype(jnp.bfloat16).reshape(row_count, local_width)
    attn_part = jnp.dot(attended_low, wo_in, preferred_element_type=jnp.float32)
    middle = inputs + lax.psum(attn_part.astype(jnp.bfloat16), "tp").astype(jnp.float32)
    second_low = layer_norm(middle, gain_two, bias_two).astype(jnp.bfloat16)
    hidden_pre = jnp.dot(second_low, wu_in, preferred_element_type=jnp.float32)
    gelu_tanh = partial(jax.nn.gelu, approximate=True)
    hidden_low = gelu_tanh(hidden_pre).astype(jnp.bfloat16)
    mlp_part = jnp.dot(hidden_low, wd_in, preferred_element_type=jnp.float32)
    output_low = (
        middle + lax.psum(mlp_part.astype(jnp.bfloat16), "tp").astype(jnp.float32)
    ).astype(jnp.bfloat16)
    result = output_low.reshape(segment, streams, features)
    grad_down = outer_sum(hidden_low, cot_low)
    hidden_grad = back_matmul(cot_low, wd_in)
    gelu_value, gelu_back = jax.vjp(gelu_tanh, hidden_pre)
    pre_grad = gelu_back(hidden_grad)[0].astype(jnp.bfloat16)
    grad_up = outer_sum(second_low, pre_grad)
    second_part = back_matmul(pre_grad, wu_in)
    second_grad = lax.psum(second_part.astype(jnp.bfloat16), "tp").astype(jnp.float32)
    norm_value, norm_two_back = jax.vjp(layer_norm, middle, gain_two, bias_two)
    middle_part, grad_gain2, grad_bias2 = norm_two_back(second_grad)
    middle_grad = cot_low.astype(jnp.float32) + middle_part
    branch_low = middle_grad.astype(jnp.bfloat16)
    grad_out = outer_sum(attended_low, branch_low)
    dout_low = back_matmul(branch_low, wo_in).astype(jnp.bfloat16)
    dout_four = dout_low.reshape(four_shape)
    delta_rows = jnp.sum(dout_four.astype(jnp.float32) * attended, axis=-1)
    delta_heads = jnp.transpose(delta_rows, (1, 2, 0))
    zero_four = jnp.zeros(four_shape, jnp.float32)
    key_whole, value_whole = (
        lax.all_gather(key_local, "seq", axis=0, tiled=True),
        lax.all_gather(value_local, "seq", axis=0, tiled=True),
    )
    key_total = key_whole.shape[0]
    key_block = segment * max(1, min(key_total // segment, 1024 // segment))

    def query_step(block_index, query_acc):
        offset = block_index * key_block
        key_part = lax.dynamic_slice_in_dim(key_whole, offset, key_block, 0).reshape(
            key_block, streams, local_heads, HEAD_DIM
        )
        value_part = lax.dynamic_slice_in_dim(value_whole, offset, key_block, 0).reshape(
            key_block, streams, local_heads, HEAD_DIM
        )
        same_clip = clip_mask(
            local_ids, clip_lookup(clip_table, offset + jnp.arange(key_block, dtype=jnp.int32))
        )
        probs_low, dscores = score_grads(
            query_four,
            key_part,
            value_part,
            dout_four,
            lse_heads,
            delta_heads,
            same_clip,
            score_scale,
        )
        return query_acc + score_scale * jnp.einsum(
            "shqk,kshe->qshe", dscores, key_part, preferred_element_type=jnp.float32
        )

    query_grad = lax.fori_loop(0, key_total // key_block, query_step, zero_four)
    amount = segment * lax.axis_size("seq")
    key_part = key_whole.reshape(amount, streams, local_heads, HEAD_DIM)
    value_part = value_whole.reshape(amount, streams, local_heads, HEAD_DIM)
    same_clip = clip_mask(local_ids, clip_lookup(clip_table, jnp.arange(amount, dtype=jnp.int32)))
    probs_low, dscores = score_grads(
        query_four, key_part, value_part, dout_four, lse_heads, delta_heads, same_clip, score_scale
    )
    key_term = score_scale * jnp.einsum(
        "shqk,qshe->kshe", dscores, query_four, preferred_element_type=jnp.float32
    )
    value_term = jnp.einsum(
        "shqk,qshe->kshe", probs_low, dout_four, preferred_element_type=jnp.float32
    )
    both_grads = lax.psum_scatter(
        jnp.concatenate(
            [
                key_term.reshape(amount, streams, local_width),
                value_term.reshape(amount, streams, local_width),
            ],
            axis=-1,
        ).astype(jnp.bfloat16),
        "seq",
        scatter_dimension=0,
        tiled=True,
    ).astype(jnp.float32)
    key_grad = both_grads[..., :local_width]
    value_grad = both_grads[..., local_width:]
    query_grad_low = query_grad.reshape(row_count, local_width).astype(jnp.bfloat16)
    key_grad_low = key_grad.reshape(row_count, local_width).astype(jnp.bfloat16)
    value_grad_low = value_grad.reshape(row_count, local_width).astype(jnp.bfloat16)
    grad_query = outer_sum(normed_low, query_grad_low)
    grad_key = outer_sum(normed_low, key_grad_low)
    grad_value = outer_sum(normed_low, value_grad_low)
    normed_part = (
        back_matmul(query_grad_low, wq_in)
        + back_matmul(key_grad_low, wk_in)
        + back_matmul(value_grad_low, wv_in)
    )
    normed_grad = lax.psum(normed_part.astype(jnp.bfloat16), "tp").astype(jnp.float32)
    norm_first, norm_one_back = jax.vjp(layer_norm, inputs, gain_one, bias_one)
    input_part, grad_gain1, grad_bias1 = norm_one_back(normed_grad)
    grad_in_low = (middle_grad + input_part).astype(jnp.bfloat16)
    grad_in = grad_in_low.reshape(segment, streams, features)
    gradients = (
        grad_query,
        grad_key,
        grad_value,
        grad_out,
        grad_up,
        grad_down,
        grad_gain1,
        grad_bias1,
        grad_gain2,
        grad_bias2,
    )
    return (result, grad_in, gradients)


def body(
    layer_in,
    cotangent,
    clip_of_frame,
    w_query,
    w_key,
    w_value,
    w_out,
    w_up,
    w_down,
    norm1_gain,
    norm1_bias,
    norm2_gain,
    norm2_bias,
):
    results = []
    for net_index in range(2):
        result, grad_in, found = net_pass(
            layer_in[net_index],
            cotangent[net_index],
            clip_of_frame,
            w_query[net_index],
            w_key[net_index],
            w_value[net_index],
            w_out[net_index],
            w_up[net_index],
            w_down[net_index],
            norm1_gain[net_index],
            norm1_bias[net_index],
            norm2_gain[net_index],
            norm2_bias[net_index],
        )
        summed = (
            lax.psum(found[0].astype(jnp.bfloat16), "seq").astype(jnp.float32),
            lax.psum(found[1].astype(jnp.bfloat16), "seq").astype(jnp.float32),
            lax.psum(found[2].astype(jnp.bfloat16), "seq").astype(jnp.float32),
            lax.psum(found[3].astype(jnp.bfloat16), "seq").astype(jnp.float32),
            lax.psum(found[4].astype(jnp.bfloat16), "seq").astype(jnp.float32),
            lax.psum(found[5].astype(jnp.bfloat16), "seq").astype(jnp.float32),
            lax.psum(found[6].astype(jnp.bfloat16), "seq").astype(jnp.float32),
            lax.psum(found[7].astype(jnp.bfloat16), "seq").astype(jnp.float32),
            lax.psum(found[8].astype(jnp.bfloat16), "seq").astype(jnp.float32),
            lax.psum(found[9].astype(jnp.bfloat16), "seq").astype(jnp.float32),
        )
        results.append((result, grad_in, summed))
    layer_out = jnp.stack([results[0][0], results[1][0]], axis=0)
    input_grad = jnp.stack([results[0][1], results[1][1]], axis=0)
    stacked = [jnp.stack([results[0][2][slot], results[1][2][slot]], axis=0) for slot in range(10)]
    return (
        layer_out,
        input_grad,
        stacked[0],
        stacked[1],
        stacked[2],
        stacked[3],
        stacked[4],
        stacked[5],
        stacked[6],
        stacked[7],
        stacked[8],
        stacked[9],
    )


def solution(mesh):
    placed = (
        P(None, "seq", None, None),
        P(None, "seq", None, None),
        P(),
        P(None, None, "tp"),
        P(None, None, "tp"),
        P(None, None, "tp"),
        P(None, "tp", None),
        P(None, None, "tp"),
        P(None, "tp", None),
        P(),
        P(),
        P(),
        P(),
    )
    return jax.shard_map(
        body,
        mesh=mesh,
        in_specs=placed,
        out_specs=(
            P(None, "seq", None, None),
            P(None, "seq", None, None),
            P(None, None, "tp"),
            P(None, None, "tp"),
            P(None, None, "tp"),
            P(None, "tp", None),
            P(None, None, "tp"),
            P(None, "tp", None),
            P(),
            P(),
            P(),
            P(),
        ),
        check_vma=False,
    )
```

profile of v0, /device:TPU:0, one launch (start us, length us, event | category | flops | bytes accessed | tf_op | source)
XLA Modules:
  0.0 727.2 jit_solution(16172148787605729522)
XLA Ops:
  8.8 2.1 convert_reduce_fusion.1
  10.9 3.8 multiply_reduce_fusion.3
  15.4 2.0 add_convert_fusion.7
  25.2 2.0 slice_convert_fusion.1
  28.7 2.7 fusion.187
  32.1 30.0 %all-gather.7.cloned.1.call-done = bf16[2048,2,128]{0,2,1:T(8,128)(2,1)} async-done(((bf16[256,2,128]{0,2,1:T(8,128)(2,1)}), bf16[2048,2,128]{0,2,1:T(8,128)(2,1)}) %all-gather.7.cloned.1.call-update) | async-done | bytes 1048592 | tf_op jit(solution)/shard_map/all_gather | solution.py:94
  62.2 6.4 select_reduce_fusion.3
  68.6 34.7 %all-gather.11.cloned.1.call-done = bf16[2048,2,128]{0,2,1:T(8,128)(2,1)} async-done(((bf16[256,2,128]{0,2,1:T(8,128)(2,1)}), bf16[2048,2,128]{0,2,1:T(8,128)(2,1)}) %all-gather.11.cloned.1.call-update) | async-done | bytes 1048592 | tf_op jit(solution)/shard_map/all_gather | solution.py:94
  103.2 7.0 fusion.20
  110.3 3.2 copy-done.14
  113.5 2.6 fusion.22
  116.1 28.3 %all-gather.9.cloned.1.call-done = bf16[2048,2,128]{0,2,1:T(8,128)(2,1)} async-done(((bf16[256,2,128]{0,2,1:T(8,128)(2,1)}), bf16[2048,2,128]{0,2,1:T(8,128)(2,1)}) %all-gather.9.cloned.1.call-update) | async-done | bytes 1048592 | tf_op jit(solution)/shard_map/all_gather | solution.py:95
  144.4 6.3 fusion.192
  151.0 33.7 %all-gather.5.cloned.1.call-done = bf16[2048,2,128]{0,2,1:T(8,128)(2,1)} async-done(((bf16[256,2,128]{0,2,1:T(8,128)(2,1)}), bf16[2048,2,128]{0,2,1:T(8,128)(2,1)}) %all-gather.5.cloned.1.call-update) | async-done | bytes 1048592 | tf_op jit(solution)/shard_map/all_gather | solution.py:95
  184.7 6.3 fusion.193
  193.1 2.0 convolution_convert_fusion.9
  195.1 2.0 convolution_convert_fusion.8
  202.6 2.1 reshape_squeeze.6
  211.7 20.5 %all-reduce.22.cloned.1.call-done = (bf16[512,512]{1,0:T(8,128)(2,1)}, bf16[512,512]{1,0:T(8,128)(2,1)}) async-done(((bf16[512,512]{1,0:T(8,128)(2,1)}, bf16[512,512]{1,0:T(8,128)(2,1)}), (bf16[512,512]{1,0:T(8,128)(2,1)}, bf16[512,512]{1,0:T(8,128)(2,1)})) %all-reduce.22.cloned.1.call-update) | async-done | bytes 1048592 | tf_op jit(solution)/shard_map/psum | solution.py:115
  235.4 2.1 fusion.101
  248.0 2.6 fusion.58
  251.9 31.2 %all-reduce.20.cloned.1.call-done = (bf16[512,512]{1,0:T(8,128)(2,1)}, bf16[512,512]{1,0:T(8,128)(2,1)}) async-done(((bf16[512,512]{1,0:T(8,128)(2,1)}, bf16[512,512]{1,0:T(8,128)(2,1)}), (bf16[512,512]{1,0:T(8,128)(2,1)}, bf16[512,512]{1,0:T(8,128)(2,1)})) %all-reduce.20.cloned.1.call-update) | async-done | bytes 1048592 | tf_op jit(solution)/shard_map/psum | solution.py:131
  283.1 2.2 fusion.86
  285.3 2.2 fusion.84
  300.2 7.0 fusion.40
  307.2 8.4 %fusion.38 = bf16[2,2,64,2048]{3,2,1,0:T(8,128)(2,1)} fusion(bf16[256,2,2,64]{0,3,2,1:T(8,128)(2,1)S(1)} %copy.87, f32[2,2,256,2048]{3,2,1,0:T(8,128)} %get-tuple-element.749, bf16[256,2,2,64]{0,3,2,1:T(8,128)(2,1)S(1)} %copy.95, bf16[2048,2,2,64]{0,3,2,1:T(8,128)(2,1)} %bitcast.305, f32[2,2,256]{2,1,0:T(2,128)} %bitcast.348, ...), kind=kOutput, calls=%fused_computation.70 | convolution fusion | flops 550502400 | bytes 11804672 | tf_op jit(solution)/shard_map/shqk,qshe->kshe/dot_general | solution.py:182
  317.2 6.9 fusion.43
  324.1 8.4 %fusion.39 = bf16[2,2,64,2048]{3,2,1,0:T(8,128)(2,1)} fusion(bf16[256,2,2,64]{0,3,2,1:T(8,128)(2,1)S(1)} %copy.91, f32[2,2,256,2048]{3,2,1,0:T(8,128)} %copy-done.14, bf16[256,2,2,64]{0,3,2,1:T(8,128)(2,1)S(1)} %copy-done.44, bf16[2048,2,2,64]{0,3,2,1:T(8,128)(2,1)} %bitcast.308, f32[2,2,256]{2,1,0:T(2,128)} %bitcast.350, f32[2,2,256]{2,1,0:T(2,128)} %log_add_fusion, ...), kind=kOutput, calls=%fused_computation.71 | convolution fusion | flops 550502400 | bytes 11804672 | tf_op jit(solution)/shard_map/shqk,qshe->kshe/dot_general | solution.py:182
  332.5 2.4 copy.110
  334.9 3.7 copy.109
  338.6 3.7 copy.101
  342.2 3.7 copy.100
  345.9 4.8 pad_maximum_fusion.1
  350.7 3.3 pad_maximum_fusion
  354.0 21.0 %while.33 = (s32[]{:T(128)}, f32[256,2,2,64]{0,3,2,1:T(8,128)}, bf16[2048,2,128]{0,2,1:T(8,128)(2,1)}, s32[2,256]{1,0:T(2,128)S(1)}, s32[2,2]{1,0:T(2,128)S(1)},...) while((s32[]{:T(128)}, f32[256,2,2,64]{0,3,2,1:T(8,128)}, ...), condition=%wide.region_35.36_spmd.clone, body=%wide.region_33.35_spmd.clone.sunk | while | flops 409690112 | bytes 13932765 | solution.py:174
  356.6 2.7 fusion.286
  359.3 5.6 fusion.287
  367.5 2.7 fusion.286
  370.2 4.9 fusion.287
  376.3 20.4 %while.32 = (s32[]{:T(128)}, f32[256,2,2,64]{0,3,2,1:T(8,128)}, bf16[2048,2,128]{0,2,1:T(8,128)(2,1)}, s32[2,256]{1,0:T(2,128)S(1)}, s32[2,2]{1,0:T(2,128)S(1)},...) while((s32[]{:T(128)}, f32[256,2,2,64]{0,3,2,1:T(8,128)}, ...), condition=%wide.region_24.25_spmd.clone, body=%wide.region_22.24_spmd.clone.sunk | while | flops 409690112 | bytes 14457081 | solution.py:174
  379.0 2.7 fusion.279
  381.7 4.9 fusion.280
  389.2 2.7 fusion.279
  391.9 4.9 fusion.280
  399.3 2.2 fusion.132
  401.4 109.7 %all-reduce.16.cloned.1.call-done = (bf16[2048,2,256]{2,1,0:T(2,128)(2,1)}, bf16[2048,2,256]{2,1,0:T(2,128)(2,1)}) async-done(((bf16[2048,2,256]{2,1,0:T(2,128)(2,1)}, bf16[2048,2,256]{2,1,0:T(2,128)(2,1)}), (bf16[2048,2,256]{2,1,0:T(2,128)(2,1)}, bf16[2048,2,256]{2,1,0:T(2,128)(2,1)})) %all-reduce.16.cloned.1.call-update) | async-done | bytes 4194320
  515.1 2.0 fusion.46
  518.9 2.0 fusion.73
  528.0 2.0 fusion.72
  530.1 1.9 fusion.66
  533.0 1.9 fusion.68
  537.0 32.7 %all-reduce.18.cloned.1.call-done = (bf16[512,512]{1,0:T(8,128)(2,1)}, bf16[512,512]{1,0:T(8,128)(2,1)}, bf16[512,512]{1,0:T(8,128)(2,1)}, bf16[512,512]{1,0:T(8,128)(2,1)}) async-done(((bf16[512,512]{1,0:T(8,128)(2,1)}, bf16[512,512]{1,0:T(8,128)(2,1)}, bf16[512,512]{1,0:T(8,128)(2,1)}, bf16[512,512]{1,0:T(8,128)(2,1)}), (bf16[512,512]{1,0:T(8,128)(2,1)}, bf16[512,512]{1,0:T(8,128)(2,1)}, ...) | async-done | bytes 2097168 | tf_op jit(solution)/shard_map/psum | solution.py:122
  569.7 2.5 add_convert_fusion.2
  572.2 2.1 stack_reshape.13
  579.4 2.3 fusion.85
  581.7 3.2 add_convert_fusion.1
  586.3 2.5 add_convert_fusion
  591.3 39.2 %all-reduce.2 = (bf16[1,512]{1,0:T(2,128)(2,1)S(1)}, bf16[1,512]{1,0:T(2,128)(2,1)S(1)}, bf16[1,512]{1,0:T(2,128)(2,1)S(1)}, bf16[1,512]{1,0:T(2,128)(2,1)S(1)},...) all-reduce(bf16[1,512]{1,0:T(2,128)(2,1)S(1)} %stack.173, ...), channel_id=1, replica_groups=mesh['seq'=8,'tp'=4] {'seq'}, use_global_device_ids=true, to_apply=%region_55.56 | all-reduce | flops 4096 | bytes 16384 | tf_op jit(solution)/shard_map/psum | solution.py:272
  632.9 2.5 pad_maximum_fusion.3
  635.4 2.5 pad_maximum_fusion.2
  637.9 72.8 %all-reduce.14.cloned.1.call-done = (bf16[1,512,128]{2,1,0:T(8,128)(2,1)}, bf16[1,512,128]{2,1,0:T(8,128)(2,1)}, bf16[1,512,128]{2,1,0:T(8,128)(2,1)}, bf16[1,51...) async-done(((bf16[1,512,128]{2,1,0:T(8,128)(2,1)}, ...) | async-done | bytes 3145744 | tf_op jit(solution)/shard_map/psum | solution.py:266
  712.5 1.8 maximum_convert_fusion.5
  714.3 2.1 maximum_convert_fusion.2
  716.4 3.8 maximum_convert_fusion
  (298 shorter events, 98.1 us)
Async XLA Ops:
  7.2 8.2 %copy-start.8 = (bf16[2,256,2,512]{3,2,1,0:T(2,128)(2,1)S(1)}, bf16[2,256,2,512]{3,2,1,0:T(2,128)(2,1)}, u32[]{:S(2)}) copy-start(bf16[2,256,2,512]{3,2,1,0:T(2,128)(2,1)} %param.17) | copy-start | bytes 3145732
  7.2 55.0 %all-gather.7.cloned.1.call-start = ((), (), s32[]{:S(2)}) async-start(), calls=%async_computation.1 | async-start | bytes 1179648 | tf_op jit(solution)/shard_map/all_gather | solution.py:94
  14.7 7.6 %copy-start.34 = (bf16[2,512,128]{2,1,0:T(8,128)(2,1)S(1)}, bf16[2,512,128]{2,1,0:T(8,128)(2,1)}, u32[]{:S(2)}) copy-start(bf16[2,512,128]{2,1,0:T(8,128)(2,1)} %param.22) | copy-start | bytes 786436
  15.4 9.2 %copy-start.39 = (bf16[2,512,128]{2,1,0:T(8,128)(2,1)S(1)}, bf16[2,512,128]{2,1,0:T(8,128)(2,1)}, u32[]{:S(2)}) copy-start(bf16[2,512,128]{2,1,0:T(8,128)(2,1)} %param.20) | copy-start | bytes 786436
  17.6 9.6 %copy-start.4 = (bf16[512,512]{1,0:T(8,128)(2,1)}, bf16[512,512]{1,0:T(8,128)(2,1)S(1)}, u32[]{:S(2)}) copy-start(bf16[512,512]{1,0:T(8,128)(2,1)S(1)} %convert_element_type.334) | copy-start | bytes 1572868
  19.8 83.5 %all-gather.11.cloned.1.call-start = ((), (), s32[]{:S(2)}) async-start(), calls=%async_computation.3 | async-start | bytes 1179648 | tf_op jit(solution)/shard_map/all_gather | solution.py:94
  20.0 8.2 %copy-start.6 = (bf16[512,512]{1,0:T(8,128)(2,1)}, bf16[512,512]{1,0:T(8,128)(2,1)S(1)}, u32[]{:S(2)}) copy-start(bf16[512,512]{1,0:T(8,128)(2,1)S(1)} %convert_element_type.351) | copy-start | bytes 1572868
  20.0 7.3 copy-start.64
  20.0 7.9 %copy-start.46 = (s32[2,2]{1,0:T(2,128)S(1)}, s32[2,2]{1,0:T(2,128)}, u32[]{:S(2)}) copy-start(s32[2,2]{1,0:T(2,128)} %param.19) | copy-start | bytes 52
  22.2 122.1 %all-gather.9.cloned.1.call-start = ((), (), s32[]{:S(2)}) async-start(), calls=%async_computation.2 | async-start | bytes 1179648 | tf_op jit(solution)/shard_map/all_gather | solution.py:95
  23.4 161.3 %all-gather.5.cloned.1.call-start = ((), (), s32[]{:S(2)}) async-start(), calls=%async_computation | async-start | bytes 1179648 | tf_op jit(solution)/shard_map/all_gather | solution.py:95
  24.5 207.7 %all-reduce.22.cloned.1.call-start = ((), (), s32[]{:S(2)}) async-start(), calls=%async_computation.8 | async-start | bytes 2097152 | tf_op jit(solution)/shard_map/psum | solution.py:115
  32.1 152.6 %copy-start.12 = (pred[2,256,2048]{2,1,0:T(8,128)(4,1)}, pred[2,256,2048]{2,1,0:T(8,128)(4,1)S(1)}, u32[]{:S(2)}) copy-start(pred[2,256,2048]{2,1,0:T(8,128)(4,1)S(1)} %broadcast_compare_fusion.2) | copy-start | bytes 3145732
  68.6 41.7 %copy-start.47 = (f32[2,2,256]{2,1,0:T(2,128)}, f32[2,2,256]{2,1,0:T(2,128)S(1)}, u32[]{:S(2)}) copy-start(f32[2,2,256]{2,1,0:T(2,128)S(1)} %get-tuple-element.748) | copy-start | bytes 12292
  110.2 5.9 copy-start.56
  110.2 74.5 %copy-start.63 = (f32[2,2,256]{2,1,0:T(2,128)}, f32[2,2,256]{2,1,0:T(2,128)S(1)}, u32[]{:S(2)}) copy-start(f32[2,2,256]{2,1,0:T(2,128)S(1)} %get-tuple-element.634) | copy-start | bytes 12292
  116.1 34.6 %copy-start.55 = (f32[2,2,256]{2,1,0:T(2,128)}, f32[2,2,256]{2,1,0:T(2,128)S(1)}, u32[]{:S(2)}) copy-start(f32[2,2,256]{2,1,0:T(2,128)S(1)} %fusion.22) | copy-start | bytes 12292
  151.0 44.1 %copy-start.30 = (bf16[512,128]{1,0:T(8,128)(2,1)}, bf16[512,128]{1,0:T(8,128)(2,1)S(1)}, u32[]{:S(2)}) copy-start(bf16[512,128]{1,0:T(8,128)(2,1)S(1)} %reshape.815) | copy-start | bytes 393220
  191.0 14.6 %copy-start.23 = (f32[1,256,2,512]{3,2,1,0:T(2,128)S(1)}, f32[1,256,2,512]{3,2,1,0:T(2,128)}, u32[]{:S(2)}) copy-start(f32[1,256,2,512]{3,2,1,0:T(2,128)} %get-tuple-element.728) | copy-start | bytes 3145732
  191.0 15.4 %copy-start.22 = (f32[1,256,2,512]{3,2,1,0:T(2,128)S(1)}, f32[1,256,2,512]{3,2,1,0:T(2,128)}, u32[]{:S(2)}) copy-start(f32[1,256,2,512]{3,2,1,0:T(2,128)} %get-tuple-element.729) | copy-start | bytes 3145732
  193.0 12.6 %copy-start.29 = (bf16[512,128]{1,0:T(8,128)(2,1)}, bf16[512,128]{1,0:T(8,128)(2,1)S(1)}, u32[]{:S(2)}) copy-start(bf16[512,128]{1,0:T(8,128)(2,1)S(1)} %reshape.809) | copy-start | bytes 393220
  197.1 86.0 %all-reduce.20.cloned.1.call-start = ((), (), s32[]{:S(2)}) async-start(), calls=%async_computation.7 | async-start | bytes 2097152 | tf_op jit(solution)/shard_map/psum | solution.py:131
  205.6 28.2 %copy-start.50 = (f32[1,512]{1,0:T(1,128)S(1)}, f32[1,512]{1,0:T(1,128)}, u32[]{:S(2)}) copy-start(f32[1,512]{1,0:T(1,128)} %get-tuple-element.737) | copy-start | bytes 6148
  205.6 28.2 %copy-start.60 = (f32[1,512]{1,0:T(1,128)S(1)}, f32[1,512]{1,0:T(1,128)}, u32[]{:S(2)}) copy-start(f32[1,512]{1,0:T(1,128)} %get-tuple-element.739) | copy-start | bytes 6148
  206.4 36.6 %copy-start.2 = (f32[512,512]{1,0:T(8,128)}, f32[512,512]{1,0:T(8,128)S(1)}, u32[]{:S(2)}) copy-start(f32[512,512]{1,0:T(8,128)S(1)} %reshape.822) | copy-start | bytes 3145732
  207.1 30.4 %copy-start = (f32[512,512]{1,0:T(8,128)}, f32[512,512]{1,0:T(8,128)S(1)}, u32[]{:S(2)}) copy-start(f32[512,512]{1,0:T(8,128)S(1)} %reshape.823) | copy-start | bytes 3145732
  235.4 4.9 copy-start.17
  239.1 4.0 copy-start.45
  246.3 264.9 %all-reduce.16.cloned.1.call-start = ((), (), s32[]{:S(2)}) async-start(), calls=%async_computation.5 | async-start | bytes 8388608
  246.5 4.1 copy-start.38
  246.5 4.1 copy-start.66
  283.1 6.6 copy-start.21
  283.1 8.0 %copy-start.18 = (bf16[512,512]{1,0:T(8,128)(2,1)S(1)}, bf16[512,512]{1,0:T(8,128)(2,1)}, u32[]{:S(2)}) copy-start(bf16[512,512]{1,0:T(8,128)(2,1)} %reshape_squeeze.7) | copy-start | bytes 1572868
  285.3 6.8 copy-start.41
  289.0 7.2 copy-start.11
  298.5 8.6 %copy-start.42 = (bf16[256,2,2,64]{0,3,2,1:T(8,128)(2,1)}, bf16[256,2,2,64]{0,3,2,1:T(8,128)(2,1)S(1)}, u32[]{:S(2)}) copy-start(bf16[256,2,2,64]{0,3,2,1:T(8,128)(2,1)S(1)} %copy.95) | copy-start | bytes 393220
  300.2 7.0 copy-start.13
  317.2 6.9 copy-start.44
  345.9 4.8 copy-start.25
  345.9 4.8 copy-start.26
  354.0 215.7 %all-reduce.18.cloned.1.call-start = ((), (), s32[]{:S(2)}) async-start(), calls=%async_computation.6 | async-start | bytes 4194304 | tf_op jit(solution)/shard_map/psum | solution.py:122
  377.7 4.0 copy-start.43
  387.8 4.0 copy-start.43
  398.0 113.2 %copy-start.28 = (bf16[512,128]{1,0:T(8,128)(2,1)}, bf16[512,128]{1,0:T(8,128)(2,1)S(1)}, u32[]{:S(2)}) copy-start(bf16[512,128]{1,0:T(8,128)(2,1)S(1)} %convert_element_type.372) | copy-start | bytes 393220
  511.2 5.9 copy-start.24
  511.2 5.9 copy-start.40
  511.2 6.3 copy-start.35
  512.5 4.9 copy-start.31
  517.1 9.9 %copy-start.7 = (bf16[512,512]{1,0:T(8,128)(2,1)S(1)}, bf16[512,512]{1,0:T(8,128)(2,1)}, u32[]{:S(2)}) copy-start(bf16[512,512]{1,0:T(8,128)(2,1)} %copy-done.6) | copy-start | bytes 1572868
  517.4 12.6 %copy-start.5 = (bf16[512,512]{1,0:T(8,128)(2,1)S(1)}, bf16[512,512]{1,0:T(8,128)(2,1)}, u32[]{:S(2)}) copy-start(bf16[512,512]{1,0:T(8,128)(2,1)} %copy-done.4) | copy-start | bytes 1572868
  518.6 192.1 %all-reduce.14.cloned.1.call-start = ((), (), s32[]{:S(2)}) async-start(), calls=%async_computation.4 | async-start | bytes 6291456 | tf_op jit(solution)/shard_map/psum | solution.py:266
  523.8 12.1 %copy-start.32 = (bf16[256,2,128]{2,1,0:T(2,128)(2,1)S(1)}, bf16[256,2,128]{2,1,0:T(2,128)(2,1)}, u32[]{:S(2)}) copy-start(bf16[256,2,128]{2,1,0:T(2,128)(2,1)} %copy-done.31) | copy-start | bytes 393220
  536.9 39.7 %copy-start.1 = (f32[512,512]{1,0:T(8,128)S(1)}, f32[512,512]{1,0:T(8,128)}, u32[]{:S(2)}) copy-start(f32[512,512]{1,0:T(8,128)} %copy-done) | copy-start | bytes 3145732
  536.9 39.7 %copy-start.48 = (f32[512]{0:T(512)S(1)}, f32[512]{0:T(512)}, u32[]{:S(2)}) copy-start(f32[512]{0:T(512)} %div.182) | copy-start | bytes 6148
  537.0 41.0 %copy-start.49 = (f32[512]{0:T(512)S(1)}, f32[512]{0:T(512)}, u32[]{:S(2)}) copy-start(f32[512]{0:T(512)} %div.175) | copy-start | bytes 6148
  569.7 9.6 %copy-start.58 = (f32[512]{0:T(512)S(1)}, f32[512]{0:T(512)}, u32[]{:S(2)}) copy-start(f32[512]{0:T(512)} %add.430) | copy-start | bytes 6148
  569.7 9.7 %copy-start.57 = (f32[512]{0:T(512)S(1)}, f32[512]{0:T(512)}, u32[]{:S(2)}) copy-start(f32[512]{0:T(512)} %add.424) | copy-start | bytes 6148
  572.2 5.8 copy-start.3
  572.2 9.5 %copy-start.54 = (f32[512]{0:T(512)S(1)}, f32[512]{0:T(512)}, u32[]{:S(2)}) copy-start(f32[512]{0:T(512)} %negate_multiply_fusion.3) | copy-start | bytes 6148
  579.3 6.9 copy-start.10
  579.3 6.9 copy-start.53
  584.9 6.4 copy-start.61
  584.9 6.4 copy-start.62
  586.2 49.2 %copy-start.27 = (bf16[1,256,2,512]{3,2,1,0:T(2,128)(2,1)S(1)}, bf16[1,256,2,512]{3,2,1,0:T(2,128)(2,1)}, u32[]{:S(2)}) copy-start(bf16[1,256,2,512]{3,2,1,0:T(2,128)(2,1)} %stack_reshape.13) | copy-start | bytes 1572868
  (13 other events, 24.7 us)
Sparse Core Ops, SparseCore 0:
  19.9 42.2 all-gather.6
  64.8 38.4 all-gather.10
  105.9 38.4 all-gather.8
  146.3 38.4 all-gather.4
  197.2 34.9 all-reduce.21
  246.4 36.5 all-reduce.19
  354.1 157.0 all-reduce.15
  518.7 50.9 all-reduce.17
  576.2 134.5 all-reduce.13
where the time goes:
time: 737 us; the launch traced here: 727 us
  waiting for transfers between devices  394 us (53%)
  matrix products  134 us (18%)
  other arithmetic  80.8 us (11%)
  local copies, waits for them, and re-layouts  61.9 us (8%)
  blocking collectives  39.2 us (5%)
  between operations  16 us (2%)
    unnamed x10, waiting for transfers between devices  110 us
    psum x1, waiting for transfers between devices, body(): lax.psum(found[0].astype(jnp.bfloat16), 'seq').astype(jnp.float32)  72.8 us
    all_gather x2, waiting for transfers between devices, net_pass(): key_part = lax.all_gather(key_local, 'seq', axis=0, tiled=True)  64.7 us
    all_gather x2, waiting for transfers between devices, net_pass(): value_part = lax.all_gather(value_local, 'seq', axis=0, tiled=True)  62 us
    psum x1, blocking collectives, body(): lax.psum(found[6].astype(jnp.bfloat16), 'seq').astype(jnp.float32)  39.2 us
    psum x1, waiting for transfers between devices, net_pass(): lax.psum(mlp_part.astype(jnp.bfloat16), 'tp').astype(jnp.float32)  32.7 us
    psum x1, waiting for transfers between devices, net_pass(): lax.psum(second_part.astype(jnp.bfloat16), 'tp').astype(jnp.float32)  31.2 us
    dot_general x6, matrix products, raw_scores(): jnp.einsum('qshe,kshe->shqk', query_four, key_four, preferred_element_typ...  24.2 us
  transfers between devices with their start and end apart: 9, of which 9 were waited for; matrix products, arithmetic and copies ran while one was open for 20% of the time, Pallas kernels for 0%

commit v1 on v0

v1 whole, which is shorter than its diff:
```python
import math

import jax
import jax.numpy as jnp
from jax import lax
from jax.experimental import pallas as pl
from jax.experimental.pallas import tpu as pltpu
from jax.sharding import PartitionSpec as P

HEAD_DIM = 64
EPS = 1e-05
BF = jnp.bfloat16
F32 = jnp.float32
VMEM_LIMIT = 50 * 1024 * 1024
GROUP = 4
PIECES = 8
ORDER = (0, 1, 2)
RUP, RDOWN, ROUT = 64, 64, 16
C_GELU = math.sqrt(2.0 / math.pi)


def dot(a, b, ca=1, cb=0):
    return lax.dot_general(a, b, (((ca,), (cb,)), ((), ())), preferred_element_type=F32)


def place(value):
    out = 0
    for rank, bit in enumerate(ORDER):
        out = out + ((value >> bit) & 1) * (1 << (2 - rank))
    return out


def norm_parts(v):
    center = v - jnp.mean(v, axis=-1, keepdims=True)
    inv = lax.rsqrt(jnp.mean(center * center, axis=-1, keepdims=True) + EPS)
    return center * inv, inv


def norm_back(dout, hat, inv, gain):
    e = dout * gain
    mean_e = jnp.mean(e, axis=-1, keepdims=True)
    mean_eh = jnp.mean(e * hat, axis=-1, keepdims=True)
    return (e - mean_e - hat * mean_eh) * inv


def vspec():
    return pl.BlockSpec(memory_space=pltpu.VMEM)


def sspec():
    return pl.BlockSpec(memory_space=pltpu.SMEM)


def call(kernel, outs, scalars, args, scratch=(), flops=0, nbytes=0, trans=0):
    return pl.pallas_call(
        kernel,
        out_shape=[jax.ShapeDtypeStruct(s, d) for s, d in outs],
        in_specs=[sspec()] + [vspec()] * len(args),
        out_specs=[vspec()] * len(outs),
        scratch_shapes=list(scratch),
        compiler_params=pltpu.CompilerParams(vmem_limit_bytes=VMEM_LIMIT),
        cost_estimate=pl.CostEstimate(flops=flops, bytes_accessed=nbytes, transcendentals=trans),
    )(scalars, *args)


def pick(sc, refs, scratch):
    for e in range(4):
        @pl.when(sc[0] == e)
        def _(e=e):
            scratch[...] = refs[e][...]


def project_kernel(sc, x0, x1, x2, x3, wo, wy, wc, gain, bias, qkv, w_s):
    pick(sc, (wo, wc.at[0], wy, wc.at[1]), w_s)
    g = gain[pl.ds(sc[1], 1), :]
    b = bias[pl.ds(sc[1], 1), :]
    for k, ref in enumerate((x0, x1, x2, x3)):
        hat, _ = norm_parts(ref[...].astype(F32))
        a = (hat * g + b).astype(BF)
        out = dot(a, w_s[...])
        rows = pl.ds(k * ref.shape[0], ref.shape[0])
        qkv[rows, 0:128] = (out[:, 0:128].astype(BF).astype(F32) * (1.0 / math.sqrt(HEAD_DIM))).astype(BF)
        qkv[rows, 128:384] = out[:, 128:384].astype(BF)


def attend_kernel(frames, qb, act, qkv, kvx, o_out, ot_out, lse_out, qm, vt, m_s, l_s, acc):
    n = qkv.shape[0]
    lane = lax.broadcasted_iota(jnp.int32, (n, 128), 1)
    q = qkv[:, 0:128]
    qm[0] = jnp.where(lane < HEAD_DIM, q, jnp.zeros_like(q))
    qm[1] = jnp.where(lane < HEAD_DIM, jnp.zeros_like(q), q)

    def frame_step(k, v, first):
        vt[...] = v.T
        for h in range(2):
            def block(b, _, h=h):
                cols = pl.ds(pl.multiple_of(b * qb, qb), qb)
                st = dot(k, qm[h, cols, :], 1, 1)
                top = jnp.max(st, axis=0, keepdims=True)
                if first:
                    m = top
                else:
                    old = m_s[h:h + 1, cols]
                    m = jnp.maximum(old, top)
                pt = jnp.exp(st - m)
                total = jnp.sum(pt, axis=0, keepdims=True)
                new = dot(vt[h * HEAD_DIM:(h + 1) * HEAD_DIM, :], pt.astype(BF))
                rows = slice(h * HEAD_DIM, (h + 1) * HEAD_DIM)
                if not first:
                    fix = jnp.exp(old - m)
                    total = total + l_s[h:h + 1, cols] * fix
                    new = new + acc[rows, cols] * fix
                m_s[h:h + 1, cols] = m
                l_s[h:h + 1, cols] = total
                acc[rows, cols] = new
                return 0

            lax.fori_loop(0, n // qb, block, 0)

    frame_step(qkv[:, 128:256], qkv[:, 256:384], True)
    for r in range(frames - 1):
        @pl.when(act[r + 1] != 0)
        def _(r=r):
            frame_step(kvx[r, :, 0:128], kvx[r, :, 128:256], False)

    for h in range(2):
        rows = slice(h * HEAD_DIM, (h + 1) * HEAD_DIM)
        ot_out[rows, :] = acc[rows, :] / l_s[h:h + 1, :]
        lse_out[h:h + 1, :] = m_s[h:h + 1, :] + jnp.log(l_s[h:h + 1, :])
    o_out[...] = ot_out[...].T.astype(BF)


def attend_back_kernel(frames, qb, act, qkv, kvx, do, ot, lse, dq_out, dkv_own, dkv_x, qm, dom, kt, delta, dqt, dk_s, dv_s):
    n = qkv.shape[0]
    lane = lax.broadcasted_iota(jnp.int32, (n, 128), 1)
    q = qkv[:, 0:128]
    d = do[...]
    zero = jnp.zeros_like(q)
    qm[0] = jnp.where(lane < HEAD_DIM, q, zero)
    qm[1] = jnp.where(lane < HEAD_DIM, zero, q)
    dom[0] = jnp.where(lane < HEAD_DIM, d, zero)
    dom[1] = jnp.where(lane < HEAD_DIM, zero, d)
    dt = d.astype(F32).T * ot[...]
    for h in range(2):
        delta[h:h + 1, :] = jnp.sum(dt[h * HEAD_DIM:(h + 1) * HEAD_DIM, :], axis=0, keepdims=True)
    dqt[...] = jnp.zeros_like(dqt)

    def frame_step(k, v):
        kt[...] = k.T
        dk_s[...] = jnp.zeros_like(dk_s)
        dv_s[...] = jnp.zeros_like(dv_s)
        for h in range(2):
            def block(b, _, h=h):
                cols = pl.ds(pl.multiple_of(b * qb, qb), qb)
                qh = qm[h, cols, :]
                dh = dom[h, cols, :]
                pt = jnp.exp(dot(k, qh, 1, 1) - lse[h:h + 1, cols])
                dv_s[...] += dot(pt.astype(BF), dh)
                dst = (pt * (dot(v, dh, 1, 1) - delta[h:h + 1, cols])).astype(BF)
                dk_s[...] += dot(dst, qh)
                rows = slice(h * HEAD_DIM, (h + 1) * HEAD_DIM)
                dqt[rows, cols] += dot(kt[rows, :], dst)
                return 0

            lax.fori_loop(0, n // qb, block, 0)

    for r in range(frames - 1):
        @pl.when(act[r + 1] != 0)
        def _(r=r):
            frame_step(kvx[r, :, 0:128], kvx[r, :, 128:256])
            dkv_x[r, :, 0:128] = dk_s[...].astype(BF)
            dkv_x[r, :, 128:256] = dv_s[...].astype(BF)

        @pl.when(act[r + 1] == 0)
        def _(r=r):
            dkv_x[r] = jnp.zeros_like(dkv_x[r])

    frame_step(qkv[:, 128:256], qkv[:, 256:384])
    dkv_own[:, 0:128] = dk_s[...]
    dkv_own[:, 128:256] = dv_s[...]
    dq_out[...] = (dqt[...].T * (1.0 / math.sqrt(HEAD_DIM))).astype(BF)


def gelu_parts(u):
    t = jnp.tanh(C_GELU * (u + 0.044715 * (u * u * u)))
    value = 0.5 * u * (1.0 + t)
    slope = 0.5 * (1.0 + t) + 0.5 * u * (1.0 - t * t) * (C_GELU * (1.0 + 3 * 0.044715 * (u * u)))
    return value, slope


def middle_kernel(sc, x, g, o0, o1, o2, o3, wo, wy, wc, gain, bias, do_out, lout, h_out, du_out, b_out, dz_out, dy_out, gains, wo_s):
    mats = (wo, wc.at[0], wy, wc.at[1])
    for e in range(4):
        wo_s[e] = mats[e][1024:1152, :]
    gain_row = gain[pl.ds(sc[1], 1), :]
    mid = x[...].astype(F32)
    for k, ref in enumerate((o0, o1, o2, o3)):
        mid = mid + dot(ref[...], wo_s[sc[0] ^ k])
    hat, inv = norm_parts(mid)
    b = (hat * gain_row + bias[pl.ds(sc[1], 1), :]).astype(BF)
    b_out[...] = b
    cot = g[...]
    dy_out[...] = mid
    db = jnp.zeros_like(mid)
    for e in range(4):
        up = mats[e][0:512, :]
        down = mats[e][512:1024, :]
        value, slope = gelu_parts(dot(b, up))
        h = value.astype(BF)
        h_out[:, e * 512:(e + 1) * 512] = h
        dy_out[...] += dot(h, down)
        du = (dot(cot, down, 1, 1) * slope).astype(BF)
        du_out[:, e * 512:(e + 1) * 512] = du
        db = db + dot(du, up, 1, 1)
    lout[...] = dy_out[...].astype(BF)
    gains[0:1, :] = jnp.sum(db * hat, axis=0, keepdims=True)
    gains[1:2, :] = jnp.sum(db, axis=0, keepdims=True)
    dy = cot.astype(F32) + norm_back(db, hat, inv, gain_row)
    dy_out[...] = dy
    dz = dy.astype(BF)
    dz_out[...] = dz
    for k in range(4):
        do_out[k] = dot(dz, wo_s[sc[0] ^ k], 1, 1).astype(BF)


def store_pieces(dst, e, row, value, rows, sc):
    for a in range(PIECES):
        dst[place(a) ^ sc[2], e, row:row + rows, :] = value[a * rows:(a + 1) * rows, :]


def middle_grads_kernel(shards, sc, h, du, b, dz, g, o0, o1, o2, o3, out, o_s):
    for k, ref in enumerate((o0, o1, o2, o3)):
        o_s[k] = ref[...]
    for slot, e in enumerate(shards):
        cols = slice(e * 512, (e + 1) * 512)
        store_pieces(out, slot, 0, dot(b[...], du[:, cols], 0, 0).astype(BF), RUP, sc)
        store_pieces(out, slot, RUP, dot(h[:, cols], g[...], 0, 0).astype(BF), RDOWN, sc)
        store_pieces(out, slot, RUP + RDOWN, dot(o_s[sc[0] ^ e], dz[...], 0, 0).astype(BF), ROUT, sc)


def input_kernel(sc, x, dy, d0, d1, d2, d3, wo, wy, wc, gain, bias, gin, gains, keep, send, w_s, d_s):
    mats = (wo, wc.at[0], wy, wc.at[1])
    for e in range(4):
        w_s[e] = mats[e][...]
    gain_row = gain[pl.ds(sc[1], 1), :]
    hat, inv = norm_parts(x[...].astype(F32))
    a = (hat * gain_row + bias[pl.ds(sc[1], 1), :]).astype(BF)
    da = jnp.zeros_like(hat)
    for k, ref in enumerate((d0, d1, d2, d3)):
        d_s[k] = ref[...]
        da = da + dot(ref[...], w_s[sc[0] ^ k], 1, 1)
    gains[0:1, :] = jnp.sum(da * hat, axis=0, keepdims=True)
    gains[1:2, :] = jnp.sum(da, axis=0, keepdims=True)
    gin[...] = (dy[...] + norm_back(da, hat, inv, gain_row)).astype(BF)
    for e in range(4):
        dst = (keep, send)[e % 2]
        store_pieces(dst, e // 2, 0, dot(a, d_s[sc[0] ^ e], 0, 0).astype(BF), 64, sc)


def unpack_kernel(sc, one, two, up, down, out, q, k, v):
    for rel in range(2):
        net = sc[1] ^ rel
        for spot in range(PIECES):
            piece = sc[2] ^ spot
            a = 0
            for rank, bit in enumerate(ORDER):
                a = a + ((piece >> (2 - rank)) & 1) * (1 << bit)
            big = pl.ds(pl.multiple_of(a * 64, 64), 64)
            small = pl.ds(pl.multiple_of(a * 16, 16), 16)
            up[net, big, :] = one[spot, rel, 0:64, :].astype(F32)
            down[net, big, :] = one[spot, rel, 64:128, :].astype(F32)
            out[net, small, :] = one[spot, rel, 128:144, :].astype(F32)
            q[net, big, :] = two[spot, rel, :, 0:128].astype(F32)
            k[net, big, :] = two[spot, rel, :, 128:256].astype(F32)
            v[net, big, :] = two[spot, rel, :, 256:384].astype(F32)


def swap(value, axis, size, bit):
    return lax.ppermute(value, axis, [(n, n ^ bit) for n in range(size)])


def sum_rows(keep, send, seq):
    buf = keep + swap(send, "tp", 4, 1)
    size = PIECES
    for bit in ORDER:
        size //= 2
        buf = buf[:size] + swap(buf[size:], "seq", seq, 1 << bit)
    far = PIECES
    while far < seq:
        buf = buf + swap(buf, "seq", seq, far)
        far *= 2
    other = swap(buf[:, 1], "tp", 4, 2)
    buf = jnp.stack([buf[:, 0], other], axis=1)
    for bit in reversed(ORDER):
        buf = jnp.concatenate([buf, swap(buf, "seq", seq, 1 << bit)], axis=0)
    return buf


def body(layer_in, cotangent, clip_of_frame, w_query, w_key, w_value, w_out, w_up, w_down, norm1_gain, norm1_bias, norm2_gain, norm2_bias):
    seq = lax.axis_size("seq")
    frames = seq // GROUP
    i = lax.axis_index("seq")
    j = lax.axis_index("tp")
    net, core = j // 2, j % 2
    spot, frame = i % GROUP, i // GROUP
    segment, width = layer_in.shape[1], layer_in.shape[3]
    rows = segment * GROUP
    whole = jnp.where(clip_of_frame[0, frames - 1] == 0, 0, 1)
    stream = whole ^ core
    sc = jnp.stack([spot ^ j, net, place(i % PIECES)]).astype(jnp.int32)

    def mine(array):
        return lax.dynamic_slice(array, (net, 0, stream, 0), (1, segment, 1, width)).reshape(segment, width)

    x = mine(layer_in)
    cot = mine(cotangent)
    clips = lax.dynamic_index_in_dim(clip_of_frame, stream, 0, keepdims=False)
    marks = [lax.dynamic_index_in_dim(clips, frame ^ r, 0, keepdims=False) for r in range(frames)]
    act = jnp.stack([(mark == marks[0]).astype(jnp.int32) for mark in marks])

    def both(parts, axis):
        packed = jnp.concatenate(parts, axis=axis)
        own = lax.dynamic_index_in_dim(packed, net, 0, keepdims=False)
        other = lax.dynamic_index_in_dim(packed, 1 - net, 0, keepdims=False)
        got = swap(other, "tp", 4, 2)
        return own, got, swap(jnp.stack([own, got]), "tp", 4, 1)

    xs = [x] + [swap(x, "seq", seq, k) for k in range(1, GROUP)]
    w_heads = both([w_query, w_key, w_value], 2)
    w_rest = both([w_up, w_down, w_out], 1)

    (qkv,) = call(project_kernel, [((rows, 384), BF)], sc, [*xs, *w_heads, norm1_gain, norm1_bias],
                  scratch=[pltpu.VMEM((width, 384), BF)], flops=2 * rows * width * 384)

    def cross(value, r):
        if frames == 2:
            pairs = [(n * 4 + t, (n ^ GROUP) * 4 + t) for n in range(seq) for t in (0, 2)]
            return lax.ppermute(value, ("seq", "tp"), pairs)
        return swap(value, "seq", seq, GROUP * r)

    kvx = jnp.stack([cross(qkv[:, 128:384], r) for r in range(1, frames)])
    qb = 256
    o, ot, lse = call(
        lambda *refs: attend_kernel(frames, qb, *refs),
        [((rows, 128), BF), ((128, rows), F32), ((2, rows), F32)], act, [qkv, kvx],
        scratch=[pltpu.VMEM((2, rows, 128), BF), pltpu.VMEM((128, rows), BF), pltpu.VMEM((2, rows), F32),
                 pltpu.VMEM((2, rows), F32), pltpu.VMEM((128, rows), F32)], flops=8 * rows * rows * 128)
    o4 = o.reshape(GROUP, segment, 128)
    os = [o4[0]] + [swap(o4[k], "seq", seq, k) for k in range(1, GROUP)]
    do4, lout, h, du, b, dz, dy, gains2 = call(
        middle_kernel,
        [((GROUP, segment, 128), BF), ((segment, width), BF), ((segment, 2048), BF), ((segment, 2048), BF),
         ((segment, width), BF), ((segment, width), BF), ((segment, width), F32), ((2, width), F32)],
        sc, [x, cot, *os, *w_rest, norm2_gain, norm2_bias],
        scratch=[pltpu.VMEM((4, 128, width), BF)], flops=2 * segment * 512 * (2048 * 4 + 1024))
    dos = [do4[0]] + [swap(do4[k], "seq", seq, k) for k in range(1, GROUP)]
    do = jnp.concatenate(dos, axis=0)

    def grads(shards):
        (out,) = call(
            lambda *refs: middle_grads_kernel(shards, *refs), [((PIECES, 2, RUP + RDOWN + ROUT, 512), BF)],
            sc, [h, du, b, dz, cot, *os], scratch=[pltpu.VMEM((4, segment, 128), BF)], flops=4 * segment * 512 * 1152)
        return out

    send1 = grads((1, 3))
    keep1 = grads((0, 2))
    one = sum_rows(keep1, send1, seq)

    dq, dkv_own, dkv_x = call(
        lambda *refs: attend_back_kernel(frames, qb, *refs),
        [((rows, 128), BF), ((rows, 256), F32), ((frames - 1, rows, 256), BF)], act, [qkv, kvx, do, ot, lse],
        scratch=[pltpu.VMEM((2, rows, 128), BF), pltpu.VMEM((2, rows, 128), BF), pltpu.VMEM((128, rows), BF),
                 pltpu.VMEM((2, rows), F32), pltpu.VMEM((128, rows), F32), pltpu.VMEM((rows, 128), F32),
                 pltpu.VMEM((rows, 128), F32)], flops=20 * rows * rows * 128)
    total = dkv_own
    for r in range(1, frames):
        total = total + cross(dkv_x[r - 1], r).astype(F32)
    dqkv = jnp.concatenate([dq, total.astype(BF)], axis=1).reshape(GROUP, segment, 384)
    ds = [dqkv[0]] + [swap(dqkv[k], "seq", seq, k) for k in range(1, GROUP)]
    gin, gains1, keep2, send2 = call(
        input_kernel,
        [((segment, width), BF), ((2, width), F32), ((PIECES, 2, 64, 384), BF), ((PIECES, 2, 64, 384), BF)],
        sc, [x, dy, *ds, *w_heads, norm1_gain, norm1_bias],
        scratch=[pltpu.VMEM((4, width, 384), BF), pltpu.VMEM((4, segment, 384), BF)], flops=4 * segment * 512 * 1536)
    two = sum_rows(keep2, send2, seq)

    def spread(own):
        across = swap(own, "tp", 4, 2)
        pair = jnp.stack([own, across])
        other = swap(pair, "tp", 4, 1)
        nets = jnp.stack([pair, other], axis=2)
        nets = jnp.where(stream == 0, nets, nets[:, :, ::-1])
        return jnp.where(net == 0, nets, nets[::-1])

    layer_out = spread(lout)
    input_grad = spread(gin)

    small = jnp.concatenate([gains1, gains2], axis=0)
    small = jnp.where(jnp.arange(2)[:, None, None] == net, small[None], 0.0)
    for bit in (1, 2):
        small = small + swap(small, "tp", 4, bit)
    bit = 1
    while bit < seq:
        small = small + swap(small, "seq", seq, bit)
        bit *= 2

    up, down, out, gq, gk, gv = call(
        unpack_kernel,
        [((2, 512, 512), F32), ((2, 512, 512), F32), ((2, 128, 512), F32)] + [((2, 512, 128), F32)] * 3,
        sc, [one, two], flops=1000)
    return (layer_out, input_grad, gq, gk, gv, out, up, down, small[:, 0], small[:, 1], small[:, 2], small[:, 3])


def solution(mesh):
    tokens = P(None, "seq", None, None)
    columns = P(None, None, "tp")
    rows = P(None, "tp", None)
    return jax.shard_map(
        body,
        mesh=mesh,
        in_specs=(tokens, tokens, P(), columns, columns, columns, rows, columns, rows, P(), P(), P(), P()),
        out_specs=(tokens, tokens, columns, columns, columns, rows, columns, rows, P(), P(), P(), P()),
        check_vma=False,
    )
```

time: 737 us -> 298 us (0.40); the launches traced: 727 us -> 298 us
  waiting for transfers between devices: 394 us -> 170 us
  matrix products: 134 us -> 0 us
  other arithmetic: 80.8 us -> 12.3 us
  Pallas kernels: 0 us -> 50.5 us
  local copies, waits for them, and re-layouts: 61.9 us -> 14.4 us
  starting transfers between devices: 1.2 us -> 47.4 us
  blocking collectives: 39.2 us -> 0 us
  between operations: 16 us -> 3.25 us
    ppermute x0 -> x43, waiting for transfers between devices: none -> 170 us  [the longest x41 152 us: swap(): return lax.ppermute(value, axis, [(n, n ^ bit) for n in range(size)])]
    psum x4 -> x0, waiting for transfers between devices: 157 us -> none  [the longest x1 72.8 us: body(): lax.psum(found[0].astype(jnp.bfloat16), 'seq').astype(jnp.float32)]
    dot_general x52 -> x0, matrix products: 134 us -> none  [the longest x6 24.2 us: raw_scores(): jnp.einsum('qshe,kshe->shqk', query_four, key_four, preferred_element_typ...]
    all_gather x4 -> x0, waiting for transfers between devices: 127 us -> none  [the longest x2 64.7 us: net_pass(): key_part = lax.all_gather(key_local, 'seq', axis=0, tiled=True)]
    unnamed x10 -> x0, waiting for transfers between devices: 110 us -> none
    pallas_call x0 -> x8, Pallas kernels: none -> 50.5 us  [call(): pl.pallas_call(kernel, out_shape=[jax.ShapeDtypeStruct(s, d) for s, d in...]
    ppermute x0 -> x43, starting transfers between devices: none -> 47.4 us  [the longest x41 37.3 us: swap(): return lax.ppermute(value, axis, [(n, n ^ bit) for n in range(size)])]
    psum x1 -> x0, blocking collectives: 39.2 us -> none  [body(): lax.psum(found[6].astype(jnp.bfloat16), 'seq').astype(jnp.float32)]
  transfers between devices with their start and end apart: 9 -> 43, of which waited for: 9 -> 26; matrix products, arithmetic and copies ran while one was open for 20% -> 6% of each run, Pallas kernels for 0% -> 12%
where the time goes in v1:
time: 298 us
  waiting for transfers between devices  170 us (57%)
  Pallas kernels  50.5 us (17%)
  starting transfers between devices  47.4 us (16%)
  local copies, waits for them, and re-layouts  14.4 us (5%)
  other arithmetic  12.3 us (4%)
  between operations  3.25 us (1%)
    ppermute x41, waiting for transfers between devices, swap(): return lax.ppermute(value, axis, [(n, n ^ bit) for n in range(size)])  152 us
    pallas_call x8, Pallas kernels, call(): pl.pallas_call(kernel, out_shape=[jax.ShapeDtypeStruct(s, d) for s, d in...  50.5 us
    ppermute x41, starting transfers between devices, swap(): return lax.ppermute(value, axis, [(n, n ^ bit) for n in range(size)])  37.3 us
    ppermute x2, waiting for transfers between devices, cross(): return lax.ppermute(value, ('seq', 'tp'), pairs)  17.8 us
    ppermute x2, starting transfers between devices, cross(): return lax.ppermute(value, ('seq', 'tp'), pairs)  10.1 us
    unnamed x40, local copies, waits for them, and re-layouts  8.27 us
  transfers between devices with their start and end apart: 43, of which 26 were waited for; matrix products, arithmetic and copies ran while one was open for 6% of the time, Pallas kernels for 12%

profile of v1, /device:TPU:0, one launch (start us, length us, event | category | flops | bytes accessed | tf_op | source)
XLA Modules:
  0.0 297.9 jit_solution(1873175002569990524)
XLA Ops:
  0.7 1.4 constant_dynamic-update-slice_fusion.5
  2.1 1.3 constant_dynamic-update-slice_fusion.4
  3.4 1.0 constant_dynamic-update-slice_fusion.3
  4.6 3.0 %collective-permute-start.9 = (bf16[1152,512]{1,0:T(8,128)(2,1)S(1)}, bf16[1152,512]{1,0:T(8,128)(2,1)S(1)}, u32[]{:S(2)}, u32[]{:S(2)}) collective-permute-start(bf16[1152,512]{1,0:T(8,128)(2,1)S(1)} %get-tuple-element.84), channel_id=1, source_target_pairs={{0,2},{1,3},{2,0},{3,1},{4,6},{5,7},{6,4},{7,5},{8,10},{9,11},{10,... | collective-permute-start | bytes 3538952 | tf_op jit(solution)/shard_map/ppermute | solution.py:279
  7.8 25.8 %collective-permute-done.9.wy = bf16[1152,512]{1,0:T(8,128)(2,1)S(1)} collective-permute-done((bf16[1152,512]{1,0:T(8,128)(2,1)S(1)}, bf16[1152,512]{1,0:T(8,128)(2,1)S(1)}, u32[]{:S(2)}, u32[]{:S(2)}) %collective-permute-start.9) | collective-permute-done | bytes 1179680 | tf_op jit(solution)/shard_map/ppermute | solution.py:279
  33.6 1.8 pad_maximum_fusion
  35.5 1.8 collective-permute-start.3
  37.4 9.8 %collective-permute-done.3.wy = bf16[512,384]{1,0:T(8,128)(2,1)S(1)} collective-permute-done((bf16[512,384]{1,0:T(8,128)(2,1)S(1)}, bf16[512,384]{1,0:T(8,128)(2,1)S(1)}, u32[]{:S(2)}, u32[]{:S(2)}) %collective-permute-start.3) | collective-permute-done | bytes 393248 | tf_op jit(solution)/shard_map/ppermute | solution.py:279
  47.1 1.0 pad_maximum_fusion.5
  49.9 1.8 collective-permute-start
  51.7 1.6 collective-permute-start.1
  53.6 5.2 %collective-permute-done.x1 = bf16[256,512]{1,0:T(8,128)(2,1)S(1)} collective-permute-done((bf16[256,512]{1,0:T(8,128)(2,1)S(1)}, bf16[256,512]{1,0:T(8,128)(2,1)S(1)}, u32[]{:S(2)}, u32[]{:S(2)}) %collective-permute-start) | collective-permute-done | bytes 262176 | tf_op jit(solution)/shard_map/ppermute | solution.py:279
  58.7 2.1 collective-permute-done.1.x2
  60.9 4.7 %collective-permute-done.2.x3 = bf16[256,512]{1,0:T(8,128)(2,1)S(1)} collective-permute-done((bf16[256,512]{1,0:T(8,128)(2,1)S(1)}, bf16[256,512]{1,0:T(8,128)(2,1)S(1)}, u32[]{:S(2)}, u32[]{:S(2)}) %collective-permute-start.2) | collective-permute-done | bytes 262176 | tf_op jit(solution)/shard_map/ppermute | solution.py:279
  65.6 1.9 shard_map.220.refs_1_
  68.3 4.7 %collective-permute-start.5 = (bf16[1024,256]{1,0:T(8,128)(2,1)}, bf16[1024,256]{1,0:T(8,128)(2,1)S(1)}, u32[]{:S(2)}, u32[]{:S(2)}) collective-permute-start(bf16[1024,256]{1,0:T(8,128)(2,1)} %slice.144), channel_id=1, source_target_pairs={{0,16},{2,18},{4,20},{6,22},{8,24},{10,26},{12,28},{14,30},{16,0},... | collective-permute-start | bytes 1572872 | tf_op jit(solution)/shard_map/ppermute | solution.py:338
  75.0 11.2 %collective-permute-done.5 = bf16[1024,256]{1,0:T(8,128)(2,1)S(1)} collective-permute-done((bf16[1024,256]{1,0:T(8,128)(2,1)}, bf16[1024,256]{1,0:T(8,128)(2,1)S(1)}, u32[]{:S(2)}, u32[]{:S(2)}) %collective-permute-start.5) | collective-permute-done | bytes 524320 | tf_op jit(solution)/shard_map/ppermute | solution.py:338
  86.2 13.2 %shard_map.221 = (bf16[1024,128]{1,0:T(8,128)(2,1)S(1)}, f32[128,1024]{1,0:T(8,128)S(1)}, f32[2,1024]{1,0:T(2,128)S(1)}) custom-call(s32[2]{0:T(128)S(1)} %add_convert_fusion.1.refs_0_, bf16[1024,384]{1,0:T(8,128)(2,1)S(1)} %shard_map.220.refs_1_, bf16[1,1024,256]{2,1,0:T(8,128)(2,1)S(1)} %bitcast.67), custom_call_target="tpu_custom_call" | custom-call | flops 1073741824 | tf_op jit(solution)/shard_map/pallas_call | solution.py:55
  99.5 1.7 collective-permute-start.6
  102.0 1.1 collective-permute-start.8
  103.8 1.6 collective-permute-done.7.o2.refs_8_
  105.5 1.7 collective-permute-done.8.o3.refs_9_
  107.2 7.5 %shard_map.222 = (bf16[4,256,128]{2,1,0:T(8,128)(2,1)S(1)}, bf16[256,512]{1,0:T(8,128)(2,1)S(1)}, bf16[256,2048]{1,0:T(8,128)(2,1)S(1)}, bf16[256,2048]{1,0:T(8,...) custom-call(s32[3]{0:T(128)S(1)} %pad_add_fusion.sc.refs_0_, ...), custom_call_target="tpu_custom_call" | custom-call | flops 2415919104 | tf_op jit(solution)/shard_map/pallas_call | solution.py:55
  114.7 1.2 copy-done.2
  115.9 2.8 shard_map.226
  119.3 1.1 collective-permute-start.14
  120.4 1.8 collective-permute-start.15
  122.2 1.0 collective-permute-done.13
  123.5 2.3 collective-permute-done.15
  125.9 15.1 %shard_map.223 = (bf16[1024,128]{1,0:T(8,128)(2,1)S(1)}, f32[1024,256]{1,0:T(8,128)S(1)}, bf16[1,1024,256]{2,1,0:T(8,128)(2,1)S(1)}) custom-call(s32[2]{0:T(128)S(1)} %add_convert_fusion.1.refs_0_, bf16[1024,384]{1,0:T(8,128)(2,1)S(1)} %shard_map.220.refs_1_, bf16[1,1024,256]{2,1,0:T(8,128)(2,1)S(1)} %bitcast.68, ...), custom_call_target="tpu_custom_call" | custom-call | flops 2684354560 | tf_op jit(solution)/shard_map/pallas_call | solution.py:55
  141.1 5.4 %collective-permute-start.16 = (bf16[1024,256]{1,0:T(8,128)(2,1)S(1)}, bf16[1024,256]{1,0:T(8,128)(2,1)S(1)}, u32[]{:S(2)}, u32[]{:S(2)}) collective-permute-start(bf16[1024,256]{1,0:T(8,128)(2,1)S(1)} %bitcast.69), channel_id=1, source_target_pairs={{0,16},{2,18},{4,20},{6,22},{8,24},{10,26},{12,28},{14,30},{16,0},... | collective-permute-start | bytes 1572872 | tf_op jit(solution)/shard_map/ppermute | solution.py:338
  146.5 2.7 shard_map.225
  149.2 2.4 add.101
  152.4 6.6 %collective-permute-done.16 = bf16[1024,256]{1,0:T(8,128)(2,1)S(1)} collective-permute-done((bf16[1024,256]{1,0:T(8,128)(2,1)S(1)}, bf16[1024,256]{1,0:T(8,128)(2,1)S(1)}, u32[]{:S(2)}, u32[]{:S(2)}) %collective-permute-start.16) | collective-permute-done | bytes 524320 | tf_op jit(solution)/shard_map/ppermute | solution.py:338
  159.3 1.1 collective-permute-start.17
  160.9 1.9 collective-permute-start.19
  162.8 1.5 collective-permute-start.11
  164.4 11.7 %collective-permute-done.17.d1 = bf16[256,384]{1,0:T(8,128)(2,1)S(1)} collective-permute-done((bf16[256,384]{1,0:T(8,128)(2,1)S(1)}, bf16[256,384]{1,0:T(8,128)(2,1)S(1)}, u32[]{:S(2)}, u32[]{:S(2)}) %collective-permute-start.17) | collective-permute-done | bytes 196640 | tf_op jit(solution)/shard_map/ppermute | solution.py:279
  176.1 3.6 %shard_map.224 = (bf16[256,512]{1,0:T(8,128)(2,1)S(1)}, f32[2,512]{1,0:T(2,128)S(1)}, bf16[8,2,64,384]{3,2,1,0:T(8,128)(2,1)S(1)}, bf16[8,2,64,384]{3,2,1,0:T(8,128)(2,1)}) custom-call(s32[3]{0:T(128)S(1)} %pad_add_fusion.sc.refs_0_, bf16[256,512]{1,0:T(8,128)(2,1)S(1)} %bitcast.64, f32[256,512]{1,0:T(8,128)S(1)} %get-tuple-element.38.dy, ...), custom_call_target="tpu_custom_call" | custom-call | flops 805306368 | tf_op jit(solution)/shard_map/pallas_call | solution.py:55
  181.7 1.5 collective-permute-start.39
  186.1 3.2 %collective-permute-done.40 = f32[2,4,512]{2,0,1:T(2,128)S(1)} collective-permute-done((f32[2,4,512]{2,0,1:T(2,128)S(1)}, f32[2,4,512]{2,0,1:T(2,128)S(1)}, u32[]{:S(2)}, u32[]{:S(2)}) %collective-permute-start.40) | collective-permute-done | bytes 16416 | tf_op jit(solution)/shard_map/ppermute | solution.py:279
  189.3 1.2 collective-permute-start.41
  190.6 1.5 collective-permute-start.20
  192.1 4.9 %collective-permute-done.41 = f32[2,4,512]{2,0,1:T(2,128)S(1)} collective-permute-done((f32[2,4,512]{2,0,1:T(2,128)S(1)}, f32[2,4,512]{2,0,1:T(2,128)S(1)}, u32[]{:S(2)}, u32[]{:S(2)}) %collective-permute-start.41) | collective-permute-done | bytes 16416 | tf_op jit(solution)/shard_map/ppermute | solution.py:279
  197.0 3.0 collective-permute-start.42
  200.0 1.1 slice_add_fusion.1
  201.3 1.1 pad_maximum_fusion.3
  203.0 1.4 add.105
  204.5 1.1 collective-permute-start.31
  205.6 11.1 %collective-permute-done.25 = bf16[1,2,144,512]{3,2,1,0:T(8,128)(2,1)S(1)} collective-permute-done((bf16[1,2,144,512]{3,2,1,0:T(8,128)(2,1)S(1)}, bf16[1,2,144,512]{3,2,1,0:T(8,128)(2,1)S(1)}, u32[]{:S(2)}, u32[]{:S(2)}) %collective-permute-start.25) | collective-permute-done | bytes 294944 | tf_op jit(solution)/shard_map/ppermute | solution.py:279
  216.7 1.6 collective-permute-start.26
  218.5 4.1 %collective-permute-done.26 = bf16[1,144,512]{2,1,0:T(8,128)(2,1)S(1)} collective-permute-done((bf16[1,144,512]{2,1,0:T(8,128)(2,1)S(1)}, bf16[1,144,512]{2,1,0:T(8,128)(2,1)S(1)}, u32[]{:S(2)}, u32[]{:S(2)}) %collective-permute-start.26) | collective-permute-done | bytes 147488 | tf_op jit(solution)/shard_map/ppermute | solution.py:279
  222.9 2.2 collective-permute-done.32
  225.9 12.9 %collective-permute-done.27 = bf16[1,2,144,512]{3,2,1,0:T(8,128)(2,1)S(1)} collective-permute-done((bf16[1,2,144,512]{3,2,1,0:T(8,128)(2,1)S(1)}, bf16[1,2,144,512]{3,2,1,0:T(8,128)(2,1)S(1)}, u32[]{:S(2)}, u32[]{:S(2)}) %collective-permute-start.27) | collective-permute-done | bytes 294944 | tf_op jit(solution)/shard_map/ppermute | solution.py:279
  239.0 1.9 collective-permute-done.33
  241.6 3.4 %collective-permute-done.34 = bf16[1,64,384]{2,1,0:T(8,128)(2,1)S(1)} collective-permute-done((bf16[1,64,384]{2,1,0:T(8,128)(2,1)S(1)}, bf16[1,64,384]{2,1,0:T(8,128)(2,1)S(1)}, u32[]{:S(2)}, u32[]{:S(2)}) %collective-permute-start.34) | collective-permute-done | bytes 49184 | tf_op jit(solution)/shard_map/ppermute | solution.py:279
  245.1 11.1 %collective-permute-done.28 = bf16[2,2,144,512]{3,2,1,0:T(8,128)(2,1)S(1)} collective-permute-done((bf16[2,2,144,512]{3,2,1,0:T(8,128)(2,1)S(1)}, bf16[2,2,144,512]{3,2,1,0:T(8,128)(2,1)S(1)}, u32[]{:S(2)}, u32[]{:S(2)}) %collective-permute-start.28) | collective-permute-done | bytes 589856 | tf_op jit(solution)/shard_map/ppermute | solution.py:279
  256.3 1.2 collective-permute-start.29
  258.1 5.2 %collective-permute-done.36 = bf16[2,2,64,384]{3,2,1,0:T(8,128)(2,1)S(1)} collective-permute-done((bf16[2,2,64,384]{3,2,1,0:T(8,128)(2,1)S(1)}, bf16[2,2,64,384]{3,2,1,0:T(8,128)(2,1)S(1)}, u32[]{:S(2)}, u32[]{:S(2)}) %collective-permute-start.36) | collective-permute-done | bytes 196640 | tf_op jit(solution)/shard_map/ppermute | solution.py:279
  263.4 1.0 collective-permute-start.37
  264.5 2.0 copy.30
  266.8 25.0 %collective-permute-done.37 = bf16[4,2,64,384]{3,2,1,0:T(8,128)(2,1)S(1)} collective-permute-done((bf16[4,2,64,384]{3,2,1,0:T(8,128)(2,1)S(1)}, bf16[4,2,64,384]{3,2,1,0:T(8,128)(2,1)S(1)}, u32[]{:S(2)}, u32[]{:S(2)}) %collective-permute-start.37) | collective-permute-done | bytes 393248 | tf_op jit(solution)/shard_map/ppermute | solution.py:279
  292.2 2.0 copy.29
  294.2 3.6 %shard_map.227 = (f32[2,512,512]{2,1,0:T(8,128)}, f32[2,512,512]{2,1,0:T(8,128)}, f32[2,128,512]{2,1,0:T(8,128)}, f32[2,512,128]{2,1,0:T(8,128)}, f32[2,512,128]{2,1,0:T(8,128)}, /*index=5*/f32[2,512,128]{2,1,0:T(8,128)}) custom-call(s32[3]{0:T(128)S(1)} %pad_add_fusion.sc.refs_0_, bf16[8,2,144,512]{3,2,1,0:T(8,128)(2,1)S(1)} %pad_maximum_fusion.1.one, ...), custom_call_target="tpu_custom_call" | custom-call | flops 1000 | tf_op jit(solution)/shard_map/pallas_call | solution.py:55
  (128 shorter events, 17.1 us)
Async XLA Ops:
  0.6 48.7 %copy-start = (bf16[2,256,2,512]{3,2,1,0:T(2,128)(2,1)S(1)}, bf16[2,256,2,512]{3,2,1,0:T(2,128)(2,1)}, u32[]{:S(2)}) copy-start(bf16[2,256,2,512]{3,2,1,0:T(2,128)(2,1)} %param.13) | copy-start | bytes 3145732
  4.3 3.3 %copy-start.12 = (bf16[2,512,128]{2,1,0:T(8,128)(2,1)S(1)}, bf16[2,512,128]{2,1,0:T(8,128)(2,1)}, u32[]{:S(2)}) copy-start(bf16[2,512,128]{2,1,0:T(8,128)(2,1)} %param.16) | copy-start | bytes 786436
  4.4 3.3 %copy-start.13 = (bf16[2,512,128]{2,1,0:T(8,128)(2,1)S(1)}, bf16[2,512,128]{2,1,0:T(8,128)(2,1)}, u32[]{:S(2)}) copy-start(bf16[2,512,128]{2,1,0:T(8,128)(2,1)} %param.17) | copy-start | bytes 786436
  4.4 3.4 %copy-start.14 = (bf16[2,512,128]{2,1,0:T(8,128)(2,1)S(1)}, bf16[2,512,128]{2,1,0:T(8,128)(2,1)}, u32[]{:S(2)}) copy-start(bf16[2,512,128]{2,1,0:T(8,128)(2,1)} %param.18) | copy-start | bytes 786436
  4.6 30.8 %copy-start.9 = (bf16[1,1152,512]{2,1,0:T(8,128)(2,1)}, bf16[1,1152,512]{2,1,0:T(8,128)(2,1)S(1)}, u32[]{:S(2)}) copy-start(bf16[1,1152,512]{2,1,0:T(8,128)(2,1)S(1)} %get-tuple-element.85) | copy-start | bytes 3538948
  4.6 29.0 %collective-permute-start.9 = (bf16[1152,512]{1,0:T(8,128)(2,1)S(1)}, bf16[1152,512]{1,0:T(8,128)(2,1)S(1)}, u32[]{:S(2)}, u32[]{:S(2)}) collective-permute-start(bf16[1152,512]{1,0:T(8,128)(2,1)S(1)} %get-tuple-element.84), channel_id=1, source_target_pairs={{0,2},{1,3},{2,0},{3,1},{4,6},{5,7},{6,4},{7,5},{8,10},{9,11},{10,... | collective-permute-start | bytes 3538952 | tf_op jit(solution)/shard_map/ppermute | solution.py:279
  33.6 1.8 copy-start.10
  35.4 12.7 %copy-start.15 = (s32[2,2]{1,0:T(2,128)S(1)}, s32[2,2]{1,0:T(2,128)}, u32[]{:S(2)}) copy-start(s32[2,2]{1,0:T(2,128)} %param.15) | copy-start | bytes 52
  35.4 30.2 %copy-start.5 = (f32[2,512]{1,0:T(2,128)S(1)}, f32[2,512]{1,0:T(2,128)}, u32[]{:S(2)}) copy-start(f32[2,512]{1,0:T(2,128)} %gain.5) | copy-start | bytes 12292
  35.4 30.2 %copy-start.6 = (f32[2,512]{1,0:T(2,128)S(1)}, f32[2,512]{1,0:T(2,128)}, u32[]{:S(2)}) copy-start(f32[2,512]{1,0:T(2,128)} %bias.5) | copy-start | bytes 12292
  35.4 71.8 %collective-permute-start.10 = (bf16[2,1152,512]{2,1,0:T(8,128)(2,1)}, bf16[2,1152,512]{2,1,0:T(8,128)(2,1)}, u32[]{:S(2)}, u32[]{:S(2)}) collective-permute-start(bf16[2,1152,512]{2,1,0:T(8,128)(2,1)} %pad_maximum_fusion), channel_id=1, source_target_pairs={{0,1},{1,0},{2,3},{3,2},{4,5},{5,4},{6,7},{7,6},{8,9},{9,8},{10,11... | collective-permute-start | bytes 7077896 | tf_op jit(solution)/shard_map/ppermute | solution.py:279
  35.5 11.6 %collective-permute-start.3 = (bf16[512,384]{1,0:T(8,128)(2,1)S(1)}, bf16[512,384]{1,0:T(8,128)(2,1)S(1)}, u32[]{:S(2)}, u32[]{:S(2)}) collective-permute-start(bf16[512,384]{1,0:T(8,128)(2,1)S(1)} %get-tuple-element.90), channel_id=1, source_target_pairs={{0,2},{1,3},{2,0},{3,1},{4,6},{5,7},{6,4},{7,5},{8,10},{9,11},{10,... | collective-permute-start | bytes 1179656 | tf_op jit(solution)/shard_map/ppermute | solution.py:279
  48.1 17.5 %collective-permute-start.4 = (bf16[2,512,384]{2,1,0:T(8,128)(2,1)}, bf16[2,512,384]{2,1,0:T(8,128)(2,1)S(1)}, u32[]{:S(2)}, u32[]{:S(2)}) collective-permute-start(bf16[2,512,384]{2,1,0:T(8,128)(2,1)} %pad_maximum_fusion.5), channel_id=1, source_target_pairs={{0,1},{1,0},{2,3},{3,2},{4,5},{5,4},{6,7},{7,6},{8,9},{9,8},{10,11... | collective-permute-start | bytes 2359304 | tf_op jit(solution)/shard_map/ppermute | solution.py:279
  49.9 8.8 %collective-permute-start = (bf16[256,512]{1,0:T(8,128)(2,1)S(1)}, bf16[256,512]{1,0:T(8,128)(2,1)S(1)}, u32[]{:S(2)}, u32[]{:S(2)}) collective-permute-start(bf16[256,512]{1,0:T(8,128)(2,1)S(1)} %bitcast.59), channel_id=1, source_target_pairs={{0,4},{4,0},{8,12},{12,8},{16,20},{20,16},{24,28},{28,24},{1,5},{5... | collective-permute-start | bytes 786440 | tf_op jit(solution)/shard_map/ppermute | solution.py:279
  51.7 9.1 %collective-permute-start.1 = (bf16[256,512]{1,0:T(8,128)(2,1)S(1)}, bf16[256,512]{1,0:T(8,128)(2,1)S(1)}, u32[]{:S(2)}, u32[]{:S(2)}) collective-permute-start(bf16[256,512]{1,0:T(8,128)(2,1)S(1)} %bitcast.60), channel_id=1, source_target_pairs={{0,8},{4,12},{8,0},{12,4},{16,24},{20,28},{24,16},{28,20},{1,9},{5... | collective-permute-start | bytes 786440 | tf_op jit(solution)/shard_map/ppermute | solution.py:279
  53.3 12.3 %collective-permute-start.2 = (bf16[256,512]{1,0:T(8,128)(2,1)S(1)}, bf16[256,512]{1,0:T(8,128)(2,1)S(1)}, u32[]{:S(2)}, u32[]{:S(2)}) collective-permute-start(bf16[256,512]{1,0:T(8,128)(2,1)S(1)} %bitcast.61), channel_id=1, source_target_pairs={{0,12},{4,8},{8,4},{12,0},{16,28},{20,24},{24,20},{28,16},{1,13},{... | collective-permute-start | bytes 786440 | tf_op jit(solution)/shard_map/ppermute | solution.py:279
  65.6 33.9 %copy-start.4 = (bf16[2,512,384]{2,1,0:T(8,128)(2,1)}, bf16[2,512,384]{2,1,0:T(8,128)(2,1)S(1)}, u32[]{:S(2)}) copy-start(bf16[2,512,384]{2,1,0:T(8,128)(2,1)S(1)} %collective-permute-done.4.wc) | copy-start | bytes 2359300
  68.3 17.9 %collective-permute-start.5 = (bf16[1024,256]{1,0:T(8,128)(2,1)}, bf16[1024,256]{1,0:T(8,128)(2,1)S(1)}, u32[]{:S(2)}, u32[]{:S(2)}) collective-permute-start(bf16[1024,256]{1,0:T(8,128)(2,1)} %slice.144), channel_id=1, source_target_pairs={{0,16},{2,18},{4,20},{6,22},{8,24},{10,26},{12,28},{14,30},{16,0},... | collective-permute-start | bytes 1572872 | tf_op jit(solution)/shard_map/ppermute | solution.py:338
  73.1 30.0 %copy-start.11 = (bf16[2,256,2,512]{3,2,1,0:T(2,128)(2,1)S(1)}, bf16[2,256,2,512]{3,2,1,0:T(2,128)(2,1)}, u32[]{:S(2)}) copy-start(bf16[2,256,2,512]{3,2,1,0:T(2,128)(2,1)} %param.14) | copy-start | bytes 3145732
  86.2 20.9 %copy-start.7 = (f32[2,512]{1,0:T(2,128)S(1)}, f32[2,512]{1,0:T(2,128)}, u32[]{:S(2)}) copy-start(f32[2,512]{1,0:T(2,128)} %gain.4) | copy-start | bytes 12292
  86.2 20.9 %copy-start.8 = (f32[2,512]{1,0:T(2,128)S(1)}, f32[2,512]{1,0:T(2,128)}, u32[]{:S(2)}) copy-start(f32[2,512]{1,0:T(2,128)} %bias.4) | copy-start | bytes 12292
  99.5 4.3 %collective-permute-start.6 = (bf16[256,128]{1,0:T(8,128)(2,1)S(1)}, bf16[256,128]{1,0:T(8,128)(2,1)S(1)}, u32[]{:S(2)}, u32[]{:S(2)}) collective-permute-start(bf16[256,128]{1,0:T(8,128)(2,1)S(1)} %get-tuple-element.104), channel_id=1, source_target_pairs={{0,4},{4,0},{8,12},{12,8},{16,20},{20,16},{24,28},{28,24},{1,5},{5... | collective-permute-start | bytes 196616 | tf_op jit(solution)/shard_map/ppermute | solution.py:279
  101.2 4.3 %collective-permute-start.7 = (bf16[256,128]{1,0:T(8,128)(2,1)S(1)}, bf16[256,128]{1,0:T(8,128)(2,1)S(1)}, u32[]{:S(2)}, u32[]{:S(2)}) collective-permute-start(bf16[256,128]{1,0:T(8,128)(2,1)S(1)} %get-tuple-element.103), channel_id=1, source_target_pairs={{0,8},{4,12},{8,0},{12,4},{16,24},{20,28},{24,16},{28,20},{1,9},{5... | collective-permute-start | bytes 196616 | tf_op jit(solution)/shard_map/ppermute | solution.py:279
  102.0 5.2 %collective-permute-start.8 = (bf16[256,128]{1,0:T(8,128)(2,1)S(1)}, bf16[256,128]{1,0:T(8,128)(2,1)S(1)}, u32[]{:S(2)}, u32[]{:S(2)}) collective-permute-start(bf16[256,128]{1,0:T(8,128)(2,1)S(1)} %get-tuple-element.102), channel_id=1, source_target_pairs={{0,12},{4,8},{8,4},{12,0},{16,28},{20,24},{24,20},{28,16},{1,13},{... | collective-permute-start | bytes 196616 | tf_op jit(solution)/shard_map/ppermute | solution.py:279
  114.7 1.2 copy-start.2
  118.7 30.6 %collective-permute-start.22 = (bf16[8,2,144,512]{3,2,1,0:T(8,128)(2,1)}, bf16[8,2,144,512]{3,2,1,0:T(8,128)(2,1)S(1)}, u32[]{:S(2)}, u32[]{:S(2)}) collective-permute-start(bf16[8,2,144,512]{3,2,1,0:T(8,128)(2,1)} %shard_map.226), channel_id=1, source_target_pairs={{0,1},{1,0},{2,3},{3,2},{4,5},{5,4},{6,7},{7,6},{8,9},{9,8},{10,11... | collective-permute-start | bytes 7077896 | tf_op jit(solution)/shard_map/ppermute | solution.py:279
  118.7 4.6 %collective-permute-start.13 = (bf16[256,128]{1,0:T(8,128)(2,1)S(1)}, bf16[256,128]{1,0:T(8,128)(2,1)S(1)}, u32[]{:S(2)}, u32[]{:S(2)}) collective-permute-start(bf16[256,128]{1,0:T(8,128)(2,1)S(1)} %get-tuple-element.101), channel_id=1, source_target_pairs={{0,4},{4,0},{8,12},{12,8},{16,20},{20,16},{24,28},{28,24},{1,5},{5... | collective-permute-start | bytes 196616 | tf_op jit(solution)/shard_map/ppermute | solution.py:279
  119.3 4.3 %collective-permute-start.14 = (bf16[256,128]{1,0:T(8,128)(2,1)S(1)}, bf16[256,128]{1,0:T(8,128)(2,1)S(1)}, u32[]{:S(2)}, u32[]{:S(2)}) collective-permute-start(bf16[256,128]{1,0:T(8,128)(2,1)S(1)} %get-tuple-element.100), channel_id=1, source_target_pairs={{0,8},{4,12},{8,0},{12,4},{16,24},{20,28},{24,16},{28,20},{1,9},{5... | collective-permute-start | bytes 196616 | tf_op jit(solution)/shard_map/ppermute | solution.py:279
  120.4 5.5 %collective-permute-start.15 = (bf16[256,128]{1,0:T(8,128)(2,1)S(1)}, bf16[256,128]{1,0:T(8,128)(2,1)S(1)}, u32[]{:S(2)}, u32[]{:S(2)}) collective-permute-start(bf16[256,128]{1,0:T(8,128)(2,1)S(1)} %get-tuple-element.99), channel_id=1, source_target_pairs={{0,12},{4,8},{8,4},{12,0},{16,28},{20,24},{24,20},{28,16},{1,13},{... | collective-permute-start | bytes 196616 | tf_op jit(solution)/shard_map/ppermute | solution.py:279
  125.9 20.6 %copy-start.3 = (bf16[256,2048]{1,0:T(8,128)(2,1)S(1)}, bf16[256,2048]{1,0:T(8,128)(2,1)}, u32[]{:S(2)}) copy-start(bf16[256,2048]{1,0:T(8,128)(2,1)} %get-tuple-element.47.refs_2_) | copy-start | bytes 3145732
  141.1 17.9 %collective-permute-start.16 = (bf16[1024,256]{1,0:T(8,128)(2,1)S(1)}, bf16[1024,256]{1,0:T(8,128)(2,1)S(1)}, u32[]{:S(2)}, u32[]{:S(2)}) collective-permute-start(bf16[1024,256]{1,0:T(8,128)(2,1)S(1)} %bitcast.69), channel_id=1, source_target_pairs={{0,16},{2,18},{4,20},{6,22},{8,24},{10,26},{12,28},{14,30},{16,0},... | collective-permute-start | bytes 1572872 | tf_op jit(solution)/shard_map/ppermute | solution.py:338
  151.7 28.0 %collective-permute-start.23 = (bf16[4,2,144,512]{3,2,1,0:T(8,128)(2,1)S(1)}, bf16[4,2,144,512]{3,2,1,0:T(8,128)(2,1)S(1)}, u32[]{:S(2)}, u32[]{:S(2)}) collective-permute-start(bf16[4,2,144,512]{3,2,1,0:T(8,128)(2,1)S(1)} %slice.152), channel_id=1, source_target_pairs={{0,4},{4,0},{8,12},{12,8},{16,20},{20,16},{24,28},{28,24},{1,5},{5... | collective-permute-start | bytes 3538952 | tf_op jit(solution)/shard_map/ppermute | solution.py:279
  159.3 16.8 %collective-permute-start.17 = (bf16[256,384]{1,0:T(8,128)(2,1)S(1)}, bf16[256,384]{1,0:T(8,128)(2,1)S(1)}, u32[]{:S(2)}, u32[]{:S(2)}) collective-permute-start(bf16[256,384]{1,0:T(8,128)(2,1)S(1)} %get-tuple-element.88), channel_id=1, source_target_pairs={{0,4},{4,0},{8,12},{12,8},{16,20},{20,16},{24,28},{28,24},{1,5},{5... | collective-permute-start | bytes 589832 | tf_op jit(solution)/shard_map/ppermute | solution.py:279
  160.3 15.7 %collective-permute-start.18 = (bf16[256,384]{1,0:T(8,128)(2,1)S(1)}, bf16[256,384]{1,0:T(8,128)(2,1)S(1)}, u32[]{:S(2)}, u32[]{:S(2)}) collective-permute-start(bf16[256,384]{1,0:T(8,128)(2,1)S(1)} %get-tuple-element.89), channel_id=1, source_target_pairs={{0,8},{4,12},{8,0},{12,4},{16,24},{20,28},{24,16},{28,20},{1,9},{5... | collective-permute-start | bytes 589832 | tf_op jit(solution)/shard_map/ppermute | solution.py:279
  160.9 15.1 %collective-permute-start.19 = (bf16[256,384]{1,0:T(8,128)(2,1)S(1)}, bf16[256,384]{1,0:T(8,128)(2,1)S(1)}, u32[]{:S(2)}, u32[]{:S(2)}) collective-permute-start(bf16[256,384]{1,0:T(8,128)(2,1)S(1)} %get-tuple-element.86), channel_id=1, source_target_pairs={{0,12},{4,8},{8,4},{12,0},{16,28},{20,24},{24,20},{28,16},{1,13},{... | collective-permute-start | bytes 589832 | tf_op jit(solution)/shard_map/ppermute | solution.py:279
  162.8 20.4 %collective-permute-start.11 = (bf16[256,512]{1,0:T(8,128)(2,1)S(1)}, bf16[256,512]{1,0:T(8,128)(2,1)S(1)}, u32[]{:S(2)}, u32[]{:S(2)}) collective-permute-start(bf16[256,512]{1,0:T(8,128)(2,1)S(1)} %get-tuple-element.37), channel_id=1, source_target_pairs={{0,2},{1,3},{2,0},{3,1},{4,6},{5,7},{6,4},{7,5},{8,10},{9,11},{10,... | collective-permute-start | bytes 786440 | tf_op jit(solution)/shard_map/ppermute | solution.py:279
  179.7 1.9 collective-permute-start.38
  180.7 19.3 %collective-permute-start.24 = (bf16[2,2,144,512]{3,2,1,0:T(8,128)(2,1)}, bf16[2,2,144,512]{3,2,1,0:T(8,128)(2,1)}, u32[]{:S(2)}, u32[]{:S(2)}) collective-permute-start(bf16[2,2,144,512]{3,2,1,0:T(8,128)(2,1)} %slice.154), channel_id=1, source_target_pairs={{0,8},{4,12},{8,0},{12,4},{16,24},{20,28},{24,16},{28,20},{1,9},{5... | collective-permute-start | bytes 1769480 | tf_op jit(solution)/shard_map/ppermute | solution.py:279
  181.7 3.7 %collective-permute-start.39 = (f32[2,4,512]{2,0,1:T(2,128)S(1)}, f32[2,4,512]{2,0,1:T(2,128)S(1)}, u32[]{:S(2)}, u32[]{:S(2)}) collective-permute-start(f32[2,4,512]{2,0,1:T(2,128)S(1)} %fusion.3), channel_id=1, source_target_pairs={{0,2},{1,3},{2,0},{3,1},{4,6},{5,7},{6,4},{7,5},{8,10},{9,11},{10,... | collective-permute-start | bytes 49160 | tf_op jit(solution)/shard_map/ppermute | solution.py:279
  184.1 17.2 %collective-permute-start.12 = (bf16[2,256,512]{2,1,0:T(8,128)(2,1)}, bf16[2,256,512]{2,1,0:T(8,128)(2,1)}, u32[]{:S(2)}, u32[]{:S(2)}) collective-permute-start(bf16[2,256,512]{2,1,0:T(8,128)(2,1)} %get-tuple-element.95), channel_id=1, source_target_pairs={{0,1},{1,0},{2,3},{3,2},{4,5},{5,4},{6,7},{7,6},{8,9},{9,8},{10,11... | collective-permute-start | bytes 1572872 | tf_op jit(solution)/shard_map/ppermute | solution.py:279
  184.1 18.9 %collective-permute-start.30 = (bf16[8,2,64,384]{3,2,1,0:T(8,128)(2,1)}, bf16[8,2,64,384]{3,2,1,0:T(8,128)(2,1)}, u32[]{:S(2)}, u32[]{:S(2)}) collective-permute-start(bf16[8,2,64,384]{3,2,1,0:T(8,128)(2,1)} %get-tuple-element.51), channel_id=1, source_target_pairs={{0,1},{1,0},{2,3},{3,2},{4,5},{5,4},{6,7},{7,6},{8,9},{9,8},{10,11... | collective-permute-start | bytes 2359304 | tf_op jit(solution)/shard_map/ppermute | solution.py:279
  185.5 3.8 %collective-permute-start.40 = (f32[2,4,512]{2,0,1:T(2,128)S(1)}, f32[2,4,512]{2,0,1:T(2,128)S(1)}, u32[]{:S(2)}, u32[]{:S(2)}) collective-permute-start(f32[2,4,512]{2,0,1:T(2,128)S(1)} %fusion.10), channel_id=1, source_target_pairs={{0,4},{4,0},{8,12},{12,8},{16,20},{20,16},{24,28},{28,24},{1,5},{5... | collective-permute-start | bytes 49160 | tf_op jit(solution)/shard_map/ppermute | solution.py:279
  189.3 7.7 %collective-permute-start.41 = (f32[2,4,512]{2,0,1:T(2,128)S(1)}, f32[2,4,512]{2,0,1:T(2,128)S(1)}, u32[]{:S(2)}, u32[]{:S(2)}) collective-permute-start(f32[2,4,512]{2,0,1:T(2,128)S(1)} %add.111), channel_id=1, source_target_pairs={{0,8},{4,12},{8,0},{12,4},{16,24},{20,28},{24,16},{28,20},{1,9},{5... | collective-permute-start | bytes 49160 | tf_op jit(solution)/shard_map/ppermute | solution.py:279
  190.6 32.1 %collective-permute-start.20 = (bf16[256,512]{1,0:T(8,128)(2,1)S(1)}, bf16[256,512]{1,0:T(8,128)(2,1)S(1)}, u32[]{:S(2)}, u32[]{:S(2)}) collective-permute-start(bf16[256,512]{1,0:T(8,128)(2,1)S(1)} %get-tuple-element.45), channel_id=1, source_target_pairs={{0,2},{1,3},{2,0},{3,1},{4,6},{5,7},{6,4},{7,5},{8,10},{9,11},{10,... | collective-permute-start | bytes 786440 | tf_op jit(solution)/shard_map/ppermute | solution.py:279
  197.0 5.4 %collective-permute-start.42 = (f32[2,4,512]{2,0,1:T(2,128)S(1)}, f32[2,4,512]{2,0,1:T(2,128)S(1)}, u32[]{:S(2)}, u32[]{:S(2)}) collective-permute-start(f32[2,4,512]{2,0,1:T(2,128)S(1)} %add.112), channel_id=1, source_target_pairs={{0,16},{4,20},{8,24},{12,28},{16,0},{20,4},{24,8},{28,12},{1,17},{... | collective-permute-start | bytes 49160 | tf_op jit(solution)/shard_map/ppermute | solution.py:279
  201.2 15.5 %collective-permute-start.25 = (bf16[1,2,144,512]{3,2,1,0:T(8,128)(2,1)S(1)}, bf16[1,2,144,512]{3,2,1,0:T(8,128)(2,1)S(1)}, u32[]{:S(2)}, u32[]{:S(2)}) collective-permute-start(bf16[1,2,144,512]{3,2,1,0:T(8,128)(2,1)S(1)} %slice.156), channel_id=1, source_target_pairs={{0,16},{4,20},{8,24},{12,28},{16,0},{20,4},{24,8},{28,12},{1,17},{... | collective-permute-start | bytes 884744 | tf_op jit(solution)/shard_map/ppermute | solution.py:279
  204.5 13.8 %collective-permute-start.31 = (bf16[4,2,64,384]{3,2,1,0:T(8,128)(2,1)S(1)}, bf16[4,2,64,384]{3,2,1,0:T(8,128)(2,1)S(1)}, u32[]{:S(2)}, u32[]{:S(2)}) collective-permute-start(bf16[4,2,64,384]{3,2,1,0:T(8,128)(2,1)S(1)} %slice.160), channel_id=1, source_target_pairs={{0,4},{4,0},{8,12},{12,8},{16,20},{20,16},{24,28},{28,24},{1,5},{5... | collective-permute-start | bytes 1179656 | tf_op jit(solution)/shard_map/ppermute | solution.py:279
  216.7 5.8 %collective-permute-start.26 = (bf16[1,144,512]{2,1,0:T(8,128)(2,1)S(1)}, bf16[1,144,512]{2,1,0:T(8,128)(2,1)S(1)}, u32[]{:S(2)}, u32[]{:S(2)}) collective-permute-start(bf16[1,144,512]{2,1,0:T(8,128)(2,1)S(1)} %get-tuple-element.97), channel_id=1, source_target_pairs={{0,2},{1,3},{2,0},{3,1},{4,6},{5,7},{6,4},{7,5},{8,10},{9,11},{10,... | collective-permute-start | bytes 442376 | tf_op jit(solution)/shard_map/ppermute | solution.py:279
  218.4 6.6 %collective-permute-start.32 = (bf16[2,2,64,384]{3,2,1,0:T(8,128)(2,1)S(1)}, bf16[2,2,64,384]{3,2,1,0:T(8,128)(2,1)S(1)}, u32[]{:S(2)}, u32[]{:S(2)}) collective-permute-start(bf16[2,2,64,384]{3,2,1,0:T(8,128)(2,1)S(1)} %slice.162), channel_id=1, source_target_pairs={{0,8},{4,12},{8,0},{12,4},{16,24},{20,28},{24,16},{28,20},{1,9},{5... | collective-permute-start | bytes 589832 | tf_op jit(solution)/shard_map/ppermute | solution.py:279
  222.6 16.2 %collective-permute-start.27 = (bf16[1,2,144,512]{3,2,1,0:T(8,128)(2,1)S(1)}, bf16[1,2,144,512]{3,2,1,0:T(8,128)(2,1)S(1)}, u32[]{:S(2)}, u32[]{:S(2)}) collective-permute-start(bf16[1,2,144,512]{3,2,1,0:T(8,128)(2,1)S(1)} %pad_maximum_fusion.11), channel_id=1, source_target_pairs={{0,16},{4,20},{8,24},{12,28},{16,0},{20,4},{24,8},{28,12},{1,17},{... | collective-permute-start | bytes 884744 | tf_op jit(solution)/shard_map/ppermute | solution.py:279
  222.8 18.7 %collective-permute-start.21 = (bf16[2,256,512]{2,1,0:T(8,128)(2,1)S(1)}, bf16[2,256,512]{2,1,0:T(8,128)(2,1)S(1)}, u32[]{:S(2)}, u32[]{:S(2)}) collective-permute-start(bf16[2,256,512]{2,1,0:T(8,128)(2,1)S(1)} %get-tuple-element.93), channel_id=1, source_target_pairs={{0,1},{1,0},{2,3},{3,2},{4,5},{5,4},{6,7},{7,6},{8,9},{9,8},{10,11... | collective-permute-start | bytes 1572872 | tf_op jit(solution)/shard_map/ppermute | solution.py:279
  225.1 15.8 %collective-permute-start.33 = (bf16[1,2,64,384]{3,2,1,0:T(8,128)(2,1)S(1)}, bf16[1,2,64,384]{3,2,1,0:T(8,128)(2,1)S(1)}, u32[]{:S(2)}, u32[]{:S(2)}) collective-permute-start(bf16[1,2,64,384]{3,2,1,0:T(8,128)(2,1)S(1)} %slice.164), channel_id=1, source_target_pairs={{0,16},{4,20},{8,24},{12,28},{16,0},{20,4},{24,8},{28,12},{1,17},{... | collective-permute-start | bytes 294920 | tf_op jit(solution)/shard_map/ppermute | solution.py:279
  238.9 17.3 %collective-permute-start.28 = (bf16[2,2,144,512]{3,2,1,0:T(8,128)(2,1)S(1)}, bf16[2,2,144,512]{3,2,1,0:T(8,128)(2,1)S(1)}, u32[]{:S(2)}, u32[]{:S(2)}) collective-permute-start(bf16[2,2,144,512]{3,2,1,0:T(8,128)(2,1)S(1)} %pad_maximum_fusion.7), channel_id=1, source_target_pairs={{0,8},{4,12},{8,0},{12,4},{16,24},{20,28},{24,16},{28,20},{1,9},{5... | collective-permute-start | bytes 1769480 | tf_op jit(solution)/shard_map/ppermute | solution.py:279
  240.9 4.2 %collective-permute-start.34 = (bf16[1,64,384]{2,1,0:T(8,128)(2,1)S(1)}, bf16[1,64,384]{2,1,0:T(8,128)(2,1)S(1)}, u32[]{:S(2)}, u32[]{:S(2)}) collective-permute-start(bf16[1,64,384]{2,1,0:T(8,128)(2,1)S(1)} %get-tuple-element.107), channel_id=1, source_target_pairs={{0,2},{1,3},{2,0},{3,1},{4,6},{5,7},{6,4},{7,5},{8,10},{9,11},{10,... | collective-permute-start | bytes 147464 | tf_op jit(solution)/shard_map/ppermute | solution.py:279
  245.1 12.5 %collective-permute-start.35 = (bf16[1,2,64,384]{3,2,1,0:T(8,128)(2,1)S(1)}, bf16[1,2,64,384]{3,2,1,0:T(8,128)(2,1)S(1)}, u32[]{:S(2)}, u32[]{:S(2)}) collective-permute-start(bf16[1,2,64,384]{3,2,1,0:T(8,128)(2,1)S(1)} %pad_maximum_fusion.15), channel_id=1, source_target_pairs={{0,16},{4,20},{8,24},{12,28},{16,0},{20,4},{24,8},{28,12},{1,17},{... | collective-permute-start | bytes 294920 | tf_op jit(solution)/shard_map/ppermute | solution.py:279
  256.3 35.5 %collective-permute-start.29 = (bf16[4,2,144,512]{3,2,1,0:T(8,128)(2,1)S(1)}, bf16[4,2,144,512]{3,2,1,0:T(8,128)(2,1)S(1)}, u32[]{:S(2)}, u32[]{:S(2)}) collective-permute-start(bf16[4,2,144,512]{3,2,1,0:T(8,128)(2,1)S(1)} %pad_maximum_fusion.2), channel_id=1, source_target_pairs={{0,4},{4,0},{8,12},{12,8},{16,20},{20,16},{24,28},{28,24},{1,5},{5... | collective-permute-start | bytes 3538952 | tf_op jit(solution)/shard_map/ppermute | solution.py:279
  257.6 5.7 %collective-permute-start.36 = (bf16[2,2,64,384]{3,2,1,0:T(8,128)(2,1)S(1)}, bf16[2,2,64,384]{3,2,1,0:T(8,128)(2,1)S(1)}, u32[]{:S(2)}, u32[]{:S(2)}) collective-permute-start(bf16[2,2,64,384]{3,2,1,0:T(8,128)(2,1)S(1)} %pad_maximum_fusion.14), channel_id=1, source_target_pairs={{0,8},{4,12},{8,0},{12,4},{16,24},{20,28},{24,16},{28,20},{1,9},{5... | collective-permute-start | bytes 589832 | tf_op jit(solution)/shard_map/ppermute | solution.py:279
  263.4 28.4 %collective-permute-start.37 = (bf16[4,2,64,384]{3,2,1,0:T(8,128)(2,1)S(1)}, bf16[4,2,64,384]{3,2,1,0:T(8,128)(2,1)S(1)}, u32[]{:S(2)}, u32[]{:S(2)}) collective-permute-start(bf16[4,2,64,384]{3,2,1,0:T(8,128)(2,1)S(1)} %pad_maximum_fusion.10), channel_id=1, source_target_pairs={{0,4},{4,0},{8,12},{12,8},{16,20},{20,16},{24,28},{28,24},{1,5},{5... | collective-permute-start | bytes 1179656 | tf_op jit(solution)/shard_map/ppermute | solution.py:279
  291.9 6.0 %copy-start.1 = (bf16[2,256,2,512]{3,2,1,0:T(2,128)(2,1)S(1)}, bf16[2,256,2,512]{3,2,1,0:T(2,128)(2,1)}, u32[]{:S(2)}) copy-start(bf16[2,256,2,512]{3,2,1,0:T(2,128)(2,1)} %param.13) | copy-start | bytes 3145732

commit v2 on v1

v2 whole, which is shorter than its diff:
```python
import math

import jax
import jax.numpy as jnp
from jax import lax
from jax.experimental import pallas as pl
from jax.experimental.pallas import tpu as pltpu
from jax.sharding import PartitionSpec as P

HEAD_DIM = 64
EPS = 1e-05
BF = jnp.bfloat16
F32 = jnp.float32
VMEM_LIMIT = 50 * 1024 * 1024
OPT = {}


def tied(name, value, *deps, default=1):
    return tie(value, *deps) if OPT.get(name, default) else value


GROUP = 4
RUP, RDOWN, ROUT = 128, 128, 32
ROWS = RUP + RDOWN + ROUT
DU_AT, H_AT, B_AT, DZ_AT, O_AT, ALL = 0, 1024, 2048, 2560, 3072, 3328
RGAIN = 16
C_GELU = math.sqrt(2.0 / math.pi)


def dot(a, b, ca=1, cb=0):
    return lax.dot_general(a, b, (((ca,), (cb,)), ((), ())), preferred_element_type=F32)


def norm_parts(v):
    center = v - jnp.mean(v, axis=-1, keepdims=True)
    inv = lax.rsqrt(jnp.mean(center * center, axis=-1, keepdims=True) + EPS)
    return center * inv, inv


def norm_back(dout, hat, inv, gain):
    e = dout * gain
    mean_e = jnp.mean(e, axis=-1, keepdims=True)
    mean_eh = jnp.mean(e * hat, axis=-1, keepdims=True)
    return (e - mean_e - hat * mean_eh) * inv


def vspec():
    return pl.BlockSpec(memory_space=pltpu.VMEM)


def sspec():
    return pl.BlockSpec(memory_space=pltpu.SMEM)


def call(kernel, outs, scalars, args, scratch=(), us=1.0, name=None, after=()):
    us = OPT.get('us_' + name, us) if name else us
    count = len(args) + 1

    def run(*refs):
        kernel(*refs[:count], *refs[count + len(after):])

    return pl.pallas_call(
        run,
        out_shape=[jax.ShapeDtypeStruct(s, d) for s, d in outs],
        in_specs=[sspec()] + [vspec()] * len(args) + [pl.BlockSpec(memory_space=pl.ANY)] * len(after),
        out_specs=[vspec()] * len(outs),
        scratch_shapes=list(scratch),
        compiler_params=pltpu.CompilerParams(vmem_limit_bytes=VMEM_LIMIT),
        cost_estimate=pl.CostEstimate(flops=int(us * 1.1e9), bytes_accessed=0, transcendentals=0),
    )(scalars, *args, *after)


def pick_shard(sc, wo, wy, wc, w_s):
    for e, ref in enumerate((wo, wc, wy, wc)):
        @pl.when(sc[0] == e)
        def _(ref=ref):
            w_s[...] = ref[...]


def project_kernel(sc, x0, x1, x2, x3, wo, wy, wc, gain, bias, qkv, a_out, w_s):
    pick_shard(sc, wo, wy, wc, w_s)
    g = gain[pl.ds(sc[1], 1), :]
    b = bias[pl.ds(sc[1], 1), :]
    for k, ref in enumerate((x0, x1, x2, x3)):
        hat, _ = norm_parts(ref[...].astype(F32))
        a = (hat * g + b).astype(BF)
        out = dot(a, w_s[...])
        rows = pl.ds(k * ref.shape[0], ref.shape[0])
        a_out[rows, :] = a
        qkv[rows, 0:128] = (out[:, 0:128].astype(BF).astype(F32) * (1.0 / math.sqrt(HEAD_DIM))).astype(BF)
        qkv[rows, 128:384] = out[:, 128:384].astype(BF)


def attend_block(k, vt, qm, m_s, l_s, acc, qb, first):
    n = qm.shape[1]
    for h in range(2):
        rows = slice(h * HEAD_DIM, (h + 1) * HEAD_DIM)

        def block(b, _, h=h, rows=rows):
            cols = pl.ds(pl.multiple_of(b * qb, qb), qb)
            st = dot(k, qm[h, cols, :], 1, 1)
            m = jnp.max(st, axis=0, keepdims=True)
            if not first:
                old = m_s[h:h + 1, cols]
                m = jnp.maximum(old, m)
            pt = jnp.exp(st - m)
            total = jnp.sum(pt, axis=0, keepdims=True)
            new = dot(vt[rows, :], pt.astype(BF))
            if not first:
                fix = jnp.exp(old - m)
                total = total + l_s[h:h + 1, cols] * fix
                new = new + acc[rows, cols] * fix
            m_s[h:h + 1, cols] = m
            l_s[h:h + 1, cols] = total
            acc[rows, cols] = new
            return 0

        lax.fori_loop(0, n // qb, block, 0)


def split_heads(value, dst):
    lane = lax.broadcasted_iota(jnp.int32, value.shape, 1)
    zero = jnp.zeros_like(value)
    dst[0] = jnp.where(lane < HEAD_DIM, value, zero)
    dst[1] = jnp.where(lane < HEAD_DIM, zero, value)


def attend_own_kernel(qb, act, qkv, qm, m_s, l_s, acc, vt):
    split_heads(qkv[:, 0:128], qm)
    vt[...] = qkv[:, 256:384].T
    attend_block(qkv[:, 128:256], vt, qm, m_s, l_s, acc, qb, True)


def attend_cross_kernel(qb, act, qm, m_in, l_in, acc_in, *refs):
    kvx = refs[:-7]
    o_out, ot_out, lse_out, m_s, l_s, acc, vt = refs[-7:]
    m_s[...] = m_in[...]
    l_s[...] = l_in[...]
    acc[...] = acc_in[...]
    for r, kv in enumerate(kvx):
        @pl.when(act[r + 1] != 0)
        def _(kv=kv):
            vt[...] = kv[:, 128:256].T
            attend_block(kv[:, 0:128], vt, qm, m_s, l_s, acc, qb, False)
    for h in range(2):
        rows = slice(h * HEAD_DIM, (h + 1) * HEAD_DIM)
        ot_out[rows, :] = acc[rows, :] / l_s[h:h + 1, :]
        lse_out[h:h + 1, :] = m_s[h:h + 1, :] + jnp.log(l_s[h:h + 1, :])
    o_out[...] = ot_out[...].T.astype(BF)


def back_block(k, v, qm, dom, lse, delta, kt, dk_s, dv_s, dqt, qb):
    kt[...] = k.T
    dk_s[...] = jnp.zeros_like(dk_s)
    dv_s[...] = jnp.zeros_like(dv_s)
    n = qm.shape[1]
    for h in range(2):
        rows = slice(h * HEAD_DIM, (h + 1) * HEAD_DIM)

        def block(b, _, h=h, rows=rows):
            cols = pl.ds(pl.multiple_of(b * qb, qb), qb)
            qh = qm[h, cols, :]
            dh = dom[h, cols, :]
            pt = jnp.exp(dot(k, qh, 1, 1) - lse[h:h + 1, cols])
            dv_s[...] += dot(pt.astype(BF), dh)
            dst = (pt * (dot(v, dh, 1, 1) - delta[h:h + 1, cols])).astype(BF)
            dk_s[...] += dot(dst, qh)
            dqt[rows, cols] += dot(kt[rows, :], dst)
            return 0

        lax.fori_loop(0, n // qb, block, 0)


def back_cross_kernel(qb, frames, act, d0, d1, d2, d3, qm, ot, lse, *refs):
    kvx, refs = refs[:frames - 1], refs[frames - 1:]
    dkv_x, (dom, delta, dqt, kt, dk_s, dv_s) = refs[:frames - 1], refs[frames - 1:]
    seg = d0.shape[0]
    for k, ref in enumerate((d0, d1, d2, d3)):
        cols = slice(k * seg, (k + 1) * seg)
        d = ref[...]
        split_heads(d, dom.at[:, cols, :])
        dt = d.astype(F32).T * ot[:, cols]
        for h in range(2):
            delta[h:h + 1, cols] = jnp.sum(dt[h * HEAD_DIM:(h + 1) * HEAD_DIM, :], axis=0, keepdims=True)
    dqt[...] = jnp.zeros_like(dqt)
    for r in range(frames - 1):
        @pl.when(act[r + 1] != 0)
        def _(r=r):
            back_block(kvx[r][:, 0:128], kvx[r][:, 128:256], qm, dom, lse, delta, kt, dk_s, dv_s, dqt, qb)
            dkv_x[r][:, 0:128] = dk_s[...].astype(BF)
            dkv_x[r][:, 128:256] = dv_s[...].astype(BF)

        @pl.when(act[r + 1] == 0)
        def _(r=r):
            dkv_x[r][...] = jnp.zeros_like(dkv_x[r])


def back_own_kernel(qb, act, qkv, qm, dom, lse, delta, dqt_in, dq_out, dkv_own, dqt, kt, dk_s, dv_s):
    dqt[...] = dqt_in[...]
    back_block(qkv[:, 128:256], qkv[:, 256:384], qm, dom, lse, delta, kt, dk_s, dv_s, dqt, qb)
    dkv_own[:, 0:128] = dk_s[...]
    dkv_own[:, 128:256] = dv_s[...]
    dq_out[...] = (dqt[...].T * (1.0 / math.sqrt(HEAD_DIM))).astype(BF)


def gelu_parts(u):
    t = jnp.tanh(C_GELU * (u + 0.044715 * (u * u * u)))
    value = 0.5 * u * (1.0 + t)
    slope = 0.5 * (1.0 + t) + 0.5 * u * (1.0 - t * t) * (C_GELU * (1.0 + 3 * 0.044715 * (u * u)))
    return value, slope


def middle_kernel(sc, x, g, o0, o1, o2, o3, w0, w1, w2, w3, gain, bias, do_out, lout, keep, send, dy_out, gains, wo_s, o_s):
    mats = (w0, w1, w2, w3)
    for e in range(4):
        wo_s[e] = mats[e][1024:1152, :]
    gain_row = gain[pl.ds(sc[1], 1), :]
    mid = x[...].astype(F32)
    for k, ref in enumerate((o0, o1, o2, o3)):
        o_s[k] = ref[...]
        mid = mid + dot(ref[...], wo_s[sc[0] ^ k])
    hat, inv = norm_parts(mid)
    b = (hat * gain_row + bias[pl.ds(sc[1], 1), :]).astype(BF)
    cot = g[...]
    dy_out[...] = mid
    db = jnp.zeros_like(mid)
    for e in range(4):
        up = mats[e][0:512, :]
        down = mats[e][512:1024, :]
        value, slope = gelu_parts(dot(b, up))
        h = value.astype(BF)
        pack, spot = (keep, send)[e % 2], 512 * (e // 2)
        pack[:, H_AT + spot:H_AT + spot + 512] = h
        dy_out[...] += dot(h, down)
        du = (dot(cot, down, 1, 1) * slope).astype(BF)
        pack[:, DU_AT + spot:DU_AT + spot + 512] = du
        db = db + dot(du, up, 1, 1)
    lout[...] = dy_out[...].astype(BF)
    gains[0:1, :] = jnp.sum(db * hat, axis=0, keepdims=True)
    gains[1:2, :] = jnp.sum(db, axis=0, keepdims=True)
    dy = cot.astype(F32) + norm_back(db, hat, inv, gain_row)
    dy_out[...] = dy
    dz = dy.astype(BF)
    for e in range(4):
        pack, spot = (keep, send)[e % 2], 128 * (e // 2)
        pack[:, O_AT + spot:O_AT + spot + 128] = o_s[sc[0] ^ e]
    for pack in (keep, send):
        pack[:, B_AT:B_AT + 512] = b
        pack[:, DZ_AT:DZ_AT + 512] = dz
    for k in range(4):
        do_out[k] = dot(dz, wo_s[sc[0] ^ k], 1, 1).astype(BF)


def store_pieces(dst, e, row, value, rows, sc):
    for a in range(GROUP):
        dst[a ^ sc[2], e, row:row + rows, :] = value[a * rows:(a + 1) * rows, :]


def grads_kernel(sc, mine, other, g_mine, g_other, out, both, g):
    n = mine.shape[0]
    both[0:n, :] = mine[...]
    both[n:2 * n, :] = other[...]
    g[0:n, :] = g_mine[...]
    g[n:2 * n, :] = g_other[...]
    for e in range(2):
        du = both[:, DU_AT + 512 * e:DU_AT + 512 * e + 512]
        h = both[:, H_AT + 512 * e:H_AT + 512 * e + 512]
        o = both[:, O_AT + 128 * e:O_AT + 128 * e + 128]
        store_pieces(out, e, 0, dot(both[:, B_AT:B_AT + 512], du, 0, 0).astype(BF), RUP, sc)
        store_pieces(out, e, RUP, dot(h, g[...], 0, 0).astype(BF), RDOWN, sc)
        store_pieces(out, e, RUP + RDOWN, dot(o, both[:, DZ_AT:DZ_AT + 512], 0, 0).astype(BF), ROUT, sc)


def grads_heads_kernel(sc, a, dqkv, keep, send):
    grad = dot(a[...], dqkv[...], 0, 0).astype(BF)
    size = grad.shape[0] // 2
    for n in range(2):
        @pl.when(sc[3] == n)
        def _(n=n):
            keep[...] = grad[n * size:(n + 1) * size, :]
            send[...] = grad[(1 - n) * size:(2 - n) * size, :]


def input_kernel(sc, x, dy, d0, d1, d2, d3, w0, w1, w2, w3, gain, bias, gains2, lout, pack, gains, w_s):
    mats = (w0, w1, w2, w3)
    for e in range(4):
        w_s[e] = mats[e][...]
    gain_row = gain[pl.ds(sc[1], 1), :]
    hat, inv = norm_parts(x[...].astype(F32))
    da = jnp.zeros_like(hat)
    for k, ref in enumerate((d0, d1, d2, d3)):
        da = da + dot(ref[...], w_s[sc[0] ^ k], 1, 1)
    n = x.shape[0]
    pack[0:n, :] = (dy[...] + norm_back(da, hat, inv, gain_row)).astype(BF)
    pack[n:2 * n, :] = lout[...]
    gains[...] = jnp.zeros_like(gains)
    gains[0:1, :] = jnp.sum(da * hat, axis=0, keepdims=True)
    gains[1:2, :] = jnp.sum(da, axis=0, keepdims=True)
    gains[2:4, :] = gains2[...]


def unpack_kernel(sc, p0, p1, p2, p3, up, down, out, gains):
    total = jnp.zeros((RGAIN, 512), F32)
    for k, src in enumerate((p0, p1, p2, p3)):
        a = k ^ sc[2]
        for rel in range(2):
            net, row = sc[1] ^ rel, rel * ROWS
            up[net, pl.ds(pl.multiple_of(a * RUP, RUP), RUP), :] = src[row:row + RUP, :].astype(F32)
            down[net, pl.ds(pl.multiple_of(a * RDOWN, RDOWN), RDOWN), :] = src[row + RUP:row + RUP + RDOWN, :].astype(F32)
            out[net, pl.ds(pl.multiple_of(a * ROUT, ROUT), ROUT), :] = src[row + RUP + RDOWN:row + ROWS, :].astype(F32)
        total = total + src[2 * ROWS:2 * ROWS + RGAIN, :].astype(F32)
    gains[sc[1]] = total[0:8, :]
    gains[sc[1] ^ 1] = total[8:16, :]


def unpack_heads_kernel(sc, mine, other, q, k, v):
    size = mine.shape[1]
    for rel in range(2):
        net = sc[1] ^ rel
        for core, src in enumerate((mine, other)):
            rows = pl.ds(pl.multiple_of((core ^ sc[3]) * size, size), size)
            q[net, rows, :] = src[rel, :, 0:128].astype(F32)
            k[net, rows, :] = src[rel, :, 128:256].astype(F32)
            v[net, rows, :] = src[rel, :, 256:384].astype(F32)


def swap(value, axis, size, bit):
    return lax.ppermute(value, axis, [(n, n ^ bit) for n in range(size)])


def tie(value, *deps):
    return lax.optimization_barrier((value, deps))[0]


def body(layer_in, cotangent, clip_of_frame, w_query, w_key, w_value, w_out, w_up, w_down, norm1_gain, norm1_bias, norm2_gain, norm2_bias):
    seq = lax.axis_size("seq")
    frames = seq // GROUP
    i = lax.axis_index("seq")
    j = lax.axis_index("tp")
    net, core = j // 2, j % 2
    spot, frame = i % GROUP, i // GROUP
    segment, width = layer_in.shape[1], layer_in.shape[3]
    rows = segment * GROUP
    whole = jnp.where(clip_of_frame[0, frames - 1] == 0, 0, 1)
    stream = whole ^ core

    def mine(array, stream):
        return lax.dynamic_slice(array, (net, 0, stream, 0), (1, segment, 1, width)).reshape(segment, width)

    x = mine(layer_in, stream)
    cot = mine(cotangent, stream)
    cot_other = mine(cotangent, 1 - stream)
    clips = lax.dynamic_index_in_dim(clip_of_frame, stream, 0, keepdims=False)
    marks = [lax.dynamic_index_in_dim(clips, frame ^ r, 0, keepdims=False) for r in range(frames)]
    act = jnp.stack([(mark == marks[0]).astype(jnp.int32) for mark in marks])
    sc = jnp.concatenate([jnp.stack([spot ^ j, net, spot, core]).astype(jnp.int32), act[1:]])

    def nets_of(parts, axis):
        packed = jnp.concatenate(parts, axis=axis)
        own = lax.dynamic_index_in_dim(packed, net, 0, keepdims=False)
        other = lax.dynamic_index_in_dim(packed, 1 - net, 0, keepdims=False)
        return own, other

    def across(value):
        return swap(value, "tp", 4, 2)

    def beside(value):
        return swap(value, "tp", 4, 1)

    def to_group(chunks, only=None):
        out = [chunks[0]]
        for k in range(1, GROUP):
            if only is None:
                out.append(swap(chunks[k], "seq", seq, k))
            else:
                pairs = [(n * 4 + t, (n ^ k) * 4 + t) for n in range(seq) for t in only]
                out.append(lax.ppermute(chunks[k], ("seq", "tp"), pairs))
        return out

    def chunks_of(array):
        return [array[k * segment:(k + 1) * segment] for k in range(GROUP)]

    paired = (0, 2) if frames == 2 else (0, 1, 2, 3)

    def cross(value, r):
        pairs = [(n * 4 + t, (n ^ (GROUP * r)) * 4 + t) for n in range(seq) for t in paired]
        return lax.ppermute(value, ("seq", "tp"), pairs)

    xs = to_group([x] * GROUP)
    head_own, head_other = nets_of([w_query, w_key, w_value], 2)
    spots = [(n * 4, n % GROUP) for n in range(seq)]
    unit_y = lax.ppermute(tie(head_other, x), ("seq", "tp"), [(n + p, n + (p ^ 2)) for n, p in spots])
    unit = jnp.where(spot == j, head_own, unit_y)
    unit_c = lax.ppermute(unit, ("seq", "tp"), [(n + q, n + (q ^ 1)) for n, p in spots for q in (p, p ^ 2)])
    rest_own, rest_other = nets_of([w_up, w_down, w_out], 1)
    rest_y = across(tie(rest_other, unit_y))

    qkv, a = call(project_kernel, [((rows, 384), BF), ((rows, width), BF)], sc, [*xs, head_own, unit_y, unit_c, norm1_gain, norm1_bias],
                  scratch=[pltpu.VMEM((width, 384), BF)], us=2, name="k1")
    qb = 256
    kvx = [cross(qkv[:, 128:384], r) for r in range(1, frames)]
    qm, m_own, l_own, acc_own = call(
        lambda *refs: attend_own_kernel(qb, *refs),
        [((2, rows, 128), BF), ((2, rows), F32), ((2, rows), F32), ((128, rows), F32)], act, [qkv],
        scratch=[pltpu.VMEM((128, rows), BF)], us=7, name="own")
    o, ot, lse = call(
        lambda *refs: attend_cross_kernel(qb, *refs),
        [((rows, 128), BF), ((128, rows), F32), ((2, rows), F32)], act, [qm, m_own, l_own, acc_own, *kvx],
        scratch=[pltpu.VMEM((2, rows), F32), pltpu.VMEM((2, rows), F32), pltpu.VMEM((128, rows), F32),
                 pltpu.VMEM((128, rows), BF)], us=7, name="cross")

    os = to_group(chunks_of(o))
    head_y = across(tied('head_y', head_other, rest_y))
    rest = [rest_own, beside(tied('rest_c', rest_own, m_own)), rest_y, beside(tied('rest_yc', rest_y, o))]
    do4, lout, keep, send, dy, gains2 = call(
        middle_kernel,
        [((GROUP, segment, 128), BF), ((segment, width), BF), ((segment, ALL), BF), ((segment, ALL), BF),
         ((segment, width), F32), ((2, width), F32)],
        sc, [x, cot, *os, *rest, norm2_gain, norm2_bias],
        scratch=[pltpu.VMEM((4, 128, width), BF), pltpu.VMEM((4, segment, 128), BF)], us=8, name="mid")
    dos = to_group([do4[k] for k in range(GROUP)])

    (chip,) = call(
        grads_kernel, [((GROUP, 2, ROWS, 512), BF)], sc, [keep, beside(send), cot, cot_other],
        scratch=[pltpu.VMEM((2 * segment, ALL), BF), pltpu.VMEM((2 * segment, width), BF)], us=4, name="grads")

    def add(*terms):
        total = terms[0].astype(F32)
        for term in terms[1:]:
            total = total + term.astype(F32)
        return total.astype(BF)

    def over_frames(value, *deps):
        bit = GROUP
        while bit < seq:
            value = add(value, tie(swap(value, "seq", seq, bit), *deps))
            bit *= 2
        return value

    def add_group(parts, *deps):
        return add(parts[0], *[tie(part, *deps) for part in parts[1:]])

    head_c = beside(tie(head_own, o))
    head_yc = beside(tie(head_y, chip))
    head = [head_own, head_c, head_y, head_yc]
    group = to_group([chip[k] for k in range(GROUP)])
    back = call(
        lambda *refs: back_cross_kernel(qb, frames, *refs),
        [((rows, 256), BF)] * (frames - 1) + [((2, rows, 128), BF), ((2, rows), F32), ((128, rows), F32)],
        tie(act, chip, head_c, head_y), [*dos, qm, ot, lse, *kvx],
        scratch=[pltpu.VMEM((128, rows), BF), pltpu.VMEM((rows, 128), F32), pltpu.VMEM((rows, 128), F32)], us=8, name="bx")
    dkv_x, (dom, delta, dqt) = back[:frames - 1], back[frames - 1:]
    dkv_far = [cross(dkv_x[r - 1], r) for r in range(1, frames)]
    dq, dkv_own = call(
        lambda *refs: back_own_kernel(qb, *refs),
        [((rows, 128), BF), ((rows, 256), F32)], tie(act, group[1], group[2], dqt, head_yc), [qkv, qm, dom, lse, delta, dqt],
        scratch=[pltpu.VMEM((128, rows), F32), pltpu.VMEM((128, rows), BF), pltpu.VMEM((rows, 128), F32),
                 pltpu.VMEM((rows, 128), F32)], us=8, name="bo")
    total = dkv_own
    for far in dkv_far:
        total = total + far.astype(F32)
    dqkv = jnp.concatenate([dq, total.astype(BF)], axis=1)
    ds = to_group(chunks_of(dqkv))

    keep_c, send_c = call(grads_heads_kernel, [((width // 2, 384), BF)] * 2, sc, [a, dqkv], us=2, name="kc")
    sum_c = add(keep_c, beside(send_c))
    mine = add(group[0], *[tied("mine", part, sum_c) for part in group[1:]])
    net_0 = mine[0]
    bit = GROUP
    got_0 = swap(net_0, "seq", seq, GROUP)
    got_c = swap(tied("c_mine", sum_c, mine), "seq", seq, GROUP)

    pack, gains = call(
        input_kernel, [((2 * segment, width), BF), ((RGAIN, width), F32)],
        tied("k5_m", sc, mine), [x, dy, *ds, *head, norm1_gain, norm1_bias, gains2, lout],
        scratch=[pltpu.VMEM((4, width, 384), BF)], us=2, name="k5")
    gains = tied('g_0', gains, got_0)
    gains = add(gains, beside(gains))
    cross_y = across(jnp.concatenate([mine[1], gains]))
    gains = jnp.where(jnp.arange(RGAIN)[:, None] < 8, gains, jnp.roll(cross_y[ROWS:], 8, axis=0))
    net_1 = jnp.concatenate([cross_y[:ROWS], gains])
    pack = tied('pack_y', pack, cross_y)
    pack_y = across(pack)
    sum_c = add(sum_c, tied("c2_y", got_c, cross_y))
    net_0 = add(net_0, tied("n0_y", got_0, cross_y))
    got_1 = swap(net_1, "seq", seq, GROUP)
    all_c = jnp.stack(to_group([tied('c_n1', sum_c, net_1)] * GROUP))
    all_c = tied('c_g1', all_c, got_1)
    net_1 = add(net_1, tied("n1_c", got_1, all_c, default=0))
    bit = 2 * GROUP
    while bit < seq:
        sum_c, net_0, net_1 = [add(value, swap(value, "seq", seq, bit)) for value in (sum_c, net_0, net_1)]
        bit *= 2
    all_g = to_group([tied("ag_py", jnp.concatenate([net_0, net_1]), pack_y, default=0)] * GROUP)

    def shard(number):
        return lax.dynamic_index_in_dim(all_c, spot ^ number, 0, keepdims=False)

    far_c = across(jnp.stack([shard(j ^ 2), shard(j ^ 3)]))
    mine_c = jnp.stack([shard(j), far_c[0]])
    other_c = beside(jnp.stack([shard(j ^ 1), far_c[1]]))

    def spread(own, far, own_c, far_c):
        out = []
        for n in range(2):
            near = net == n
            mine_n = jnp.where(near, own, far)
            other_n = jnp.where(near, own_c, far_c)
            out.append(jnp.stack([jnp.where(stream == s, mine_n, other_n) for s in range(2)], axis=1))
        return jnp.stack(out)

    pack = tied('pack_y', pack, cross_y)
    pack_y = across(pack)
    packs = [pack, pack_y, beside(tied('pc', pack, pack_y)), beside(pack_y)]
    input_grad = spread(*[part[:segment] for part in packs])
    layer_out = spread(*[part[segment:] for part in packs])
    gq, gk, gv = call(unpack_heads_kernel, [((2, 512, 128), F32)] * 3, sc, [mine_c, other_c], us=1, name="uc")
    up, down, out, gains = call(
        unpack_kernel, [((2, 512, 512), F32), ((2, 512, 512), F32), ((2, 128, 512), F32), ((2, 8, width), F32)],
        tie(sc, gq, layer_out, input_grad), all_g, us=3, name="up")
    return (layer_out, input_grad, gq, gk, gv, out, up, down, gains[:, 0], gains[:, 1], gains[:, 2], gains[:, 3])


def solution(mesh):
    tokens = P(None, "seq", None, None)
    columns = P(None, None, "tp")
    rows = P(None, "tp", None)
    return jax.shard_map(
        body,
        mesh=mesh,
        in_specs=(tokens, tokens, P(), columns, columns, columns, rows, columns, rows, P(), P(), P(), P()),
        out_specs=(tokens, tokens, columns, columns, columns, rows, columns, rows, P(), P(), P(), P()),
        check_vma=False,
    )
```

time: 298 us -> 203 us (0.68)
  waiting for transfers between devices: 170 us -> 69 us
  local copies, waits for them, and re-layouts: 14.4 us -> 23.6 us
  other arithmetic: 12.3 us -> 4.98 us
  starting transfers between devices: 47.4 us -> 50.7 us
    ppermute x41 -> x39, waiting for transfers between devices: 152 us -> 61 us  [swap(): return lax.ppermute(value, axis, [(n, n ^ bit) for n in range(size)])]
    ppermute x2, waiting for transfers between devices: 17.8 us -> 6.58 us  [cross(): return lax.ppermute(value, ('seq', 'tp'), pairs)]
    unnamed x40 -> x69, local copies, waits for them, and re-layouts: 8.27 us -> 16.5 us
    add x13 -> x0, other arithmetic: 5.38 us -> none  [the longest x2 3.78 us: sum_rows(): buf = keep + swap(send, 'tp', 4, 1)]
    ppermute x0 -> x2, starting transfers between devices: none -> 5.1 us  [the longest x1 3.79 us: body(): lax.ppermute(tie(head_other, x), ('seq', 'tp'), [(n + p, n + (p ^ 2)) for...]
    another operation x9 -> x12, other arithmetic: 5.03 us -> 1.96 us  [the longest x1 1.14 us: body(): all_c = jnp.stack(to_group([tied('c_n1', sum_c, net_1)] * GROUP))]
    ppermute x41 -> x39, starting transfers between devices: 37.3 us -> 35.7 us  [swap(): return lax.ppermute(value, axis, [(n, n ^ bit) for n in range(size)])]
    pallas_call x8 -> x11, Pallas kernels: 50.5 us -> 50.9 us  [call(): pl.pallas_call(run, out_shape=[jax.ShapeDtypeStruct(s, d) for s, d in out...]
  transfers between devices with their start and end apart: 43 -> 43, of which waited for: 26 -> 19; matrix products, arithmetic and copies ran while one was open for 6% -> 8% of each run, Pallas kernels for 12% -> 20%
where the time goes in v2:
time: 203 us
  waiting for transfers between devices  69 us (34%)
  Pallas kernels  50.9 us (25%)
  starting transfers between devices  50.7 us (25%)
  local copies, waits for them, and re-layouts  23.6 us (12%)
  other arithmetic  4.98 us (2%)
  between operations  3.42 us (2%)
    ppermute x39, waiting for transfers between devices, swap(): return lax.ppermute(value, axis, [(n, n ^ bit) for n in range(size)])  61 us
    pallas_call x11, Pallas kernels, call(): pl.pallas_call(run, out_shape=[jax.ShapeDtypeStruct(s, d) for s, d in out...  50.9 us
    ppermute x39, starting transfers between devices, swap(): return lax.ppermute(value, axis, [(n, n ^ bit) for n in range(size)])  35.7 us
    unnamed x69, local copies, waits for them, and re-layouts  16.5 us
    ppermute x2, starting transfers between devices, cross(): return lax.ppermute(value, ('seq', 'tp'), pairs)  9.82 us
    ppermute x2, waiting for transfers between devices, cross(): return lax.ppermute(value, ('seq', 'tp'), pairs)  6.58 us
  transfers between devices with their start and end apart: 43, of which 19 were waited for; matrix products, arithmetic and copies ran while one was open for 8% of the time, Pallas kernels for 20%

profile of v2, /device:TPU:0, one launch (start us, length us, event | category | flops | bytes accessed | tf_op | source)
XLA Modules:
  0.0 202.6 jit_solution(10128587292439307786)
XLA Ops:
  0.7 1.4 slice.116
  3.4 4.0 %collective-permute-start.2 = (bf16[256,512]{1,0:T(8,128)(2,1)S(1)}, bf16[256,512]{1,0:T(8,128)(2,1)S(1)}, u32[]{:S(2)}, u32[]{:S(2)}) collective-permute-start(bf16[256,512]{1,0:T(8,128)(2,1)S(1)} %bitcast.89), channel_id=1, source_target_pairs={{0,12},{4,8},{8,4},{12,0},{16,28},{20,24},{24,20},{28,16},{1,13},{... | collective-permute-start | bytes 786440 | tf_op jit(solution)/shard_map/ppermute | solution.py:328
  8.3 3.8 %collective-permute-start.3 = (bf16[512,384]{1,0:T(8,128)(2,1)S(1)}, bf16[512,384]{1,0:T(8,128)(2,1)S(1)}, u32[]{:S(2)}, u32[]{:S(2)}) collective-permute-start(bf16[512,384]{1,0:T(8,128)(2,1)S(1)} %dynamic-slice_bitcast_fusion.2), channel_id=1, source_target_pairs={{0,2},{5,7},{10,8},{15,13},{16,18},{21,23},{26,24},{31,29}} | collective-permute-start | bytes 1179656 | tf_op jit(solution)/shard_map/ppermute | solution.py:392
  14.2 1.3 constant_dynamic-update-slice_fusion.5
  15.5 1.3 constant_dynamic-update-slice_fusion.4
  16.9 1.4 collective-permute-done.3.refs_6_
  18.4 1.3 collective-permute-start.4
  19.9 2.5 %collective-permute-start.10 = (bf16[1152,512]{1,0:T(8,128)(2,1)S(1)}, bf16[1152,512]{1,0:T(8,128)(2,1)}, u32[]{:S(2)}, u32[]{:S(2)}) collective-permute-start(bf16[1152,512]{1,0:T(8,128)(2,1)S(1)} %get-tuple-element.75), channel_id=1, source_target_pairs={{0,2},{1,3},{2,0},{3,1},{4,6},{5,7},{6,4},{7,5},{8,10},{9,11},{10,... | collective-permute-start | bytes 3538952 | tf_op jit(solution)/shard_map/ppermute | solution.py:328
  22.5 0.7 copy-done.2
  23.2 0.9 copy-done.3
  24.2 1.9 shard_map.220
  26.1 1.0 copy-done.8
  27.1 4.5 %collective-permute-start.5 = (bf16[1024,256]{1,0:T(8,128)(2,1)S(1)}, bf16[1024,256]{1,0:T(8,128)(2,1)S(1)}, u32[]{:S(2)}, u32[]{:S(2)}) collective-permute-start(bf16[1024,256]{1,0:T(8,128)(2,1)S(1)} %slice.117), channel_id=1, source_target_pairs={{0,16},{2,18},{4,20},{6,22},{8,24},{10,26},{12,28},{14,30},{16,0},... | collective-permute-start | bytes 1572872 | tf_op jit(solution)/shard_map/ppermute | solution.py:387
  31.6 6.8 %shard_map.221 = (bf16[2,1024,128]{2,1,0:T(8,128)(2,1)S(1)}, f32[2,1024]{1,0:T(2,128)S(1)}, f32[2,1024]{1,0:T(2,128)S(1)}, f32[128,1024]{1,0:T(8,128)S(1)}) custom-call(s32[2]{0:T(128)S(1)} %pad_add_fusion.refs_0_, bf16[1024,384]{1,0:T(8,128)(2,1)S(1)} %get-tuple-element.68.refs_1_), custom_call_target="tpu_custom_call" | custom-call | flops 7699999744 | tf_op jit(solution)/shard_map/pallas_call | solution.py:62
  38.5 6.0 %collective-permute-done.5.refs_5_.refs_8_ = bf16[1024,256]{1,0:T(8,128)(2,1)S(1)} collective-permute-done((bf16[1024,256]{1,0:T(8,128)(2,1)S(1)}, bf16[1024,256]{1,0:T(8,128)(2,1)S(1)}, u32[]{:S(2)}, u32[]{:S(2)}) %collective-permute-start.5) | collective-permute-done | bytes 524320 | tf_op jit(solution)/shard_map/ppermute | solution.py:387
  44.4 7.0 %shard_map.222 = (bf16[1024,128]{1,0:T(8,128)(2,1)S(1)}, f32[128,1024]{1,0:T(8,128)S(1)}, f32[2,1024]{1,0:T(2,128)S(1)}) custom-call(s32[2]{0:T(128)S(1)} %pad_add_fusion.refs_0_, bf16[2,1024,128]{2,1,0:T(8,128)(2,1)S(1)} %get-tuple-element.69.refs_1_.refs_5_.refs_2_, f32[2,1024]{1,0:T(2,128)S(1)} %get-tuple-element.70.refs_2_, ...), custom_call_target="tpu_custom_call" | custom-call | flops 7699999744 | tf_op jit(solution)/shard_map/pallas_call | solution.py:62
  51.5 0.8 copy-done.13
  53.0 3.3 %collective-permute-start.6 = (bf16[256,128]{1,0:T(8,128)(2,1)S(1)}, bf16[256,128]{1,0:T(8,128)(2,1)S(1)}, u32[]{:S(2)}, u32[]{:S(2)}) collective-permute-start(bf16[256,128]{1,0:T(8,128)(2,1)S(1)} %get-tuple-element.183), channel_id=1, source_target_pairs={{0,4},{4,0},{8,12},{12,8},{16,20},{20,16},{24,28},{28,24},{1,5},{5... | collective-permute-start | bytes 196616 | tf_op jit(solution)/shard_map/ppermute | solution.py:328
  56.4 2.3 %constant_dynamic-slice_fusion.4 = (bf16[1,256,1,512]{3,2,1,0:T(2,128)(2,1)S(1)}, bf16[1,256,1,512]{3,2,1,0:T(2,128)(2,1)S(1)}) fusion(bf16[2,256,2,512]{3,2,1,0:T(2,128)(2,1)} %param.14, s32[]{:T(128)S(6)} %select_n.173, s32[]{:T(128)S(6)} %select_n.177, s32[]{:T(128)S(6)} %select_n.166), kind=kLoop, calls=%fused_computation.85 | loop fusion | bytes 1048588 | tf_op jit(solution)/shard_map/dynamic_slice | solution.py:348
  59.2 8.3 %shard_map.223 = (bf16[4,256,128]{2,1,0:T(8,128)(2,1)S(1)}, bf16[256,512]{1,0:T(8,128)(2,1)S(1)}, bf16[256,3328]{1,0:T(8,128)(2,1)}, bf16[256,3328]{1,0:T(8,128)...) custom-call(s32[5]{0:T(128)S(1)} %concatenate.25.refs_0_, bf16[256,512]{1,0:T(8,128)(2,1)S(1)} %bitcast.93, ...), custom_call_target="tpu_custom_call" | custom-call | flops 8800000000 | tf_op jit(solution)/shard_map/pallas_call | solution.py:62
  68.7 1.6 collective-permute-start.19
  70.3 1.4 collective-permute-start.18
  71.9 1.4 collective-permute-start.17
  73.4 1.5 copy-done.10
  74.8 3.4 %shard_map.224 = bf16[4,2,288,512]{3,2,1,0:T(8,128)(2,1)} custom-call(s32[5]{0:T(128)S(1)} %concatenate.25.refs_0_, bf16[256,3328]{1,0:T(8,128)(2,1)S(1)} %copy-done.10, bf16[256,3328]{1,0:T(8,128)(2,1)S(1)} %collective-permute-done.12.refs_2_, bf16[256,512]{1,0:T(8,128)(2,1)S(1)} %bitcast.96, bf16[256,512]{1,0:T(8,128)(2,1)S(1)} %bitcast.97), custom_call_target="tpu_custom_call" | custom-call | flops 4400000000 | tf_op jit(solution)/shard_map/pallas_call | solution.py:62
  78.2 1.6 slice_bitcast_fusion.1
  80.0 1.0 collective-permute-start.13
  81.1 7.8 %shard_map.225 = (bf16[1024,256]{1,0:T(8,128)(2,1)S(1)}, bf16[2,1024,128]{2,1,0:T(8,128)(2,1)S(1)}, f32[2,1024]{1,0:T(2,128)S(1)}, f32[128,1024]{1,0:T(8,128)S(1)}) custom-call(s32[2]{0:T(128)S(1)} %pad_add_fusion.refs_0_, bf16[256,128]{1,0:T(8,128)(2,1)S(1)} %get-tuple-element.180.refs_1_, bf16[256,128]{1,0:T(8,128)(2,1)S(1)} %collective-permute-done.17.refs_2_, ...), custom_call_target="tpu_custom_call" | custom-call | flops 8800000000 | tf_op jit(solution)/shard_map/pallas_call | solution.py:62
  88.9 5.3 %collective-permute-start.21 = (bf16[1024,256]{1,0:T(8,128)(2,1)S(1)}, bf16[1024,256]{1,0:T(8,128)(2,1)S(1)}, u32[]{:S(2)}, u32[]{:S(2)}) collective-permute-start(bf16[1024,256]{1,0:T(8,128)(2,1)S(1)} %get-tuple-element.93), channel_id=1, source_target_pairs={{0,16},{2,18},{4,20},{6,22},{8,24},{10,26},{12,28},{14,30},{16,0},... | collective-permute-start | bytes 1572872 | tf_op jit(solution)/shard_map/ppermute | solution.py:387
  94.5 3.0 %collective-permute-done.14 = bf16[2,288,512]{2,1,0:T(8,128)(2,1)S(1)} collective-permute-done((bf16[2,288,512]{2,1,0:T(8,128)(2,1)S(1)}, bf16[2,288,512]{2,1,0:T(8,128)(2,1)S(1)}, u32[]{:S(2)}, u32[]{:S(2)}) %collective-permute-start.14) | collective-permute-done | bytes 589856 | tf_op jit(solution)/shard_map/ppermute | solution.py:328
  97.5 7.8 %shard_map.226 = (bf16[1024,128]{1,0:T(8,128)(2,1)S(1)}, f32[1024,256]{1,0:T(8,128)S(1)}) custom-call(s32[2]{0:T(128)S(1)} %pad_add_fusion.refs_0_, bf16[1024,384]{1,0:T(8,128)(2,1)S(1)} %get-tuple-element.68.refs_1_, bf16[2,1024,128]{2,1,0:T(8,128)(2,1)S(1)} %copy-done.12, bf16[2,1024,128]{2,1,0:T(8,128)(2,1)S(1)} %get-tuple-element.89.refs_3_, ...), custom_call_target="tpu_custom_call" | custom-call | flops 8800000000 | tf_op jit(solution)/shard_map/pallas_call | solution.py:62
  106.2 1.0 copy-done.9
  107.2 1.5 shard_map.227
  108.9 3.4 %collective-permute-start.26 = (bf16[256,384]{1,0:T(8,128)(2,1)S(1)}, bf16[256,384]{1,0:T(8,128)(2,1)S(1)}, u32[]{:S(2)}, u32[]{:S(2)}) collective-permute-start(bf16[256,384]{1,0:T(8,128)(2,1)S(1)} %get-tuple-element.167), channel_id=1, source_target_pairs={{0,12},{4,8},{8,4},{12,0},{16,28},{20,24},{24,20},{28,16},{1,13},{... | collective-permute-start | bytes 589832 | tf_op jit(solution)/shard_map/ppermute | solution.py:328
  112.3 0.8 collective-permute-start.24
  113.1 1.5 collective-permute-done.23
  114.6 1.4 fusion.2
  116.1 1.5 collective-permute-start.27
  117.6 1.3 collective-permute-done.26.refs_6_
  118.9 3.7 %collective-permute-done.24.refs_4_ = bf16[256,384]{1,0:T(8,128)(2,1)S(1)} collective-permute-done((bf16[256,384]{1,0:T(8,128)(2,1)S(1)}, bf16[256,384]{1,0:T(8,128)(2,1)S(1)}, u32[]{:S(2)}, u32[]{:S(2)}) %collective-permute-start.24) | collective-permute-done | bytes 196640 | tf_op jit(solution)/shard_map/ppermute | solution.py:328
  122.6 4.6 %collective-permute-done.25.refs_5_ = bf16[256,384]{1,0:T(8,128)(2,1)S(1)} collective-permute-done((bf16[256,384]{1,0:T(8,128)(2,1)S(1)}, bf16[256,384]{1,0:T(8,128)(2,1)S(1)}, u32[]{:S(2)}, u32[]{:S(2)}) %collective-permute-start.25) | collective-permute-done | bytes 196640 | tf_op jit(solution)/shard_map/ppermute | solution.py:328
  127.2 1.6 shard_map.228
  128.8 2.4 %collective-permute-done.27 = bf16[288,512]{1,0:T(8,128)(2,1)S(1)} collective-permute-done((bf16[288,512]{1,0:T(8,128)(2,1)S(1)}, bf16[288,512]{1,0:T(8,128)(2,1)S(1)}, u32[]{:S(2)}, u32[]{:S(2)}) %collective-permute-start.27) | collective-permute-done | bytes 294944 | tf_op jit(solution)/shard_map/ppermute | solution.py:328
  131.2 1.2 collective-permute-done.28
  132.4 1.0 collective-permute-start.29
  133.5 11.8 %collective-permute-done.33 = bf16[256,384]{1,0:T(8,128)(2,1)S(1)} collective-permute-done((bf16[256,384]{1,0:T(8,128)(2,1)S(1)}, bf16[256,384]{1,0:T(8,128)(2,1)S(1)}, u32[]{:S(2)}, u32[]{:S(2)}) %collective-permute-start.33) | collective-permute-done | bytes 196640 | tf_op jit(solution)/shard_map/ppermute | solution.py:328
  145.4 0.7 pad_maximum_fusion.9
  146.2 2.2 %collective-permute-start.35 = (bf16[256,384]{1,0:T(8,128)(2,1)S(1)}, bf16[256,384]{1,0:T(8,128)(2,1)S(1)}, u32[]{:S(2)}, u32[]{:S(2)}) collective-permute-start(bf16[256,384]{1,0:T(8,128)(2,1)S(1)} %add_convert_fusion.3), channel_id=1, source_target_pairs={{0,8},{4,12},{8,0},{12,4},{16,24},{20,28},{24,16},{28,20},{1,9},{5... | collective-permute-start | bytes 589832 | tf_op jit(solution)/shard_map/ppermute | solution.py:328
  148.4 1.3 collective-permute-start.34
  149.7 1.1 collective-permute-start.30
  150.7 9.6 %collective-permute-done.36 = bf16[256,384]{1,0:T(8,128)(2,1)S(1)} collective-permute-done((bf16[256,384]{1,0:T(8,128)(2,1)S(1)}, bf16[256,384]{1,0:T(8,128)(2,1)S(1)}, u32[]{:S(2)}, u32[]{:S(2)}) %collective-permute-start.36) | collective-permute-done | bytes 196640 | tf_op jit(solution)/shard_map/ppermute | solution.py:328
  160.3 1.0 collective-permute-done.35
  162.1 1.1 pad_maximum_fusion.3
  163.2 1.9 collective-permute-done.37
  165.3 1.2 collective-permute-start.38
  167.4 3.2 %collective-permute-start.41 = (bf16[592,512]{1,0:T(8,128)(2,1)S(1)}, bf16[592,512]{1,0:T(8,128)(2,1)S(1)}, u32[]{:S(2)}, u32[]{:S(2)}) collective-permute-start(bf16[592,512]{1,0:T(8,128)(2,1)S(1)} %pad_maximum_fusion.4.refs_1_), channel_id=1, source_target_pairs={{0,8},{4,12},{8,0},{12,4},{16,24},{20,28},{24,16},{28,20},{1,9},{5... | collective-permute-start | bytes 1818632 | tf_op jit(solution)/shard_map/ppermute | solution.py:328
  170.6 3.4 %collective-permute-done.38 = bf16[2,256,384]{2,1,0:T(8,128)(2,1)S(1)} collective-permute-done((bf16[2,256,384]{2,1,0:T(8,128)(2,1)S(1)}, bf16[2,256,384]{2,1,0:T(8,128)(2,1)S(1)}, u32[]{:S(2)}, u32[]{:S(2)}) %collective-permute-start.38) | collective-permute-done | bytes 393248 | tf_op jit(solution)/shard_map/ppermute | solution.py:328
  174.0 1.6 collective-permute-start.40
  176.4 2.0 %copy.31 = bf16[2,256,2,512]{3,2,1,0:T(2,128)(2,1)} copy(bf16[2,256,2,512]{3,1,2,0:T(8,128)(2,1)S(1)} %pad_maximum_fusion.2) | data formatting | bytes 2097152
  178.6 2.0 %copy.30 = bf16[2,256,2,512]{3,2,1,0:T(2,128)(2,1)} copy(bf16[2,256,2,512]{3,1,2,0:T(8,128)(2,1)S(1)} %pad_maximum_fusion.1) | data formatting | bytes 2097152
  180.6 1.8 shard_map.229
  182.4 2.4 %collective-permute-done.42.refs_4_ = bf16[592,512]{1,0:T(8,128)(2,1)S(1)} collective-permute-done((bf16[592,512]{1,0:T(8,128)(2,1)S(1)}, bf16[592,512]{1,0:T(8,128)(2,1)S(1)}, u32[]{:S(2)}, u32[]{:S(2)}) %collective-permute-start.42) | collective-permute-done | bytes 606240 | tf_op jit(solution)/shard_map/ppermute | solution.py:328
  184.9 12.4 %collective-permute-done.41.refs_3_ = bf16[592,512]{1,0:T(8,128)(2,1)S(1)} collective-permute-done((bf16[592,512]{1,0:T(8,128)(2,1)S(1)}, bf16[592,512]{1,0:T(8,128)(2,1)S(1)}, u32[]{:S(2)}, u32[]{:S(2)}) %collective-permute-start.41) | collective-permute-done | bytes 606240 | tf_op jit(solution)/shard_map/ppermute | solution.py:328
  197.2 3.0 %shard_map.230 = (f32[2,512,512]{2,1,0:T(8,128)}, f32[2,512,512]{2,1,0:T(8,128)}, f32[2,128,512]{2,1,0:T(8,128)}, f32[2,8,512]{2,1,0:T(8,128)S(1)}) custom-call(s32[5]{0:T(128)S(1)} %concatenate.25.refs_0_, bf16[592,512]{1,0:T(8,128)(2,1)S(1)} %pad_maximum_fusion.4.refs_1_, bf16[592,512]{1,0:T(8,128)(2,1)S(1)} %collective-permute-done.40.refs_2_, ...), custom_call_target="tpu_custom_call" | custom-call | flops 3300000000 | tf_op jit(solution)/shard_map/pallas_call | solution.py:62
  (149 shorter events, 12.2 us)
Async XLA Ops:
  0.6 2.1 %copy-start = (bf16[2,256,2,512]{3,2,1,0:T(2,128)(2,1)S(1)}, bf16[2,256,2,512]{3,2,1,0:T(2,128)(2,1)}, u32[]{:S(2)}) copy-start(bf16[2,256,2,512]{3,2,1,0:T(2,128)(2,1)} %param.13) | copy-start | bytes 3145732
  0.7 7.4 %copy-start.21 = (bf16[2,512,128]{2,1,0:T(8,128)(2,1)S(1)}, bf16[2,512,128]{2,1,0:T(8,128)(2,1)}, u32[]{:S(2)}) copy-start(bf16[2,512,128]{2,1,0:T(8,128)(2,1)} %param.16) | copy-start | bytes 786436
  0.7 7.4 %copy-start.22 = (bf16[2,512,128]{2,1,0:T(8,128)(2,1)S(1)}, bf16[2,512,128]{2,1,0:T(8,128)(2,1)}, u32[]{:S(2)}) copy-start(bf16[2,512,128]{2,1,0:T(8,128)(2,1)} %param.17) | copy-start | bytes 786436
  0.7 7.5 %copy-start.23 = (bf16[2,512,128]{2,1,0:T(8,128)(2,1)S(1)}, bf16[2,512,128]{2,1,0:T(8,128)(2,1)}, u32[]{:S(2)}) copy-start(bf16[2,512,128]{2,1,0:T(8,128)(2,1)} %param.18) | copy-start | bytes 786436
  3.3 8.9 %copy-start.27 = (s32[2,2]{1,0:T(2,128)S(1)}, s32[2,2]{1,0:T(2,128)}, u32[]{:S(2)}) copy-start(s32[2,2]{1,0:T(2,128)} %param.15) | copy-start | bytes 52
  3.4 19.1 %collective-permute-start.2 = (bf16[256,512]{1,0:T(8,128)(2,1)S(1)}, bf16[256,512]{1,0:T(8,128)(2,1)S(1)}, u32[]{:S(2)}, u32[]{:S(2)}) collective-permute-start(bf16[256,512]{1,0:T(8,128)(2,1)S(1)} %bitcast.89), channel_id=1, source_target_pairs={{0,12},{4,8},{8,4},{12,0},{16,28},{20,24},{24,20},{28,16},{1,13},{... | collective-permute-start | bytes 786440 | tf_op jit(solution)/shard_map/ppermute | solution.py:328
  7.4 15.1 %collective-permute-start.1 = (bf16[256,512]{1,0:T(8,128)(2,1)S(1)}, bf16[256,512]{1,0:T(8,128)(2,1)S(1)}, u32[]{:S(2)}, u32[]{:S(2)}) collective-permute-start(bf16[256,512]{1,0:T(8,128)(2,1)S(1)} %bitcast.90), channel_id=1, source_target_pairs={{0,8},{4,12},{8,0},{12,4},{16,24},{20,28},{24,16},{28,20},{1,9},{5... | collective-permute-start | bytes 786440 | tf_op jit(solution)/shard_map/ppermute | solution.py:328
  7.9 14.6 %collective-permute-start = (bf16[256,512]{1,0:T(8,128)(2,1)S(1)}, bf16[256,512]{1,0:T(8,128)(2,1)S(1)}, u32[]{:S(2)}, u32[]{:S(2)}) collective-permute-start(bf16[256,512]{1,0:T(8,128)(2,1)S(1)} %bitcast.91), channel_id=1, source_target_pairs={{0,4},{4,0},{8,12},{12,8},{16,20},{20,16},{24,28},{28,24},{1,5},{5... | collective-permute-start | bytes 786440 | tf_op jit(solution)/shard_map/ppermute | solution.py:328
  8.3 8.5 %copy-start.17 = (bf16[512,384]{1,0:T(8,128)(2,1)}, bf16[512,384]{1,0:T(8,128)(2,1)S(1)}, u32[]{:S(2)}) copy-start(bf16[512,384]{1,0:T(8,128)(2,1)S(1)} %dynamic-slice_bitcast_fusion.2) | copy-start | bytes 1179652
  8.3 9.9 %collective-permute-start.3 = (bf16[512,384]{1,0:T(8,128)(2,1)S(1)}, bf16[512,384]{1,0:T(8,128)(2,1)S(1)}, u32[]{:S(2)}, u32[]{:S(2)}) collective-permute-start(bf16[512,384]{1,0:T(8,128)(2,1)S(1)} %dynamic-slice_bitcast_fusion.2), channel_id=1, source_target_pairs={{0,2},{5,7},{10,8},{15,13},{16,18},{21,23},{26,24},{31,29}} | collective-permute-start | bytes 1179656 | tf_op jit(solution)/shard_map/ppermute | solution.py:392
  14.2 2.7 %copy-start.24 = (bf16[2,128,512]{2,1,0:T(8,128)(2,1)S(1)}, bf16[2,128,512]{2,1,0:T(8,128)(2,1)}, u32[]{:S(2)}) copy-start(bf16[2,128,512]{2,1,0:T(8,128)(2,1)} %param.19) | copy-start | bytes 786436
  18.4 4.8 %collective-permute-start.4 = (bf16[512,384]{1,0:T(8,128)(2,1)S(1)}, bf16[512,384]{1,0:T(8,128)(2,1)S(1)}, u32[]{:S(2)}, u32[]{:S(2)}) collective-permute-start(bf16[512,384]{1,0:T(8,128)(2,1)S(1)} %get-tuple-element.146), channel_id=1, source_target_pairs={{0,1},{2,3},{5,4},{7,6},{10,11},{8,9},{15,14},{13,12},{16,17},{18,... | collective-permute-start | bytes 1179656 | tf_op jit(solution)/shard_map/ppermute | solution.py:394
  19.8 3.4 %copy-start.6 = (f32[2,512]{1,0:T(2,128)S(1)}, f32[2,512]{1,0:T(2,128)}, u32[]{:S(2)}) copy-start(f32[2,512]{1,0:T(2,128)} %refs_11_.3) | copy-start | bytes 12292
  19.8 3.4 %copy-start.7 = (f32[2,512]{1,0:T(2,128)S(1)}, f32[2,512]{1,0:T(2,128)}, u32[]{:S(2)}) copy-start(f32[2,512]{1,0:T(2,128)} %refs_12_.3) | copy-start | bytes 12292
  19.9 32.3 %collective-permute-start.10 = (bf16[1152,512]{1,0:T(8,128)(2,1)S(1)}, bf16[1152,512]{1,0:T(8,128)(2,1)}, u32[]{:S(2)}, u32[]{:S(2)}) collective-permute-start(bf16[1152,512]{1,0:T(8,128)(2,1)S(1)} %get-tuple-element.75), channel_id=1, source_target_pairs={{0,2},{1,3},{2,0},{3,1},{4,6},{5,7},{6,4},{7,5},{8,10},{9,11},{10,... | collective-permute-start | bytes 3538952 | tf_op jit(solution)/shard_map/ppermute | solution.py:328
  27.1 17.4 %collective-permute-start.5 = (bf16[1024,256]{1,0:T(8,128)(2,1)S(1)}, bf16[1024,256]{1,0:T(8,128)(2,1)S(1)}, u32[]{:S(2)}, u32[]{:S(2)}) collective-permute-start(bf16[1024,256]{1,0:T(8,128)(2,1)S(1)} %slice.117), channel_id=1, source_target_pairs={{0,16},{2,18},{4,20},{6,22},{8,24},{10,26},{12,28},{14,30},{16,0},... | collective-permute-start | bytes 1572872 | tf_op jit(solution)/shard_map/ppermute | solution.py:387
  38.4 13.1 %copy-start.11 = (bf16[2,1024,128]{2,1,0:T(8,128)(2,1)}, bf16[2,1024,128]{2,1,0:T(8,128)(2,1)S(1)}, u32[]{:S(2)}) copy-start(bf16[2,1024,128]{2,1,0:T(8,128)(2,1)S(1)} %get-tuple-element.69.refs_1_.refs_5_.refs_2_) | copy-start | bytes 1572868
  38.4 20.8 %collective-permute-start.9 = (bf16[1152,512]{1,0:T(8,128)(2,1)S(1)}, bf16[1152,512]{1,0:T(8,128)(2,1)}, u32[]{:S(2)}, u32[]{:S(2)}) collective-permute-start(bf16[1152,512]{1,0:T(8,128)(2,1)S(1)} %get-tuple-element.74.refs_7_), channel_id=1, source_target_pairs={{0,1},{1,0},{2,3},{3,2},{4,5},{5,4},{6,7},{7,6},{8,9},{9,8},{10,11... | collective-permute-start | bytes 3538952 | tf_op jit(solution)/shard_map/ppermute | solution.py:328
  52.3 6.9 %collective-permute-start.11 = (bf16[1152,512]{1,0:T(8,128)(2,1)}, bf16[1152,512]{1,0:T(8,128)(2,1)}, u32[]{:S(2)}, u32[]{:S(2)}) collective-permute-start(bf16[1152,512]{1,0:T(8,128)(2,1)} %collective-permute-done.10.refs_9_), channel_id=1, source_target_pairs={{0,1},{1,0},{2,3},{3,2},{4,5},{5,4},{6,7},{7,6},{8,9},{9,8},{10,11... | collective-permute-start | bytes 3538952 | tf_op jit(solution)/shard_map/ppermute | solution.py:328
  52.9 6.3 %copy-start.4 = (f32[2,512]{1,0:T(2,128)S(1)}, f32[2,512]{1,0:T(2,128)}, u32[]{:S(2)}) copy-start(f32[2,512]{1,0:T(2,128)} %refs_11_.2) | copy-start | bytes 12292
  52.9 6.4 %copy-start.5 = (f32[2,512]{1,0:T(2,128)S(1)}, f32[2,512]{1,0:T(2,128)}, u32[]{:S(2)}) copy-start(f32[2,512]{1,0:T(2,128)} %refs_12_.2) | copy-start | bytes 12292
  52.9 5.8 %collective-permute-start.8 = (bf16[256,128]{1,0:T(8,128)(2,1)S(1)}, bf16[256,128]{1,0:T(8,128)(2,1)S(1)}, u32[]{:S(2)}, u32[]{:S(2)}) collective-permute-start(bf16[256,128]{1,0:T(8,128)(2,1)S(1)} %get-tuple-element.181), channel_id=1, source_target_pairs={{0,12},{4,8},{8,4},{12,0},{16,28},{20,24},{24,20},{28,16},{1,13},{... | collective-permute-start | bytes 196616 | tf_op jit(solution)/shard_map/ppermute | solution.py:328
  52.9 5.8 %collective-permute-start.7 = (bf16[256,128]{1,0:T(8,128)(2,1)S(1)}, bf16[256,128]{1,0:T(8,128)(2,1)S(1)}, u32[]{:S(2)}, u32[]{:S(2)}) collective-permute-start(bf16[256,128]{1,0:T(8,128)(2,1)S(1)} %get-tuple-element.182), channel_id=1, source_target_pairs={{0,8},{4,12},{8,0},{12,4},{16,24},{20,28},{24,16},{28,20},{1,9},{5... | collective-permute-start | bytes 196616 | tf_op jit(solution)/shard_map/ppermute | solution.py:328
  53.0 6.2 %collective-permute-start.6 = (bf16[256,128]{1,0:T(8,128)(2,1)S(1)}, bf16[256,128]{1,0:T(8,128)(2,1)S(1)}, u32[]{:S(2)}, u32[]{:S(2)}) collective-permute-start(bf16[256,128]{1,0:T(8,128)(2,1)S(1)} %get-tuple-element.183), channel_id=1, source_target_pairs={{0,4},{4,0},{8,12},{12,8},{16,20},{20,16},{24,28},{28,24},{1,5},{5... | collective-permute-start | bytes 196616 | tf_op jit(solution)/shard_map/ppermute | solution.py:328
  59.2 9.0 %copy-start.18 = (bf16[512,384]{1,0:T(8,128)(2,1)S(1)}, bf16[512,384]{1,0:T(8,128)(2,1)}, u32[]{:S(2)}) copy-start(bf16[512,384]{1,0:T(8,128)(2,1)} %copy-done.17) | copy-start | bytes 1179652
  67.6 4.4 %collective-permute-start.12 = (bf16[256,3328]{1,0:T(8,128)(2,1)}, bf16[256,3328]{1,0:T(8,128)(2,1)S(1)}, u32[]{:S(2)}, u32[]{:S(2)}) collective-permute-start(bf16[256,3328]{1,0:T(8,128)(2,1)} %get-tuple-element.78), channel_id=1, source_target_pairs={{0,1},{1,0},{2,3},{3,2},{4,5},{5,4},{6,7},{7,6},{8,9},{9,8},{10,11... | collective-permute-start | bytes 5111816 | tf_op jit(solution)/shard_map/ppermute | solution.py:328
  67.6 12.2 %collective-permute-start.15 = (bf16[512,384]{1,0:T(8,128)(2,1)S(1)}, bf16[512,384]{1,0:T(8,128)(2,1)S(1)}, u32[]{:S(2)}, u32[]{:S(2)}) collective-permute-start(bf16[512,384]{1,0:T(8,128)(2,1)S(1)} %get-tuple-element.80.refs_5_.refs_7_), channel_id=1, source_target_pairs={{0,1},{1,0},{2,3},{3,2},{4,5},{5,4},{6,7},{7,6},{8,9},{9,8},{10,11... | collective-permute-start | bytes 1179656 | tf_op jit(solution)/shard_map/ppermute | solution.py:328
  68.2 11.7 %collective-permute-start.16 = (bf16[512,384]{1,0:T(8,128)(2,1)S(1)}, bf16[512,384]{1,0:T(8,128)(2,1)S(1)}, u32[]{:S(2)}, u32[]{:S(2)}) collective-permute-start(bf16[512,384]{1,0:T(8,128)(2,1)S(1)} %copy-done.18), channel_id=1, source_target_pairs={{0,2},{1,3},{2,0},{3,1},{4,6},{5,7},{6,4},{7,5},{8,10},{9,11},{10,... | collective-permute-start | bytes 1179656 | tf_op jit(solution)/shard_map/ppermute | solution.py:328
  68.7 11.3 %collective-permute-start.19 = (bf16[256,128]{1,0:T(8,128)(2,1)S(1)}, bf16[256,128]{1,0:T(8,128)(2,1)S(1)}, u32[]{:S(2)}, u32[]{:S(2)}) collective-permute-start(bf16[256,128]{1,0:T(8,128)(2,1)S(1)} %get-tuple-element.177), channel_id=1, source_target_pairs={{0,12},{4,8},{8,4},{12,0},{16,28},{20,24},{24,20},{28,16},{1,13},{... | collective-permute-start | bytes 196616 | tf_op jit(solution)/shard_map/ppermute | solution.py:328
  70.3 10.7 %collective-permute-start.18 = (bf16[256,128]{1,0:T(8,128)(2,1)S(1)}, bf16[256,128]{1,0:T(8,128)(2,1)S(1)}, u32[]{:S(2)}, u32[]{:S(2)}) collective-permute-start(bf16[256,128]{1,0:T(8,128)(2,1)S(1)} %get-tuple-element.178), channel_id=1, source_target_pairs={{0,8},{4,12},{8,0},{12,4},{16,24},{20,28},{24,16},{28,20},{1,9},{5... | collective-permute-start | bytes 196616 | tf_op jit(solution)/shard_map/ppermute | solution.py:328
  71.9 9.1 %collective-permute-start.17 = (bf16[256,128]{1,0:T(8,128)(2,1)S(1)}, bf16[256,128]{1,0:T(8,128)(2,1)S(1)}, u32[]{:S(2)}, u32[]{:S(2)}) collective-permute-start(bf16[256,128]{1,0:T(8,128)(2,1)S(1)} %get-tuple-element.179), channel_id=1, source_target_pairs={{0,4},{4,0},{8,12},{12,8},{16,20},{20,16},{24,28},{28,24},{1,5},{5... | collective-permute-start | bytes 196616 | tf_op jit(solution)/shard_map/ppermute | solution.py:328
  73.4 1.5 copy-start.10
  78.2 2.8 %copy-start.12 = (bf16[2,1024,128]{2,1,0:T(8,128)(2,1)S(1)}, bf16[2,1024,128]{2,1,0:T(8,128)(2,1)}, u32[]{:S(2)}) copy-start(bf16[2,1024,128]{2,1,0:T(8,128)(2,1)} %copy-done.11) | copy-start | bytes 1572868
  78.2 2.8 %copy-start.14 = (f32[128,1024]{1,0:T(8,128)S(1)}, f32[128,1024]{1,0:T(8,128)}, u32[]{:S(2)}) copy-start(f32[128,1024]{1,0:T(8,128)} %copy-done.13) | copy-start | bytes 1572868
  78.2 2.8 %copy-start.16 = (f32[2,1024]{1,0:T(2,128)S(1)}, f32[2,1024]{1,0:T(2,128)}, u32[]{:S(2)}) copy-start(f32[2,1024]{1,0:T(2,128)} %copy-done.15) | copy-start | bytes 24580
  79.9 14.7 %collective-permute-start.20 = (bf16[512,384]{1,0:T(8,128)(2,1)S(1)}, bf16[512,384]{1,0:T(8,128)(2,1)S(1)}, u32[]{:S(2)}, u32[]{:S(2)}) collective-permute-start(bf16[512,384]{1,0:T(8,128)(2,1)S(1)} %collective-permute-done.16.refs_9_), channel_id=1, source_target_pairs={{0,1},{1,0},{2,3},{3,2},{4,5},{5,4},{6,7},{7,6},{8,9},{9,8},{10,11... | collective-permute-start | bytes 1179656 | tf_op jit(solution)/shard_map/ppermute | solution.py:328
  79.9 17.6 %collective-permute-start.14 = (bf16[2,288,512]{2,1,0:T(8,128)(2,1)S(1)}, bf16[2,288,512]{2,1,0:T(8,128)(2,1)S(1)}, u32[]{:S(2)}, u32[]{:S(2)}) collective-permute-start(bf16[2,288,512]{2,1,0:T(8,128)(2,1)S(1)} %get-tuple-element.148), channel_id=1, source_target_pairs={{0,8},{4,12},{8,0},{12,4},{16,24},{20,28},{24,16},{28,20},{1,9},{5... | collective-permute-start | bytes 1769480 | tf_op jit(solution)/shard_map/ppermute | solution.py:328
  80.0 17.5 %collective-permute-start.13 = (bf16[2,288,512]{2,1,0:T(8,128)(2,1)S(1)}, bf16[2,288,512]{2,1,0:T(8,128)(2,1)S(1)}, u32[]{:S(2)}, u32[]{:S(2)}) collective-permute-start(bf16[2,288,512]{2,1,0:T(8,128)(2,1)S(1)} %get-tuple-element.150), channel_id=1, source_target_pairs={{0,4},{4,0},{8,12},{12,8},{16,20},{20,16},{24,28},{28,24},{1,5},{5... | collective-permute-start | bytes 1769480 | tf_op jit(solution)/shard_map/ppermute | solution.py:328
  88.9 17.1 %collective-permute-start.21 = (bf16[1024,256]{1,0:T(8,128)(2,1)S(1)}, bf16[1024,256]{1,0:T(8,128)(2,1)S(1)}, u32[]{:S(2)}, u32[]{:S(2)}) collective-permute-start(bf16[1024,256]{1,0:T(8,128)(2,1)S(1)} %get-tuple-element.93), channel_id=1, source_target_pairs={{0,16},{2,18},{4,20},{6,22},{8,24},{10,26},{12,28},{14,30},{16,0},... | collective-permute-start | bytes 1572872 | tf_op jit(solution)/shard_map/ppermute | solution.py:387
  94.2 20.5 %collective-permute-start.23 = (bf16[2,288,512]{2,1,0:T(8,128)(2,1)S(1)}, bf16[2,288,512]{2,1,0:T(8,128)(2,1)S(1)}, u32[]{:S(2)}, u32[]{:S(2)}) collective-permute-start(bf16[2,288,512]{2,1,0:T(8,128)(2,1)S(1)} %get-tuple-element.149), channel_id=1, source_target_pairs={{0,12},{4,8},{8,4},{12,0},{16,28},{20,24},{24,20},{28,16},{1,13},{... | collective-permute-start | bytes 1769480 | tf_op jit(solution)/shard_map/ppermute | solution.py:328
  106.0 1.2 copy-start.9
  108.7 4.3 %collective-permute-start.22 = (bf16[256,384]{1,0:T(8,128)(2,1)S(1)}, bf16[256,384]{1,0:T(8,128)(2,1)S(1)}, u32[]{:S(2)}, u32[]{:S(2)}) collective-permute-start(bf16[256,384]{1,0:T(8,128)(2,1)S(1)} %get-tuple-element.95), channel_id=1, source_target_pairs={{0,1},{1,0},{2,3},{3,2},{4,5},{5,4},{6,7},{7,6},{8,9},{9,8},{10,11... | collective-permute-start | bytes 589832 | tf_op jit(solution)/shard_map/ppermute | solution.py:328
  108.9 10.0 %collective-permute-start.26 = (bf16[256,384]{1,0:T(8,128)(2,1)S(1)}, bf16[256,384]{1,0:T(8,128)(2,1)S(1)}, u32[]{:S(2)}, u32[]{:S(2)}) collective-permute-start(bf16[256,384]{1,0:T(8,128)(2,1)S(1)} %get-tuple-element.167), channel_id=1, source_target_pairs={{0,12},{4,8},{8,4},{12,0},{16,28},{20,24},{24,20},{28,16},{1,13},{... | collective-permute-start | bytes 589832 | tf_op jit(solution)/shard_map/ppermute | solution.py:328
  112.3 10.3 %collective-permute-start.24 = (bf16[256,384]{1,0:T(8,128)(2,1)S(1)}, bf16[256,384]{1,0:T(8,128)(2,1)S(1)}, u32[]{:S(2)}, u32[]{:S(2)}) collective-permute-start(bf16[256,384]{1,0:T(8,128)(2,1)S(1)} %get-tuple-element.169), channel_id=1, source_target_pairs={{0,4},{4,0},{8,12},{12,8},{16,20},{20,16},{24,28},{28,24},{1,5},{5... | collective-permute-start | bytes 589832 | tf_op jit(solution)/shard_map/ppermute | solution.py:328
  113.1 14.1 %collective-permute-start.25 = (bf16[256,384]{1,0:T(8,128)(2,1)S(1)}, bf16[256,384]{1,0:T(8,128)(2,1)S(1)}, u32[]{:S(2)}, u32[]{:S(2)}) collective-permute-start(bf16[256,384]{1,0:T(8,128)(2,1)S(1)} %get-tuple-element.170), channel_id=1, source_target_pairs={{0,8},{4,12},{8,0},{12,4},{16,24},{20,28},{24,16},{28,20},{1,9},{5... | collective-permute-start | bytes 589832 | tf_op jit(solution)/shard_map/ppermute | solution.py:328
  116.1 15.1 %collective-permute-start.27 = (bf16[288,512]{1,0:T(8,128)(2,1)S(1)}, bf16[288,512]{1,0:T(8,128)(2,1)S(1)}, u32[]{:S(2)}, u32[]{:S(2)}) collective-permute-start(bf16[288,512]{1,0:T(8,128)(2,1)S(1)} %get-tuple-element.172), channel_id=1, source_target_pairs={{0,16},{4,20},{8,24},{12,28},{16,0},{20,4},{24,8},{28,12},{1,17},{... | collective-permute-start | bytes 884744 | tf_op jit(solution)/shard_map/ppermute | solution.py:328
  131.2 17.2 %copy-start.19 = (bf16[288,512]{1,0:T(8,128)(2,1)}, bf16[288,512]{1,0:T(8,128)(2,1)S(1)}, u32[]{:S(2)}) copy-start(bf16[288,512]{1,0:T(8,128)(2,1)S(1)} %collective-permute-done.27) | copy-start | bytes 884740
  131.2 1.2 collective-permute-start.28
  132.4 12.8 %collective-permute-start.29 = (bf16[304,512]{1,0:T(8,128)(2,1)S(1)}, bf16[304,512]{1,0:T(8,128)(2,1)S(1)}, u32[]{:S(2)}, u32[]{:S(2)}) collective-permute-start(bf16[304,512]{1,0:T(8,128)(2,1)S(1)} %pad_maximum_fusion.8), channel_id=1, source_target_pairs={{0,2},{1,3},{2,0},{3,1},{4,6},{5,7},{6,4},{7,5},{8,10},{9,11},{10,... | collective-permute-start | bytes 933896 | tf_op jit(solution)/shard_map/ppermute | solution.py:328
  133.5 11.8 %collective-permute-start.33 = (bf16[256,384]{1,0:T(8,128)(2,1)S(1)}, bf16[256,384]{1,0:T(8,128)(2,1)S(1)}, u32[]{:S(2)}, u32[]{:S(2)}) collective-permute-start(bf16[256,384]{1,0:T(8,128)(2,1)S(1)} %add_convert_fusion.4), channel_id=1, source_target_pairs={{0,16},{4,20},{8,24},{12,28},{16,0},{20,4},{24,8},{28,12},{1,17},{... | collective-permute-start | bytes 589832 | tf_op jit(solution)/shard_map/ppermute | solution.py:328
  146.2 14.2 %collective-permute-start.36 = (bf16[256,384]{1,0:T(8,128)(2,1)S(1)}, bf16[256,384]{1,0:T(8,128)(2,1)S(1)}, u32[]{:S(2)}, u32[]{:S(2)}) collective-permute-start(bf16[256,384]{1,0:T(8,128)(2,1)S(1)} %add_convert_fusion.3), channel_id=1, source_target_pairs={{0,12},{4,8},{8,4},{12,0},{16,28},{20,24},{24,20},{28,16},{1,13},{... | collective-permute-start | bytes 589832 | tf_op jit(solution)/shard_map/ppermute | solution.py:328
  146.2 15.2 %collective-permute-start.35 = (bf16[256,384]{1,0:T(8,128)(2,1)S(1)}, bf16[256,384]{1,0:T(8,128)(2,1)S(1)}, u32[]{:S(2)}, u32[]{:S(2)}) collective-permute-start(bf16[256,384]{1,0:T(8,128)(2,1)S(1)} %add_convert_fusion.3), channel_id=1, source_target_pairs={{0,8},{4,12},{8,0},{12,4},{16,24},{20,28},{24,16},{28,20},{1,9},{5... | collective-permute-start | bytes 589832 | tf_op jit(solution)/shard_map/ppermute | solution.py:328
  148.4 13.0 %collective-permute-start.34 = (bf16[256,384]{1,0:T(8,128)(2,1)S(1)}, bf16[256,384]{1,0:T(8,128)(2,1)S(1)}, u32[]{:S(2)}, u32[]{:S(2)}) collective-permute-start(bf16[256,384]{1,0:T(8,128)(2,1)S(1)} %add_convert_fusion.3), channel_id=1, source_target_pairs={{0,4},{4,0},{8,12},{12,8},{16,20},{20,16},{24,28},{28,24},{1,5},{5... | collective-permute-start | bytes 589832 | tf_op jit(solution)/shard_map/ppermute | solution.py:328
  149.7 15.5 %collective-permute-start.37 = (bf16[304,512]{1,0:T(8,128)(2,1)}, bf16[304,512]{1,0:T(8,128)(2,1)S(1)}, u32[]{:S(2)}, u32[]{:S(2)}) collective-permute-start(bf16[304,512]{1,0:T(8,128)(2,1)} %pad_maximum_fusion.9), channel_id=1, source_target_pairs={{0,16},{4,20},{8,24},{12,28},{16,0},{20,4},{24,8},{28,12},{1,17},{... | collective-permute-start | bytes 933896 | tf_op jit(solution)/shard_map/ppermute | solution.py:328
  149.7 17.0 %collective-permute-start.30 = (bf16[512,512]{1,0:T(8,128)(2,1)S(1)}, bf16[512,512]{1,0:T(8,128)(2,1)S(1)}, u32[]{:S(2)}, u32[]{:S(2)}) collective-permute-start(bf16[512,512]{1,0:T(8,128)(2,1)S(1)} %get-tuple-element.108), channel_id=1, source_target_pairs={{0,2},{1,3},{2,0},{3,1},{4,6},{5,7},{6,4},{7,5},{8,10},{9,11},{10,... | collective-permute-start | bytes 1572872 | tf_op jit(solution)/shard_map/ppermute | solution.py:328
  163.2 3.3 %copy-start.20 = (bf16[288,512]{1,0:T(8,128)(2,1)S(1)}, bf16[288,512]{1,0:T(8,128)(2,1)}, u32[]{:S(2)}) copy-start(bf16[288,512]{1,0:T(8,128)(2,1)} %copy-done.19) | copy-start | bytes 884740
  165.3 8.7 %collective-permute-start.38 = (bf16[2,256,384]{2,1,0:T(8,128)(2,1)S(1)}, bf16[2,256,384]{2,1,0:T(8,128)(2,1)S(1)}, u32[]{:S(2)}, u32[]{:S(2)}) collective-permute-start(bf16[2,256,384]{2,1,0:T(8,128)(2,1)S(1)} %pad_maximum_fusion.5), channel_id=1, source_target_pairs={{0,2},{1,3},{2,0},{3,1},{4,6},{5,7},{6,4},{7,5},{8,10},{9,11},{10,... | collective-permute-start | bytes 1179656 | tf_op jit(solution)/shard_map/ppermute | solution.py:328
  166.7 9.0 %collective-permute-start.31 = (bf16[512,512]{1,0:T(8,128)(2,1)S(1)}, bf16[512,512]{1,0:T(8,128)(2,1)S(1)}, u32[]{:S(2)}, u32[]{:S(2)}) collective-permute-start(bf16[512,512]{1,0:T(8,128)(2,1)S(1)} %get-tuple-element.108), channel_id=1, source_target_pairs={{0,1},{1,0},{2,3},{3,2},{4,5},{5,4},{6,7},{7,6},{8,9},{9,8},{10,11... | collective-permute-start | bytes 1572872 | tf_op jit(solution)/shard_map/ppermute | solution.py:328
  166.8 9.0 %collective-permute-start.32 = (bf16[512,512]{1,0:T(8,128)(2,1)S(1)}, bf16[512,512]{1,0:T(8,128)(2,1)S(1)}, u32[]{:S(2)}, u32[]{:S(2)}) collective-permute-start(bf16[512,512]{1,0:T(8,128)(2,1)S(1)} %collective-permute-done.30), channel_id=1, source_target_pairs={{0,1},{1,0},{2,3},{3,2},{4,5},{5,4},{6,7},{7,6},{8,9},{9,8},{10,11... | collective-permute-start | bytes 1572872 | tf_op jit(solution)/shard_map/ppermute | solution.py:328
  167.3 17.5 %collective-permute-start.42 = (bf16[592,512]{1,0:T(8,128)(2,1)S(1)}, bf16[592,512]{1,0:T(8,128)(2,1)S(1)}, u32[]{:S(2)}, u32[]{:S(2)}) collective-permute-start(bf16[592,512]{1,0:T(8,128)(2,1)S(1)} %pad_maximum_fusion.4.refs_1_), channel_id=1, source_target_pairs={{0,12},{4,8},{8,4},{12,0},{16,28},{20,24},{24,20},{28,16},{1,13},{... | collective-permute-start | bytes 1818632 | tf_op jit(solution)/shard_map/ppermute | solution.py:328
  167.4 29.8 %collective-permute-start.41 = (bf16[592,512]{1,0:T(8,128)(2,1)S(1)}, bf16[592,512]{1,0:T(8,128)(2,1)S(1)}, u32[]{:S(2)}, u32[]{:S(2)}) collective-permute-start(bf16[592,512]{1,0:T(8,128)(2,1)S(1)} %pad_maximum_fusion.4.refs_1_), channel_id=1, source_target_pairs={{0,8},{4,12},{8,0},{12,4},{16,24},{20,28},{24,16},{28,20},{1,9},{5... | collective-permute-start | bytes 1818632 | tf_op jit(solution)/shard_map/ppermute | solution.py:328
  174.0 23.3 %collective-permute-start.40 = (bf16[592,512]{1,0:T(8,128)(2,1)S(1)}, bf16[592,512]{1,0:T(8,128)(2,1)S(1)}, u32[]{:S(2)}, u32[]{:S(2)}) collective-permute-start(bf16[592,512]{1,0:T(8,128)(2,1)S(1)} %pad_maximum_fusion.4.refs_1_), channel_id=1, source_target_pairs={{0,4},{4,0},{8,12},{12,8},{16,20},{20,16},{24,28},{28,24},{1,5},{5... | collective-permute-start | bytes 1818632 | tf_op jit(solution)/shard_map/ppermute | solution.py:328
  175.7 4.9 %collective-permute-start.39 = (bf16[2,256,384]{2,1,0:T(8,128)(2,1)S(1)}, bf16[2,256,384]{2,1,0:T(8,128)(2,1)S(1)}, u32[]{:S(2)}, u32[]{:S(2)}) collective-permute-start(bf16[2,256,384]{2,1,0:T(8,128)(2,1)S(1)} %pad_maximum_fusion.7), channel_id=1, source_target_pairs={{0,1},{1,0},{2,3},{3,2},{4,5},{5,4},{6,7},{7,6},{8,9},{9,8},{10,11... | collective-permute-start | bytes 1179656 | tf_op jit(solution)/shard_map/ppermute | solution.py:328
  197.2 5.4 %copy-start.1 = (bf16[2,256,2,512]{3,2,1,0:T(2,128)(2,1)S(1)}, bf16[2,256,2,512]{3,2,1,0:T(2,128)(2,1)}, u32[]{:S(2)}) copy-start(bf16[2,256,2,512]{3,2,1,0:T(2,128)(2,1)} %param.13) | copy-start | bytes 3145732
  (7 other events, 5.4 us)

commit v3 on v2

--- a/solution.py
+++ b/solution.py
@@ -12,7 +12,7 @@
 BF = jnp.bfloat16
 F32 = jnp.float32
 VMEM_LIMIT = 50 * 1024 * 1024
-OPT = {}
+OPT = {"scale": 10}
 
 
 def tied(name, value, *deps, default=1):
@@ -66,7 +66,7 @@
         out_specs=[vspec()] * len(outs),
         scratch_shapes=list(scratch),
         compiler_params=pltpu.CompilerParams(vmem_limit_bytes=VMEM_LIMIT),
-        cost_estimate=pl.CostEstimate(flops=int(us * 1.1e9), bytes_accessed=0, transcendentals=0),
+        cost_estimate=pl.CostEstimate(flops=int(us * 1.1e9 * OPT.get("scale", 1)), bytes_accessed=0, transcendentals=0),
     )(scalars, *args, *after)
 
 
@@ -281,7 +281,7 @@
             send[...] = grad[(1 - n) * size:(2 - n) * size, :]
 
 
-def input_kernel(sc, x, dy, d0, d1, d2, d3, w0, w1, w2, w3, gain, bias, gains2, lout, pack, gains, w_s):
+def input_kernel(sc, x, dy, d0, d1, d2, d3, w0, w1, w2, w3, gain, bias, gains2, gin, gains, w_s):
     mats = (w0, w1, w2, w3)
     for e in range(4):
         w_s[e] = mats[e][...]
@@ -290,28 +290,21 @@
     da = jnp.zeros_like(hat)
     for k, ref in enumerate((d0, d1, d2, d3)):
         da = da + dot(ref[...], w_s[sc[0] ^ k], 1, 1)
-    n = x.shape[0]
-    pack[0:n, :] = (dy[...] + norm_back(da, hat, inv, gain_row)).astype(BF)
-    pack[n:2 * n, :] = lout[...]
+    gin[...] = (dy[...] + norm_back(da, hat, inv, gain_row)).astype(BF)
     gains[...] = jnp.zeros_like(gains)
     gains[0:1, :] = jnp.sum(da * hat, axis=0, keepdims=True)
     gains[1:2, :] = jnp.sum(da, axis=0, keepdims=True)
     gains[2:4, :] = gains2[...]
 
 
-def unpack_kernel(sc, p0, p1, p2, p3, up, down, out, gains):
-    total = jnp.zeros((RGAIN, 512), F32)
-    for k, src in enumerate((p0, p1, p2, p3)):
-        a = k ^ sc[2]
-        for rel in range(2):
-            net, row = sc[1] ^ rel, rel * ROWS
-            up[net, pl.ds(pl.multiple_of(a * RUP, RUP), RUP), :] = src[row:row + RUP, :].astype(F32)
-            down[net, pl.ds(pl.multiple_of(a * RDOWN, RDOWN), RDOWN), :] = src[row + RUP:row + RUP + RDOWN, :].astype(F32)
-            out[net, pl.ds(pl.multiple_of(a * ROUT, ROUT), ROUT), :] = src[row + RUP + RDOWN:row + ROWS, :].astype(F32)
-        total = total + src[2 * ROWS:2 * ROWS + RGAIN, :].astype(F32)
-    gains[sc[1]] = total[0:8, :]
-    gains[sc[1] ^ 1] = total[8:16, :]
-
+def unpack_kernel(sc, p0, p1, p2, p3, q0, q1, q2, q3, up, down, out):
+    for rel, parts in enumerate(((p0, p1, p2, p3), (q0, q1, q2, q3))):
+        net = sc[1] ^ rel
+        for k, src in enumerate(parts):
+            a = k ^ sc[2]
+            up[net, pl.ds(pl.multiple_of(a * RUP, RUP), RUP), :] = src[0:RUP, :].astype(F32)
+            down[net, pl.ds(pl.multiple_of(a * RDOWN, RDOWN), RDOWN), :] = src[RUP:RUP + RDOWN, :].astype(F32)
+            out[net, pl.ds(pl.multiple_of(a * ROUT, ROUT), ROUT), :] = src[RUP + RDOWN:ROWS, :].astype(F32)
 
 def unpack_heads_kernel(sc, mine, other, q, k, v):
     size = mine.shape[1]
@@ -449,56 +442,22 @@
         [((rows, 256), BF)] * (frames - 1) + [((2, rows, 128), BF), ((2, rows), F32), ((128, rows), F32)],
         tie(act, chip, head_c, head_y), [*dos, qm, ot, lse, *kvx],
         scratch=[pltpu.VMEM((128, rows), BF), pltpu.VMEM((rows, 128), F32), pltpu.VMEM((rows, 128), F32)], us=8, name="bx")
+    lout_y = across(tied("lo_y", lout, chip))
     dkv_x, (dom, delta, dqt) = back[:frames - 1], back[frames - 1:]
     dkv_far = [cross(dkv_x[r - 1], r) for r in range(1, frames)]
     dq, dkv_own = call(
         lambda *refs: back_own_kernel(qb, *refs),
-        [((rows, 128), BF), ((rows, 256), F32)], tie(act, group[1], group[2], dqt, head_yc), [qkv, qm, dom, lse, delta, dqt],
+        [((rows, 128), BF), ((rows, 256), F32)], tie(act, group[1], group[2], dqt, head_yc, lout_y), [qkv, qm, dom, lse, delta, dqt],
         scratch=[pltpu.VMEM((128, rows), F32), pltpu.VMEM((128, rows), BF), pltpu.VMEM((rows, 128), F32),
                  pltpu.VMEM((rows, 128), F32)], us=8, name="bo")
     total = dkv_own
     for far in dkv_far:
         total = total + far.astype(F32)
     dqkv = jnp.concatenate([dq, total.astype(BF)], axis=1)
-    ds = to_group(chunks_of(dqkv))
 
     keep_c, send_c = call(grads_heads_kernel, [((width // 2, 384), BF)] * 2, sc, [a, dqkv], us=2, name="kc")
     sum_c = add(keep_c, beside(send_c))
-    mine = add(group[0], *[tied("mine", part, sum_c) for part in group[1:]])
-    net_0 = mine[0]
-    bit = GROUP
-    got_0 = swap(net_0, "seq", seq, GROUP)
-    got_c = swap(tied("c_mine", sum_c, mine), "seq", seq, GROUP)
-
-    pack, gains = call(
-        input_kernel, [((2 * segment, width), BF), ((RGAIN, width), F32)],
-        tied("k5_m", sc, mine), [x, dy, *ds, *head, norm1_gain, norm1_bias, gains2, lout],
-        scratch=[pltpu.VMEM((4, width, 384), BF)], us=2, name="k5")
-    gains = tied('g_0', gains, got_0)
-    gains = add(gains, beside(gains))
-    cross_y = across(jnp.concatenate([mine[1], gains]))
-    gains = jnp.where(jnp.arange(RGAIN)[:, None] < 8, gains, jnp.roll(cross_y[ROWS:], 8, axis=0))
-    net_1 = jnp.concatenate([cross_y[:ROWS], gains])
-    pack = tied('pack_y', pack, cross_y)
-    pack_y = across(pack)
-    sum_c = add(sum_c, tied("c2_y", got_c, cross_y))
-    net_0 = add(net_0, tied("n0_y", got_0, cross_y))
-    got_1 = swap(net_1, "seq", seq, GROUP)
-    all_c = jnp.stack(to_group([tied('c_n1', sum_c, net_1)] * GROUP))
-    all_c = tied('c_g1', all_c, got_1)
-    net_1 = add(net_1, tied("n1_c", got_1, all_c, default=0))
-    bit = 2 * GROUP
-    while bit < seq:
-        sum_c, net_0, net_1 = [add(value, swap(value, "seq", seq, bit)) for value in (sum_c, net_0, net_1)]
-        bit *= 2
-    all_g = to_group([tied("ag_py", jnp.concatenate([net_0, net_1]), pack_y, default=0)] * GROUP)
-
-    def shard(number):
-        return lax.dynamic_index_in_dim(all_c, spot ^ number, 0, keepdims=False)
-
-    far_c = across(jnp.stack([shard(j ^ 2), shard(j ^ 3)]))
-    mine_c = jnp.stack([shard(j), far_c[0]])
-    other_c = beside(jnp.stack([shard(j ^ 1), far_c[1]]))
+    ds = to_group(chunks_of(tied('ds_c', dqkv, sum_c)))
 
     def spread(own, far, own_c, far_c):
         out = []
@@ -509,15 +468,57 @@
             out.append(jnp.stack([jnp.where(stream == s, mine_n, other_n) for s in range(2)], axis=1))
         return jnp.stack(out)
 
-    pack = tied('pack_y', pack, cross_y)
-    pack_y = across(pack)
-    packs = [pack, pack_y, beside(tied('pc', pack, pack_y)), beside(pack_y)]
-    input_grad = spread(*[part[:segment] for part in packs])
-    layer_out = spread(*[part[segment:] for part in packs])
+    layer_out = spread(lout, lout_y, beside(tied("lo_c", lout, dkv_own)), beside(tied("lo_yc", lout_y, dkv_own)))
+
+    got_c = swap(sum_c, "seq", seq, GROUP)
+    mine = add(group[0], *[tied("mine", part, sum_c) for part in group[1:]])
+    got_0 = swap(mine[0], "seq", seq, GROUP)
+    cross_y = across(mine[1])
+
+    gin, gains = call(
+        input_kernel, [((segment, width), BF), ((RGAIN, width), F32)],
+        tied("k5_lo", tied("k5_c", tied("k5_m", sc, mine), got_c), layer_out), [x, dy, *ds, *head, norm1_gain, norm1_bias, gains2],
+        scratch=[pltpu.VMEM((4, width, 384), BF)], us=2, name="k5")
+    sum_c = add(sum_c, got_c)
+    bit = 2 * GROUP
+    while bit < seq:
+        sum_c = add(sum_c, swap(sum_c, "seq", seq, bit))
+        bit *= 2
+    all_c = to_group([sum_c] * GROUP)
+    gains = over_frames(gains.astype(BF))
+    net_0 = add(mine[0], tied("n0_c", got_0, gains, cross_y, *all_c[1:]))
+    bit = 2 * GROUP
+    while bit < seq:
+        net_0 = add(net_0, swap(net_0, "seq", seq, bit))
+        bit *= 2
+    all_0 = to_group([jnp.concatenate([net_0, gains])] * GROUP)
+    got_1 = swap(tied("n1_a", cross_y, net_0), "seq", seq, GROUP)
+
+    def shard(number):
+        pick = spot ^ number
+        return jnp.where(pick == 0, all_c[0], jnp.where(pick == 1, all_c[1], jnp.where(pick == 2, all_c[2], all_c[3])))
+
+    far_c = across(jnp.stack([shard(j ^ 2), shard(j ^ 3)]))
+    mine_c = jnp.stack([shard(j), far_c[0]])
+    other_c = beside(jnp.stack([shard(j ^ 1), far_c[1]]))
+    net_1 = add(cross_y, tied("n1_0", got_1, other_c, *all_0[1:]))
+    bit = 2 * GROUP
+    while bit < seq:
+        net_1 = add(net_1, swap(net_1, "seq", seq, bit))
+        bit *= 2
+    all_1 = to_group([net_1] * GROUP)
+    gin = tied("gin_1", gin, net_1)
+    gin_y = across(gin)
+    input_grad = spread(gin, gin_y, beside(tied("gin_c", gin, gin_y)), beside(gin_y))
+    gains = sum(part[ROWS:].astype(F32) for part in all_0)
+    gains = tied("gains_1", gains, net_1)
+    gains = gains + beside(gains)
+    gains_y = across(gains)
+    gains = jnp.stack([jnp.where(net == n, gains, gains_y) for n in range(2)])
     gq, gk, gv = call(unpack_heads_kernel, [((2, 512, 128), F32)] * 3, sc, [mine_c, other_c], us=1, name="uc")
-    up, down, out, gains = call(
-        unpack_kernel, [((2, 512, 512), F32), ((2, 512, 512), F32), ((2, 128, 512), F32), ((2, 8, width), F32)],
-        tie(sc, gq, layer_out, input_grad), all_g, us=3, name="up")
+    up, down, out = call(
+        unpack_kernel, [((2, 512, 512), F32), ((2, 512, 512), F32), ((2, 128, 512), F32)],
+        tie(sc, gq, input_grad, gains), [*all_0, *all_1], us=3, name="up")
     return (layer_out, input_grad, gq, gk, gv, out, up, down, gains[:, 0], gains[:, 1], gains[:, 2], gains[:, 3])
 
 

time: 203 us -> 190 us (0.936)
  waiting for transfers between devices: 69 us -> 48.9 us
  starting transfers between devices: 50.7 us -> 59.5 us
    ppermute x39 -> x47, waiting for transfers between devices: 61 us -> 42.6 us  [swap(): return lax.ppermute(value, axis, [(n, n ^ bit) for n in range(size)])]
    ppermute x39 -> x47, starting transfers between devices: 35.7 us -> 44.6 us  [swap(): return lax.ppermute(value, axis, [(n, n ^ bit) for n in range(size)])]
    unnamed x69 -> x83, local copies, waits for them, and re-layouts: 16.5 us -> 13.6 us
  transfers between devices with their start and end apart: 43 -> 51, of which waited for: 19 -> 18; matrix products, arithmetic and copies ran while one was open for 8% -> 11% of each run, Pallas kernels for 20% -> 21%
where the time goes in v3:
time: 190 us
  starting transfers between devices  59.5 us (31%)
  Pallas kernels  50.7 us (27%)
  waiting for transfers between devices  48.9 us (26%)
  local copies, waits for them, and re-layouts  22.5 us (12%)
  other arithmetic  4.51 us (2%)
  between operations  3.6 us (2%)
    pallas_call x11, Pallas kernels, call(): pl.pallas_call(run, out_shape=[jax.ShapeDtypeStruct(s, d) for s, d in out...  50.7 us
    ppermute x47, starting transfers between devices, swap(): return lax.ppermute(value, axis, [(n, n ^ bit) for n in range(size)])  44.6 us
    ppermute x47, waiting for transfers between devices, swap(): return lax.ppermute(value, axis, [(n, n ^ bit) for n in range(size)])  42.6 us
    unnamed x83, local copies, waits for them, and re-layouts  13.6 us
    ppermute x2, starting transfers between devices, cross(): return lax.ppermute(value, ('seq', 'tp'), pairs)  9.74 us
    ppermute x2, waiting for transfers between devices, cross(): return lax.ppermute(value, ('seq', 'tp'), pairs)  5.69 us
  transfers between devices with their start and end apart: 51, of which 18 were waited for; matrix products, arithmetic and copies ran while one was open for 11% of the time, Pallas kernels for 21%

profile of v3, /device:TPU:0, one launch (start us, length us, event | category | flops | bytes accessed | tf_op | source)
XLA Modules:
  0.0 189.6 jit_solution(8138141567159771618)
XLA Ops:
  0.7 1.4 slice.88
  3.4 4.0 %collective-permute-start.2 = (bf16[256,512]{1,0:T(8,128)(2,1)S(1)}, bf16[256,512]{1,0:T(8,128)(2,1)S(1)}, u32[]{:S(2)}, u32[]{:S(2)}) collective-permute-start(bf16[256,512]{1,0:T(8,128)(2,1)S(1)} %bitcast.97), channel_id=1, source_target_pairs={{0,12},{4,8},{8,4},{12,0},{16,28},{20,24},{24,20},{28,16},{1,13},{... | collective-permute-start | bytes 786440 | tf_op jit(solution)/shard_map/ppermute | solution.py:321
  8.3 3.8 %collective-permute-start.3 = (bf16[512,384]{1,0:T(8,128)(2,1)S(1)}, bf16[512,384]{1,0:T(8,128)(2,1)S(1)}, u32[]{:S(2)}, u32[]{:S(2)}) collective-permute-start(bf16[512,384]{1,0:T(8,128)(2,1)S(1)} %dynamic-slice_bitcast_fusion.2), channel_id=1, source_target_pairs={{0,2},{5,7},{10,8},{15,13},{16,18},{21,23},{26,24},{31,29}} | collective-permute-start | bytes 1179656 | tf_op jit(solution)/shard_map/ppermute | solution.py:385
  14.2 1.3 constant_dynamic-update-slice_fusion.5
  15.5 1.3 constant_dynamic-update-slice_fusion.4
  17.5 1.3 collective-permute-start.4
  18.9 1.2 dynamic-slice_bitcast_fusion
  20.1 2.5 %collective-permute-start.10 = (bf16[1152,512]{1,0:T(8,128)(2,1)}, bf16[1152,512]{1,0:T(8,128)(2,1)}, u32[]{:S(2)}, u32[]{:S(2)}) collective-permute-start(bf16[1152,512]{1,0:T(8,128)(2,1)} %get-tuple-element.77), channel_id=1, source_target_pairs={{0,2},{1,3},{2,0},{3,1},{4,6},{5,7},{6,4},{7,5},{8,10},{9,11},{10,... | collective-permute-start | bytes 3538952 | tf_op jit(solution)/shard_map/ppermute | solution.py:321
  22.6 1.9 %shard_map.220 = (bf16[1024,384]{1,0:T(8,128)(2,1)S(1)}, bf16[1024,512]{1,0:T(8,128)(2,1)S(1)}) custom-call(s32[5]{0:T(128)S(1)} %concatenate.15.refs_0_, bf16[256,512]{1,0:T(8,128)(2,1)S(1)} %bitcast.100, bf16[256,512]{1,0:T(8,128)(2,1)S(1)} %collective-permute-done.refs_2_, bf16[256,512]{1,0:T(8,128)(2,1)S(1)} %collective-permute-done.1.refs_3_, ...), custom_call_target="tpu_custom_call" | custom-call | flops 22000001024 | tf_op jit(solution)/shard_map/pallas_call | solution.py:62
  24.5 1.0 copy-done.17
  25.5 4.5 %collective-permute-start.5 = (bf16[1024,256]{1,0:T(8,128)(2,1)S(1)}, bf16[1024,256]{1,0:T(8,128)(2,1)S(1)}, u32[]{:S(2)}, u32[]{:S(2)}) collective-permute-start(bf16[1024,256]{1,0:T(8,128)(2,1)S(1)} %slice.89), channel_id=1, source_target_pairs={{0,16},{2,18},{4,20},{6,22},{8,24},{10,26},{12,28},{14,30},{16,0},... | collective-permute-start | bytes 1572872 | tf_op jit(solution)/shard_map/ppermute | solution.py:380
  30.0 6.8 %shard_map.221 = (bf16[2,1024,128]{2,1,0:T(8,128)(2,1)S(1)}, f32[2,1024]{1,0:T(2,128)S(1)}, f32[2,1024]{1,0:T(2,128)S(1)}, f32[128,1024]{1,0:T(8,128)S(1)}) custom-call(s32[2]{0:T(128)S(1)} %pad_add_fusion.refs_0_, bf16[1024,384]{1,0:T(8,128)(2,1)S(1)} %get-tuple-element.70.refs_1_), custom_call_target="tpu_custom_call" | custom-call | flops 76999999488 | tf_op jit(solution)/shard_map/pallas_call | solution.py:62
  36.9 5.7 %collective-permute-done.5.refs_5_.refs_8_ = bf16[1024,256]{1,0:T(8,128)(2,1)S(1)} collective-permute-done((bf16[1024,256]{1,0:T(8,128)(2,1)S(1)}, bf16[1024,256]{1,0:T(8,128)(2,1)S(1)}, u32[]{:S(2)}, u32[]{:S(2)}) %collective-permute-start.5) | collective-permute-done | bytes 524320 | tf_op jit(solution)/shard_map/ppermute | solution.py:380
  42.6 7.0 %shard_map.222 = (bf16[1024,128]{1,0:T(8,128)(2,1)S(1)}, f32[128,1024]{1,0:T(8,128)S(1)}, f32[2,1024]{1,0:T(2,128)S(1)}) custom-call(s32[2]{0:T(128)S(1)} %pad_add_fusion.refs_0_, bf16[2,1024,128]{2,1,0:T(8,128)(2,1)S(1)} %get-tuple-element.71.refs_1_.refs_5_.refs_2_, f32[2,1024]{1,0:T(2,128)S(1)} %get-tuple-element.72.refs_2_, ...), custom_call_target="tpu_custom_call" | custom-call | flops 76999999488 | tf_op jit(solution)/shard_map/pallas_call | solution.py:62
  50.2 3.2 %collective-permute-start.6 = (bf16[256,128]{1,0:T(8,128)(2,1)S(1)}, bf16[256,128]{1,0:T(8,128)(2,1)S(1)}, u32[]{:S(2)}, u32[]{:S(2)}) collective-permute-start(bf16[256,128]{1,0:T(8,128)(2,1)S(1)} %get-tuple-element.185), channel_id=1, source_target_pairs={{0,4},{4,0},{8,12},{12,8},{16,20},{20,16},{24,28},{28,24},{1,5},{5... | collective-permute-start | bytes 196616 | tf_op jit(solution)/shard_map/ppermute | solution.py:321
  53.4 2.3 %constant_dynamic-slice_fusion = (bf16[1,256,1,512]{3,2,1,0:T(2,128)(2,1)S(1)}, bf16[1,256,1,512]{3,2,1,0:T(2,128)(2,1)S(1)}) fusion(bf16[2,256,2,512]{3,2,1,0:T(2,128)(2,1)} %param.14, s32[]{:T(128)S(6)} %select_n.244, s32[]{:T(128)S(6)} %select_n.248, s32[]{:T(128)S(6)} %select_n.237), kind=kLoop, calls=%fused_computation.85 | loop fusion | bytes 1048588 | tf_op jit(solution)/shard_map/dynamic_slice | solution.py:341
  55.7 0.9 collective-permute-done.6.refs_4_
  56.7 8.4 %shard_map.223 = (bf16[4,256,128]{2,1,0:T(8,128)(2,1)S(1)}, bf16[256,512]{1,0:T(8,128)(2,1)S(1)}, bf16[256,3328]{1,0:T(8,128)(2,1)}, bf16[256,3328]{1,0:T(8,128)...) custom-call(s32[5]{0:T(128)S(1)} %concatenate.15.refs_0_, bf16[256,512]{1,0:T(8,128)(2,1)S(1)} %bitcast.101, ...), custom_call_target="tpu_custom_call" | custom-call | flops 88000004096 | tf_op jit(solution)/shard_map/pallas_call | solution.py:62
  66.4 1.2 collective-permute-start.20
  67.6 1.4 collective-permute-start.19
  69.0 1.0 collective-permute-start.18
  70.0 1.5 copy-done.21
  71.4 3.4 %shard_map.224 = bf16[4,2,288,512]{3,2,1,0:T(8,128)(2,1)} custom-call(s32[5]{0:T(128)S(1)} %concatenate.15.refs_0_, bf16[256,3328]{1,0:T(8,128)(2,1)S(1)} %copy-done.21, bf16[256,3328]{1,0:T(8,128)(2,1)S(1)} %collective-permute-done.12.refs_2_, bf16[256,512]{1,0:T(8,128)(2,1)S(1)} %bitcast.104, bf16[256,512]{1,0:T(8,128)(2,1)S(1)} %bitcast.105), custom_call_target="tpu_custom_call" | custom-call | flops 44000002048 | tf_op jit(solution)/shard_map/pallas_call | solution.py:62
  74.8 2.4 %slice_bitcast_fusion = (bf16[2,288,512]{2,1,0:T(8,128)(2,1)}, bf16[2,288,512]{2,1,0:T(8,128)(2,1)S(1)}, bf16[2,288,512]{2,1,0:T(8,128)(2,1)S(1)}) fusion(bf16[4,2,288,512]{3,2,1,0:T(8,128)(2,1)} %shard_map.224), kind=kLoop, calls=%fused_computation.10 | loop fusion | bytes 3538944 | tf_op jit(solution)/shard_map/squeeze | solution.py:439
  77.4 1.5 collective-permute-start.13
  78.9 1.1 collective-permute-start.14
  80.0 7.8 %shard_map.225 = (bf16[1024,256]{1,0:T(8,128)(2,1)S(1)}, bf16[2,1024,128]{2,1,0:T(8,128)(2,1)S(1)}, f32[2,1024]{1,0:T(2,128)S(1)}, f32[128,1024]{1,0:T(8,128)S(1)}) custom-call(s32[2]{0:T(128)S(1)} %pad_add_fusion.refs_0_, bf16[256,128]{1,0:T(8,128)(2,1)S(1)} %get-tuple-element.182.refs_1_, bf16[256,128]{1,0:T(8,128)(2,1)S(1)} %collective-permute-done.18.refs_2_, ...), custom_call_target="tpu_custom_call" | custom-call | flops 88000004096 | tf_op jit(solution)/shard_map/pallas_call | solution.py:62
  87.8 5.2 %collective-permute-start.24 = (bf16[1024,256]{1,0:T(8,128)(2,1)S(1)}, bf16[1024,256]{1,0:T(8,128)(2,1)S(1)}, u32[]{:S(2)}, u32[]{:S(2)}) collective-permute-start(bf16[1024,256]{1,0:T(8,128)(2,1)S(1)} %get-tuple-element.99), channel_id=1, source_target_pairs={{0,16},{2,18},{4,20},{6,22},{8,24},{10,26},{12,28},{14,30},{16,0},... | collective-permute-start | bytes 1572872 | tf_op jit(solution)/shard_map/ppermute | solution.py:380
  93.7 3.1 %collective-permute-done.15 = bf16[2,288,512]{2,1,0:T(8,128)(2,1)S(1)} collective-permute-done((bf16[2,288,512]{2,1,0:T(8,128)(2,1)S(1)}, bf16[2,288,512]{2,1,0:T(8,128)(2,1)S(1)}, u32[]{:S(2)}, u32[]{:S(2)}) %collective-permute-start.15) | collective-permute-done | bytes 589856 | tf_op jit(solution)/shard_map/ppermute | solution.py:321
  96.8 7.8 %shard_map.226 = (bf16[1024,128]{1,0:T(8,128)(2,1)S(1)}, f32[1024,256]{1,0:T(8,128)S(1)}) custom-call(s32[2]{0:T(128)S(1)} %pad_add_fusion.refs_0_, bf16[1024,384]{1,0:T(8,128)(2,1)S(1)} %copy-done.6, bf16[2,1024,128]{2,1,0:T(8,128)(2,1)S(1)} %copy-done.23, bf16[2,1024,128]{2,1,0:T(8,128)(2,1)S(1)} %get-tuple-element.92.refs_3_, ...), custom_call_target="tpu_custom_call" | custom-call | flops 88000004096 | tf_op jit(solution)/shard_map/pallas_call | solution.py:62
  104.9 1.0 copy-done.18
  105.9 1.3 shard_map.227
  107.9 0.9 collective-permute-done.25
  108.9 1.0 add_convert_fusion.4
  109.8 3.2 %collective-permute-start.27 = (bf16[256,384]{1,0:T(8,128)(2,1)S(1)}, bf16[256,384]{1,0:T(8,128)(2,1)S(1)}, u32[]{:S(2)}, u32[]{:S(2)}) collective-permute-start(bf16[256,384]{1,0:T(8,128)(2,1)S(1)} %add_convert_fusion.4), channel_id=1, source_target_pairs={{0,16},{4,20},{8,24},{12,28},{16,0},{20,4},{24,8},{28,12},{1,17},{... | collective-permute-start | bytes 589832 | tf_op jit(solution)/shard_map/ppermute | solution.py:321
  113.4 1.9 %fusion.2 = bf16[2,288,512]{2,1,0:T(8,128)(2,1)S(1)} fusion(bf16[2,288,512]{2,1,0:T(8,128)(2,1)} %collective-permute-done.26, bf16[2,288,512]{2,1,0:T(8,128)(2,1)} %copy-done.26, bf16[2,288,512]{2,1,0:T(8,128)(2,1)} %copy-done.27, bf16[4,2,288,512]{3,2,1,0:T(8,128)(2,1)} %shard_map.224), kind=kLoop, calls=%fused_computation.3 | loop fusion | flops 2359296 | bytes 2949120 | tf_op jit(solution)/shard_map/convert_element_type | solution.py:424
  115.4 0.9 collective-permute-start.30
  116.3 1.7 collective-permute-start.29
  118.0 1.0 collective-permute-start.28
  119.4 3.2 %collective-permute-done.27 = bf16[256,384]{1,0:T(8,128)(2,1)S(1)} collective-permute-done((bf16[256,384]{1,0:T(8,128)(2,1)S(1)}, bf16[256,384]{1,0:T(8,128)(2,1)S(1)}, u32[]{:S(2)}, u32[]{:S(2)}) %collective-permute-start.27) | collective-permute-done | bytes 196640 | tf_op jit(solution)/shard_map/ppermute | solution.py:321
  122.7 2.4 %collective-permute-start.35 = (bf16[256,384]{1,0:T(8,128)(2,1)S(1)}, bf16[256,384]{1,0:T(8,128)(2,1)S(1)}, u32[]{:S(2)}, u32[]{:S(2)}) collective-permute-start(bf16[256,384]{1,0:T(8,128)(2,1)S(1)} %add_convert_fusion.3), channel_id=1, source_target_pairs={{0,8},{4,12},{8,0},{12,4},{16,24},{20,28},{24,16},{28,20},{1,9},{5... | collective-permute-start | bytes 589832 | tf_op jit(solution)/shard_map/ppermute | solution.py:321
  125.1 1.4 collective-permute-done.30.refs_6_
  126.5 1.0 collective-permute-start.34
  127.5 2.7 %collective-permute-done.29.refs_5_ = bf16[256,384]{1,0:T(8,128)(2,1)S(1)} collective-permute-done((bf16[256,384]{1,0:T(8,128)(2,1)S(1)}, bf16[256,384]{1,0:T(8,128)(2,1)S(1)}, u32[]{:S(2)}, u32[]{:S(2)}) %collective-permute-start.29) | collective-permute-done | bytes 196640 | tf_op jit(solution)/shard_map/ppermute | solution.py:321
  130.3 1.6 shard_map.228
  131.9 2.9 %collective-permute-start.33 = (bf16[16,512]{1,0:T(8,128)(2,1)S(1)}, bf16[16,512]{1,0:T(8,128)(2,1)S(1)}, u32[]{:S(2)}, u32[]{:S(2)}) collective-permute-start(bf16[16,512]{1,0:T(8,128)(2,1)S(1)} %convert_element_type.99), channel_id=1, source_target_pairs={{0,16},{4,20},{8,24},{12,28},{16,0},{20,4},{24,8},{28,12},{1,17},{... | collective-permute-start | bytes 49160 | tf_op jit(solution)/shard_map/ppermute | solution.py:321
  135.0 1.9 %collective-permute-done.33 = bf16[16,512]{1,0:T(8,128)(2,1)S(1)} collective-permute-done((bf16[16,512]{1,0:T(8,128)(2,1)S(1)}, bf16[16,512]{1,0:T(8,128)(2,1)S(1)}, u32[]{:S(2)}, u32[]{:S(2)}) %collective-permute-start.33) | collective-permute-done | bytes 16416 | tf_op jit(solution)/shard_map/ppermute | solution.py:321
  136.9 2.6 %collective-permute-done.35 = bf16[256,384]{1,0:T(8,128)(2,1)S(1)} collective-permute-done((bf16[256,384]{1,0:T(8,128)(2,1)S(1)}, bf16[256,384]{1,0:T(8,128)(2,1)S(1)}, u32[]{:S(2)}, u32[]{:S(2)}) %collective-permute-start.35) | collective-permute-done | bytes 196640 | tf_op jit(solution)/shard_map/ppermute | solution.py:321
  140.0 8.1 %collective-permute-done.32 = bf16[288,512]{1,0:T(8,128)(2,1)S(1)} collective-permute-done((bf16[288,512]{1,0:T(8,128)(2,1)S(1)}, bf16[288,512]{1,0:T(8,128)(2,1)S(1)}, u32[]{:S(2)}, u32[]{:S(2)}) %collective-permute-start.32) | collective-permute-done | bytes 294944 | tf_op jit(solution)/shard_map/ppermute | solution.py:321
  148.2 1.5 collective-permute-start.42
  149.8 1.0 collective-permute-start.41
  150.7 1.1 collective-permute-start.40
  152.3 2.7 %collective-permute-start.37 = (bf16[288,512]{1,0:T(8,128)(2,1)S(1)}, bf16[288,512]{1,0:T(8,128)(2,1)S(1)}, u32[]{:S(2)}, u32[]{:S(2)}) collective-permute-start(bf16[288,512]{1,0:T(8,128)(2,1)S(1)} %collective-permute-done.31), channel_id=1, source_target_pairs={{0,16},{4,20},{8,24},{12,28},{16,0},{20,4},{24,8},{28,12},{1,17},{... | collective-permute-start | bytes 884744 | tf_op jit(solution)/shard_map/ppermute | solution.py:321
  154.9 2.0 %copy.30 = bf16[2,256,2,512]{3,2,1,0:T(2,128)(2,1)} copy(bf16[2,256,2,512]{3,1,2,0:T(8,128)(2,1)S(1)} %pad_maximum_fusion) | data formatting | bytes 2097152
  157.0 7.7 %collective-permute-done.42.refs_4_ = bf16[304,512]{1,0:T(8,128)(2,1)S(1)} collective-permute-done((bf16[304,512]{1,0:T(8,128)(2,1)S(1)}, bf16[304,512]{1,0:T(8,128)(2,1)S(1)}, u32[]{:S(2)}, u32[]{:S(2)}) %collective-permute-start.42) | collective-permute-done | bytes 311328 | tf_op jit(solution)/shard_map/ppermute | solution.py:321
  164.6 4.4 %collective-permute-done.41.refs_3_ = bf16[304,512]{1,0:T(8,128)(2,1)S(1)} collective-permute-done((bf16[304,512]{1,0:T(8,128)(2,1)S(1)}, bf16[304,512]{1,0:T(8,128)(2,1)S(1)}, u32[]{:S(2)}, u32[]{:S(2)}) %collective-permute-start.41) | collective-permute-done | bytes 311328 | tf_op jit(solution)/shard_map/ppermute | solution.py:321
  169.3 1.8 collective-permute-start.50
  171.1 0.8 collective-permute-start.49
  171.9 1.0 collective-permute-start.48
  172.9 1.9 %collective-permute-start.43 = (bf16[256,512]{1,0:T(8,128)(2,1)S(1)}, bf16[256,512]{1,0:T(8,128)(2,1)S(1)}, u32[]{:S(2)}, u32[]{:S(2)}) collective-permute-start(bf16[256,512]{1,0:T(8,128)(2,1)S(1)} %get-tuple-element.117), channel_id=1, source_target_pairs={{0,2},{1,3},{2,0},{3,1},{4,6},{5,7},{6,4},{7,5},{8,10},{9,11},{10,... | collective-permute-start | bytes 786440 | tf_op jit(solution)/shard_map/ppermute | solution.py:321
  175.0 1.8 shard_map.229
  176.7 4.5 %collective-permute-done.43 = bf16[256,512]{1,0:T(8,128)(2,1)S(1)} collective-permute-done((bf16[256,512]{1,0:T(8,128)(2,1)S(1)}, bf16[256,512]{1,0:T(8,128)(2,1)S(1)}, u32[]{:S(2)}, u32[]{:S(2)}) %collective-permute-start.43) | collective-permute-done | bytes 262176 | tf_op jit(solution)/shard_map/ppermute | solution.py:321
  184.6 2.0 %copy.31 = bf16[2,256,2,512]{3,2,1,0:T(2,128)(2,1)} copy(bf16[2,256,2,512]{3,1,2,0:T(8,128)(2,1)S(1)} %pad_maximum_fusion.1) | data formatting | bytes 2097152
  186.6 3.0 %shard_map.230 = (f32[2,512,512]{2,1,0:T(8,128)}, f32[2,512,512]{2,1,0:T(8,128)}, f32[2,128,512]{2,1,0:T(8,128)}) custom-call(s32[5]{0:T(128)S(1)} %concatenate.15.refs_0_, bf16[304,512]{1,0:T(8,128)(2,1)S(1)} %pad_maximum_fusion.6.refs_1_, bf16[304,512]{1,0:T(8,128)(2,1)S(1)} %collective-permute-done.40.refs_2_, ...), custom_call_target="tpu_custom_call" | custom-call | flops 32999999488 | tf_op jit(solution)/shard_map/pallas_call | solution.py:62
  (175 shorter events, 12.6 us)
Async XLA Ops:
  3.3 8.9 %copy-start.34 = (s32[2,2]{1,0:T(2,128)S(1)}, s32[2,2]{1,0:T(2,128)}, u32[]{:S(2)}) copy-start(s32[2,2]{1,0:T(2,128)} %param.15) | copy-start | bytes 52
  3.4 19.1 %collective-permute-start.2 = (bf16[256,512]{1,0:T(8,128)(2,1)S(1)}, bf16[256,512]{1,0:T(8,128)(2,1)S(1)}, u32[]{:S(2)}, u32[]{:S(2)}) collective-permute-start(bf16[256,512]{1,0:T(8,128)(2,1)S(1)} %bitcast.97), channel_id=1, source_target_pairs={{0,12},{4,8},{8,4},{12,0},{16,28},{20,24},{24,20},{28,16},{1,13},{... | collective-permute-start | bytes 786440 | tf_op jit(solution)/shard_map/ppermute | solution.py:321
  7.4 15.1 %collective-permute-start.1 = (bf16[256,512]{1,0:T(8,128)(2,1)S(1)}, bf16[256,512]{1,0:T(8,128)(2,1)S(1)}, u32[]{:S(2)}, u32[]{:S(2)}) collective-permute-start(bf16[256,512]{1,0:T(8,128)(2,1)S(1)} %bitcast.98), channel_id=1, source_target_pairs={{0,8},{4,12},{8,0},{12,4},{16,24},{20,28},{24,16},{28,20},{1,9},{5... | collective-permute-start | bytes 786440 | tf_op jit(solution)/shard_map/ppermute | solution.py:321
  7.9 14.7 %collective-permute-start = (bf16[256,512]{1,0:T(8,128)(2,1)S(1)}, bf16[256,512]{1,0:T(8,128)(2,1)S(1)}, u32[]{:S(2)}, u32[]{:S(2)}) collective-permute-start(bf16[256,512]{1,0:T(8,128)(2,1)S(1)} %bitcast.99), channel_id=1, source_target_pairs={{0,4},{4,0},{8,12},{12,8},{16,20},{20,16},{24,28},{28,24},{1,5},{5... | collective-permute-start | bytes 786440 | tf_op jit(solution)/shard_map/ppermute | solution.py:321
  8.3 9.1 %collective-permute-start.3 = (bf16[512,384]{1,0:T(8,128)(2,1)S(1)}, bf16[512,384]{1,0:T(8,128)(2,1)S(1)}, u32[]{:S(2)}, u32[]{:S(2)}) collective-permute-start(bf16[512,384]{1,0:T(8,128)(2,1)S(1)} %dynamic-slice_bitcast_fusion.2), channel_id=1, source_target_pairs={{0,2},{5,7},{10,8},{15,13},{16,18},{21,23},{26,24},{31,29}} | collective-permute-start | bytes 1179656 | tf_op jit(solution)/shard_map/ppermute | solution.py:385
  17.5 5.1 %collective-permute-start.4 = (bf16[512,384]{1,0:T(8,128)(2,1)S(1)}, bf16[512,384]{1,0:T(8,128)(2,1)S(1)}, u32[]{:S(2)}, u32[]{:S(2)}) collective-permute-start(bf16[512,384]{1,0:T(8,128)(2,1)S(1)} %get-tuple-element.150), channel_id=1, source_target_pairs={{0,1},{2,3},{5,4},{7,6},{10,11},{8,9},{15,14},{13,12},{16,17},{18,... | collective-permute-start | bytes 1179656 | tf_op jit(solution)/shard_map/ppermute | solution.py:387
  20.1 29.6 %collective-permute-start.10 = (bf16[1152,512]{1,0:T(8,128)(2,1)}, bf16[1152,512]{1,0:T(8,128)(2,1)}, u32[]{:S(2)}, u32[]{:S(2)}) collective-permute-start(bf16[1152,512]{1,0:T(8,128)(2,1)} %get-tuple-element.77), channel_id=1, source_target_pairs={{0,2},{1,3},{2,0},{3,1},{4,6},{5,7},{6,4},{7,5},{8,10},{9,11},{10,... | collective-permute-start | bytes 3538952 | tf_op jit(solution)/shard_map/ppermute | solution.py:321
  25.5 11.3 %copy-start.5 = (bf16[1024,384]{1,0:T(8,128)(2,1)}, bf16[1024,384]{1,0:T(8,128)(2,1)S(1)}, u32[]{:S(2)}) copy-start(bf16[1024,384]{1,0:T(8,128)(2,1)S(1)} %get-tuple-element.70.refs_1_) | copy-start | bytes 2359300
  25.5 17.1 %collective-permute-start.5 = (bf16[1024,256]{1,0:T(8,128)(2,1)S(1)}, bf16[1024,256]{1,0:T(8,128)(2,1)S(1)}, u32[]{:S(2)}, u32[]{:S(2)}) collective-permute-start(bf16[1024,256]{1,0:T(8,128)(2,1)S(1)} %slice.89), channel_id=1, source_target_pairs={{0,16},{2,18},{4,20},{6,22},{8,24},{10,26},{12,28},{14,30},{16,0},... | collective-permute-start | bytes 1572872 | tf_op jit(solution)/shard_map/ppermute | solution.py:380
  36.8 12.8 %copy-start.22 = (bf16[2,1024,128]{2,1,0:T(8,128)(2,1)}, bf16[2,1024,128]{2,1,0:T(8,128)(2,1)S(1)}, u32[]{:S(2)}) copy-start(bf16[2,1024,128]{2,1,0:T(8,128)(2,1)S(1)} %get-tuple-element.71.refs_1_.refs_5_.refs_2_) | copy-start | bytes 1572868
  36.8 19.8 %collective-permute-start.9 = (bf16[1152,512]{1,0:T(8,128)(2,1)S(1)}, bf16[1152,512]{1,0:T(8,128)(2,1)}, u32[]{:S(2)}, u32[]{:S(2)}) collective-permute-start(bf16[1152,512]{1,0:T(8,128)(2,1)S(1)} %get-tuple-element.76.refs_7_), channel_id=1, source_target_pairs={{0,1},{1,0},{2,3},{3,2},{4,5},{5,4},{6,7},{7,6},{8,9},{9,8},{10,11... | collective-permute-start | bytes 3538952 | tf_op jit(solution)/shard_map/ppermute | solution.py:321
  49.7 7.0 %collective-permute-start.11 = (bf16[1152,512]{1,0:T(8,128)(2,1)}, bf16[1152,512]{1,0:T(8,128)(2,1)}, u32[]{:S(2)}, u32[]{:S(2)}) collective-permute-start(bf16[1152,512]{1,0:T(8,128)(2,1)} %collective-permute-done.10.refs_9_), channel_id=1, source_target_pairs={{0,1},{1,0},{2,3},{3,2},{4,5},{5,4},{6,7},{7,6},{8,9},{9,8},{10,11... | collective-permute-start | bytes 3538952 | tf_op jit(solution)/shard_map/ppermute | solution.py:321
  49.8 5.9 %collective-permute-start.8 = (bf16[256,128]{1,0:T(8,128)(2,1)S(1)}, bf16[256,128]{1,0:T(8,128)(2,1)S(1)}, u32[]{:S(2)}, u32[]{:S(2)}) collective-permute-start(bf16[256,128]{1,0:T(8,128)(2,1)S(1)} %get-tuple-element.183), channel_id=1, source_target_pairs={{0,12},{4,8},{8,4},{12,0},{16,28},{20,24},{24,20},{28,16},{1,13},{... | collective-permute-start | bytes 196616 | tf_op jit(solution)/shard_map/ppermute | solution.py:321
  49.9 5.9 %collective-permute-start.7 = (bf16[256,128]{1,0:T(8,128)(2,1)S(1)}, bf16[256,128]{1,0:T(8,128)(2,1)S(1)}, u32[]{:S(2)}, u32[]{:S(2)}) collective-permute-start(bf16[256,128]{1,0:T(8,128)(2,1)S(1)} %get-tuple-element.184), channel_id=1, source_target_pairs={{0,8},{4,12},{8,0},{12,4},{16,24},{20,28},{24,16},{28,20},{1,9},{5... | collective-permute-start | bytes 196616 | tf_op jit(solution)/shard_map/ppermute | solution.py:321
  50.2 6.4 %collective-permute-start.6 = (bf16[256,128]{1,0:T(8,128)(2,1)S(1)}, bf16[256,128]{1,0:T(8,128)(2,1)S(1)}, u32[]{:S(2)}, u32[]{:S(2)}) collective-permute-start(bf16[256,128]{1,0:T(8,128)(2,1)S(1)} %get-tuple-element.185), channel_id=1, source_target_pairs={{0,4},{4,0},{8,12},{12,8},{16,20},{20,16},{24,28},{28,24},{1,5},{5... | collective-permute-start | bytes 196616 | tf_op jit(solution)/shard_map/ppermute | solution.py:321
  56.6 9.2 %copy-start.3 = (bf16[512,384]{1,0:T(8,128)(2,1)S(1)}, bf16[512,384]{1,0:T(8,128)(2,1)}, u32[]{:S(2)}) copy-start(bf16[512,384]{1,0:T(8,128)(2,1)} %copy-done.2) | copy-start | bytes 1179652
  56.7 9.2 %copy-start.29 = (bf16[512,384]{1,0:T(8,128)(2,1)S(1)}, bf16[512,384]{1,0:T(8,128)(2,1)}, u32[]{:S(2)}) copy-start(bf16[512,384]{1,0:T(8,128)(2,1)} %copy-done.28) | copy-start | bytes 1179652
  65.0 12.3 %copy-start.7 = (bf16[256,512]{1,0:T(8,128)(2,1)}, bf16[256,512]{1,0:T(8,128)(2,1)S(1)}, u32[]{:S(2)}) copy-start(bf16[256,512]{1,0:T(8,128)(2,1)S(1)} %get-tuple-element.95) | copy-start | bytes 786436
  65.0 3.9 %collective-permute-start.12 = (bf16[256,3328]{1,0:T(8,128)(2,1)}, bf16[256,3328]{1,0:T(8,128)(2,1)S(1)}, u32[]{:S(2)}, u32[]{:S(2)}) collective-permute-start(bf16[256,3328]{1,0:T(8,128)(2,1)} %get-tuple-element.81), channel_id=1, source_target_pairs={{0,1},{1,0},{2,3},{3,2},{4,5},{5,4},{6,7},{7,6},{8,9},{9,8},{10,11... | collective-permute-start | bytes 5111816 | tf_op jit(solution)/shard_map/ppermute | solution.py:321
  65.8 11.5 %collective-permute-start.16 = (bf16[512,384]{1,0:T(8,128)(2,1)S(1)}, bf16[512,384]{1,0:T(8,128)(2,1)S(1)}, u32[]{:S(2)}, u32[]{:S(2)}) collective-permute-start(bf16[512,384]{1,0:T(8,128)(2,1)S(1)} %copy-done.3), channel_id=1, source_target_pairs={{0,1},{1,0},{2,3},{3,2},{4,5},{5,4},{6,7},{7,6},{8,9},{9,8},{10,11... | collective-permute-start | bytes 1179656 | tf_op jit(solution)/shard_map/ppermute | solution.py:321
  65.9 11.5 %collective-permute-start.17 = (bf16[512,384]{1,0:T(8,128)(2,1)S(1)}, bf16[512,384]{1,0:T(8,128)(2,1)S(1)}, u32[]{:S(2)}, u32[]{:S(2)}) collective-permute-start(bf16[512,384]{1,0:T(8,128)(2,1)S(1)} %copy-done.29), channel_id=1, source_target_pairs={{0,2},{1,3},{2,0},{3,1},{4,6},{5,7},{6,4},{7,5},{8,10},{9,11},{10,... | collective-permute-start | bytes 1179656 | tf_op jit(solution)/shard_map/ppermute | solution.py:321
  66.4 12.4 %collective-permute-start.20 = (bf16[256,128]{1,0:T(8,128)(2,1)S(1)}, bf16[256,128]{1,0:T(8,128)(2,1)S(1)}, u32[]{:S(2)}, u32[]{:S(2)}) collective-permute-start(bf16[256,128]{1,0:T(8,128)(2,1)S(1)} %get-tuple-element.179), channel_id=1, source_target_pairs={{0,12},{4,8},{8,4},{12,0},{16,28},{20,24},{24,20},{28,16},{1,13},{... | collective-permute-start | bytes 196616 | tf_op jit(solution)/shard_map/ppermute | solution.py:321
  67.6 11.3 %collective-permute-start.19 = (bf16[256,128]{1,0:T(8,128)(2,1)S(1)}, bf16[256,128]{1,0:T(8,128)(2,1)S(1)}, u32[]{:S(2)}, u32[]{:S(2)}) collective-permute-start(bf16[256,128]{1,0:T(8,128)(2,1)S(1)} %get-tuple-element.180), channel_id=1, source_target_pairs={{0,8},{4,12},{8,0},{12,4},{16,24},{20,28},{24,16},{28,20},{1,9},{5... | collective-permute-start | bytes 196616 | tf_op jit(solution)/shard_map/ppermute | solution.py:321
  69.0 11.0 %collective-permute-start.18 = (bf16[256,128]{1,0:T(8,128)(2,1)S(1)}, bf16[256,128]{1,0:T(8,128)(2,1)S(1)}, u32[]{:S(2)}, u32[]{:S(2)}) collective-permute-start(bf16[256,128]{1,0:T(8,128)(2,1)S(1)} %get-tuple-element.181), channel_id=1, source_target_pairs={{0,4},{4,0},{8,12},{12,8},{16,20},{20,16},{24,28},{28,24},{1,5},{5... | collective-permute-start | bytes 196616 | tf_op jit(solution)/shard_map/ppermute | solution.py:321
  77.4 10.4 %copy-start.9 = (bf16[512,384]{1,0:T(8,128)(2,1)}, bf16[512,384]{1,0:T(8,128)(2,1)S(1)}, u32[]{:S(2)}) copy-start(bf16[512,384]{1,0:T(8,128)(2,1)S(1)} %collective-permute-done.16.refs_8_) | copy-start | bytes 1179652
  77.4 15.7 %collective-permute-start.13 = (bf16[256,512]{1,0:T(8,128)(2,1)S(1)}, bf16[256,512]{1,0:T(8,128)(2,1)S(1)}, u32[]{:S(2)}, u32[]{:S(2)}) collective-permute-start(bf16[256,512]{1,0:T(8,128)(2,1)S(1)} %get-tuple-element.95), channel_id=1, source_target_pairs={{0,2},{1,3},{2,0},{3,1},{4,6},{5,7},{6,4},{7,5},{8,10},{9,11},{10,... | collective-permute-start | bytes 786440 | tf_op jit(solution)/shard_map/ppermute | solution.py:321
  78.9 14.8 %collective-permute-start.21 = (bf16[512,384]{1,0:T(8,128)(2,1)S(1)}, bf16[512,384]{1,0:T(8,128)(2,1)S(1)}, u32[]{:S(2)}, u32[]{:S(2)}) collective-permute-start(bf16[512,384]{1,0:T(8,128)(2,1)S(1)} %collective-permute-done.17.refs_9_), channel_id=1, source_target_pairs={{0,1},{1,0},{2,3},{3,2},{4,5},{5,4},{6,7},{7,6},{8,9},{9,8},{10,11... | collective-permute-start | bytes 1179656 | tf_op jit(solution)/shard_map/ppermute | solution.py:321
  78.9 18.0 %collective-permute-start.15 = (bf16[2,288,512]{2,1,0:T(8,128)(2,1)S(1)}, bf16[2,288,512]{2,1,0:T(8,128)(2,1)S(1)}, u32[]{:S(2)}, u32[]{:S(2)}) collective-permute-start(bf16[2,288,512]{2,1,0:T(8,128)(2,1)S(1)} %get-tuple-element.153), channel_id=1, source_target_pairs={{0,8},{4,12},{8,0},{12,4},{16,24},{20,28},{24,16},{28,20},{1,9},{5... | collective-permute-start | bytes 1769480 | tf_op jit(solution)/shard_map/ppermute | solution.py:321
  78.9 17.9 %collective-permute-start.14 = (bf16[2,288,512]{2,1,0:T(8,128)(2,1)S(1)}, bf16[2,288,512]{2,1,0:T(8,128)(2,1)S(1)}, u32[]{:S(2)}, u32[]{:S(2)}) collective-permute-start(bf16[2,288,512]{2,1,0:T(8,128)(2,1)S(1)} %get-tuple-element.154), channel_id=1, source_target_pairs={{0,4},{4,0},{8,12},{12,8},{16,20},{20,16},{24,28},{28,24},{1,5},{5... | collective-permute-start | bytes 1769480 | tf_op jit(solution)/shard_map/ppermute | solution.py:321
  79.9 16.9 %copy-start.6 = (bf16[1024,384]{1,0:T(8,128)(2,1)S(1)}, bf16[1024,384]{1,0:T(8,128)(2,1)}, u32[]{:S(2)}) copy-start(bf16[1024,384]{1,0:T(8,128)(2,1)} %copy-done.5) | copy-start | bytes 2359300
  87.8 16.8 %collective-permute-start.24 = (bf16[1024,256]{1,0:T(8,128)(2,1)S(1)}, bf16[1024,256]{1,0:T(8,128)(2,1)S(1)}, u32[]{:S(2)}, u32[]{:S(2)}) collective-permute-start(bf16[1024,256]{1,0:T(8,128)(2,1)S(1)} %get-tuple-element.99), channel_id=1, source_target_pairs={{0,16},{2,18},{4,20},{6,22},{8,24},{10,26},{12,28},{14,30},{16,0},... | collective-permute-start | bytes 1572872 | tf_op jit(solution)/shard_map/ppermute | solution.py:380
  93.1 20.3 %collective-permute-start.26 = (bf16[2,288,512]{2,1,0:T(8,128)(2,1)}, bf16[2,288,512]{2,1,0:T(8,128)(2,1)}, u32[]{:S(2)}, u32[]{:S(2)}) collective-permute-start(bf16[2,288,512]{2,1,0:T(8,128)(2,1)} %get-tuple-element.152), channel_id=1, source_target_pairs={{0,12},{4,8},{8,4},{12,0},{16,28},{20,24},{24,20},{28,16},{1,13},{... | collective-permute-start | bytes 1769480 | tf_op jit(solution)/shard_map/ppermute | solution.py:321
  107.2 1.6 collective-permute-start.25
  107.4 10.6 %collective-permute-start.22 = (bf16[256,512]{1,0:T(8,128)(2,1)S(1)}, bf16[256,512]{1,0:T(8,128)(2,1)S(1)}, u32[]{:S(2)}, u32[]{:S(2)}) collective-permute-start(bf16[256,512]{1,0:T(8,128)(2,1)S(1)} %copy-done.8), channel_id=1, source_target_pairs={{0,1},{1,0},{2,3},{3,2},{4,5},{5,4},{6,7},{7,6},{8,9},{9,8},{10,11... | collective-permute-start | bytes 786440 | tf_op jit(solution)/shard_map/ppermute | solution.py:321
  107.8 11.2 %collective-permute-start.23 = (bf16[256,512]{1,0:T(8,128)(2,1)S(1)}, bf16[256,512]{1,0:T(8,128)(2,1)S(1)}, u32[]{:S(2)}, u32[]{:S(2)}) collective-permute-start(bf16[256,512]{1,0:T(8,128)(2,1)S(1)} %collective-permute-done.13), channel_id=1, source_target_pairs={{0,1},{1,0},{2,3},{3,2},{4,5},{5,4},{6,7},{7,6},{8,9},{9,8},{10,11... | collective-permute-start | bytes 786440 | tf_op jit(solution)/shard_map/ppermute | solution.py:321
  109.8 12.7 %collective-permute-start.27 = (bf16[256,384]{1,0:T(8,128)(2,1)S(1)}, bf16[256,384]{1,0:T(8,128)(2,1)S(1)}, u32[]{:S(2)}, u32[]{:S(2)}) collective-permute-start(bf16[256,384]{1,0:T(8,128)(2,1)S(1)} %add_convert_fusion.4), channel_id=1, source_target_pairs={{0,16},{4,20},{8,24},{12,28},{16,0},{20,4},{24,8},{28,12},{1,17},{... | collective-permute-start | bytes 589832 | tf_op jit(solution)/shard_map/ppermute | solution.py:321
  115.4 11.1 %collective-permute-start.30 = (bf16[256,384]{1,0:T(8,128)(2,1)S(1)}, bf16[256,384]{1,0:T(8,128)(2,1)S(1)}, u32[]{:S(2)}, u32[]{:S(2)}) collective-permute-start(bf16[256,384]{1,0:T(8,128)(2,1)S(1)} %get-tuple-element.171), channel_id=1, source_target_pairs={{0,12},{4,8},{8,4},{12,0},{16,28},{20,24},{24,20},{28,16},{1,13},{... | collective-permute-start | bytes 589832 | tf_op jit(solution)/shard_map/ppermute | solution.py:321
  116.3 14.0 %collective-permute-start.29 = (bf16[256,384]{1,0:T(8,128)(2,1)S(1)}, bf16[256,384]{1,0:T(8,128)(2,1)S(1)}, u32[]{:S(2)}, u32[]{:S(2)}) collective-permute-start(bf16[256,384]{1,0:T(8,128)(2,1)S(1)} %get-tuple-element.172), channel_id=1, source_target_pairs={{0,8},{4,12},{8,0},{12,4},{16,24},{20,28},{24,16},{28,20},{1,9},{5... | collective-permute-start | bytes 589832 | tf_op jit(solution)/shard_map/ppermute | solution.py:321
  118.0 12.3 %collective-permute-start.28 = (bf16[256,384]{1,0:T(8,128)(2,1)S(1)}, bf16[256,384]{1,0:T(8,128)(2,1)S(1)}, u32[]{:S(2)}, u32[]{:S(2)}) collective-permute-start(bf16[256,384]{1,0:T(8,128)(2,1)S(1)} %get-tuple-element.173), channel_id=1, source_target_pairs={{0,4},{4,0},{8,12},{12,8},{16,20},{20,16},{24,28},{28,24},{1,5},{5... | collective-permute-start | bytes 589832 | tf_op jit(solution)/shard_map/ppermute | solution.py:321
  119.2 11.0 %copy-start.4 = (bf16[512,384]{1,0:T(8,128)(2,1)S(1)}, bf16[512,384]{1,0:T(8,128)(2,1)}, u32[]{:S(2)}) copy-start(bf16[512,384]{1,0:T(8,128)(2,1)} %copy-done.2) | copy-start | bytes 1179652
  119.2 11.0 %copy-start.10 = (bf16[512,384]{1,0:T(8,128)(2,1)S(1)}, bf16[512,384]{1,0:T(8,128)(2,1)}, u32[]{:S(2)}) copy-start(bf16[512,384]{1,0:T(8,128)(2,1)} %copy-done.9) | copy-start | bytes 1179652
  119.2 11.0 %copy-start.14 = (f32[2,512]{1,0:T(2,128)S(1)}, f32[2,512]{1,0:T(2,128)}, u32[]{:S(2)}) copy-start(f32[2,512]{1,0:T(2,128)} %refs_11_.3) | copy-start | bytes 12292
  119.2 11.0 %copy-start.16 = (f32[2,512]{1,0:T(2,128)S(1)}, f32[2,512]{1,0:T(2,128)}, u32[]{:S(2)}) copy-start(f32[2,512]{1,0:T(2,128)} %refs_12_.3) | copy-start | bytes 12292
  119.2 11.0 %copy-start.20 = (f32[256,512]{1,0:T(8,128)S(1)}, f32[256,512]{1,0:T(8,128)}, u32[]{:S(2)}) copy-start(f32[256,512]{1,0:T(8,128)} %copy-done.19) | copy-start | bytes 1572868
  122.6 14.4 %collective-permute-start.36 = (bf16[256,384]{1,0:T(8,128)(2,1)S(1)}, bf16[256,384]{1,0:T(8,128)(2,1)S(1)}, u32[]{:S(2)}, u32[]{:S(2)}) collective-permute-start(bf16[256,384]{1,0:T(8,128)(2,1)S(1)} %add_convert_fusion.3), channel_id=1, source_target_pairs={{0,12},{4,8},{8,4},{12,0},{16,28},{20,24},{24,20},{28,16},{1,13},{... | collective-permute-start | bytes 589832 | tf_op jit(solution)/shard_map/ppermute | solution.py:321
  122.7 16.8 %collective-permute-start.35 = (bf16[256,384]{1,0:T(8,128)(2,1)S(1)}, bf16[256,384]{1,0:T(8,128)(2,1)S(1)}, u32[]{:S(2)}, u32[]{:S(2)}) collective-permute-start(bf16[256,384]{1,0:T(8,128)(2,1)S(1)} %add_convert_fusion.3), channel_id=1, source_target_pairs={{0,8},{4,12},{8,0},{12,4},{16,24},{20,28},{24,16},{28,20},{1,9},{5... | collective-permute-start | bytes 589832 | tf_op jit(solution)/shard_map/ppermute | solution.py:321
  126.5 13.1 %collective-permute-start.34 = (bf16[256,384]{1,0:T(8,128)(2,1)S(1)}, bf16[256,384]{1,0:T(8,128)(2,1)S(1)}, u32[]{:S(2)}, u32[]{:S(2)}) collective-permute-start(bf16[256,384]{1,0:T(8,128)(2,1)S(1)} %add_convert_fusion.3), channel_id=1, source_target_pairs={{0,4},{4,0},{8,12},{12,8},{16,20},{20,16},{24,28},{28,24},{1,5},{5... | collective-permute-start | bytes 589832 | tf_op jit(solution)/shard_map/ppermute | solution.py:321
  131.9 5.0 %collective-permute-start.33 = (bf16[16,512]{1,0:T(8,128)(2,1)S(1)}, bf16[16,512]{1,0:T(8,128)(2,1)S(1)}, u32[]{:S(2)}, u32[]{:S(2)}) collective-permute-start(bf16[16,512]{1,0:T(8,128)(2,1)S(1)} %convert_element_type.99), channel_id=1, source_target_pairs={{0,16},{4,20},{8,24},{12,28},{16,0},{20,4},{24,8},{28,12},{1,17},{... | collective-permute-start | bytes 49160 | tf_op jit(solution)/shard_map/ppermute | solution.py:321
  134.8 13.3 %collective-permute-start.32 = (bf16[288,512]{1,0:T(8,128)(2,1)S(1)}, bf16[288,512]{1,0:T(8,128)(2,1)S(1)}, u32[]{:S(2)}, u32[]{:S(2)}) collective-permute-start(bf16[288,512]{1,0:T(8,128)(2,1)S(1)} %get-tuple-element.175), channel_id=1, source_target_pairs={{0,16},{4,20},{8,24},{12,28},{16,0},{20,4},{24,8},{28,12},{1,17},{... | collective-permute-start | bytes 884744 | tf_op jit(solution)/shard_map/ppermute | solution.py:321
  136.9 11.2 %collective-permute-start.31 = (bf16[288,512]{1,0:T(8,128)(2,1)S(1)}, bf16[288,512]{1,0:T(8,128)(2,1)S(1)}, u32[]{:S(2)}, u32[]{:S(2)}) collective-permute-start(bf16[288,512]{1,0:T(8,128)(2,1)S(1)} %get-tuple-element.176), channel_id=1, source_target_pairs={{0,2},{1,3},{2,0},{3,1},{4,6},{5,7},{6,4},{7,5},{8,10},{9,11},{10,... | collective-permute-start | bytes 884744 | tf_op jit(solution)/shard_map/ppermute | solution.py:321
  139.7 12.4 %collective-permute-start.38 = (bf16[2,256,384]{2,1,0:T(8,128)(2,1)S(1)}, bf16[2,256,384]{2,1,0:T(8,128)(2,1)S(1)}, u32[]{:S(2)}, u32[]{:S(2)}) collective-permute-start(bf16[2,256,384]{2,1,0:T(8,128)(2,1)S(1)} %pad_maximum_fusion.3), channel_id=1, source_target_pairs={{0,2},{1,3},{2,0},{3,1},{4,6},{5,7},{6,4},{7,5},{8,10},{9,11},{10,... | collective-permute-start | bytes 1179656 | tf_op jit(solution)/shard_map/ppermute | solution.py:321
  148.2 16.4 %collective-permute-start.42 = (bf16[304,512]{1,0:T(8,128)(2,1)S(1)}, bf16[304,512]{1,0:T(8,128)(2,1)S(1)}, u32[]{:S(2)}, u32[]{:S(2)}) collective-permute-start(bf16[304,512]{1,0:T(8,128)(2,1)S(1)} %pad_maximum_fusion.6.refs_1_), channel_id=1, source_target_pairs={{0,12},{4,8},{8,4},{12,0},{16,28},{20,24},{24,20},{28,16},{1,13},{... | collective-permute-start | bytes 933896 | tf_op jit(solution)/shard_map/ppermute | solution.py:321
  149.8 19.3 %collective-permute-start.41 = (bf16[304,512]{1,0:T(8,128)(2,1)S(1)}, bf16[304,512]{1,0:T(8,128)(2,1)S(1)}, u32[]{:S(2)}, u32[]{:S(2)}) collective-permute-start(bf16[304,512]{1,0:T(8,128)(2,1)S(1)} %pad_maximum_fusion.6.refs_1_), channel_id=1, source_target_pairs={{0,8},{4,12},{8,0},{12,4},{16,24},{20,28},{24,16},{28,20},{1,9},{5... | collective-permute-start | bytes 933896 | tf_op jit(solution)/shard_map/ppermute | solution.py:321
  150.7 18.3 %collective-permute-start.40 = (bf16[304,512]{1,0:T(8,128)(2,1)S(1)}, bf16[304,512]{1,0:T(8,128)(2,1)S(1)}, u32[]{:S(2)}, u32[]{:S(2)}) collective-permute-start(bf16[304,512]{1,0:T(8,128)(2,1)S(1)} %pad_maximum_fusion.6.refs_1_), channel_id=1, source_target_pairs={{0,4},{4,0},{8,12},{12,8},{16,20},{20,16},{24,28},{28,24},{1,5},{5... | collective-permute-start | bytes 933896 | tf_op jit(solution)/shard_map/ppermute | solution.py:321
  152.2 16.9 %collective-permute-start.39 = (bf16[2,256,384]{2,1,0:T(8,128)(2,1)S(1)}, bf16[2,256,384]{2,1,0:T(8,128)(2,1)S(1)}, u32[]{:S(2)}, u32[]{:S(2)}) collective-permute-start(bf16[2,256,384]{2,1,0:T(8,128)(2,1)S(1)} %pad_maximum_fusion.4), channel_id=1, source_target_pairs={{0,1},{1,0},{2,3},{3,2},{4,5},{5,4},{6,7},{7,6},{8,9},{9,8},{10,11... | collective-permute-start | bytes 1179656 | tf_op jit(solution)/shard_map/ppermute | solution.py:321
  152.3 16.8 %collective-permute-start.37 = (bf16[288,512]{1,0:T(8,128)(2,1)S(1)}, bf16[288,512]{1,0:T(8,128)(2,1)S(1)}, u32[]{:S(2)}, u32[]{:S(2)}) collective-permute-start(bf16[288,512]{1,0:T(8,128)(2,1)S(1)} %collective-permute-done.31), channel_id=1, source_target_pairs={{0,16},{4,20},{8,24},{12,28},{16,0},{20,4},{24,8},{28,12},{1,17},{... | collective-permute-start | bytes 884744 | tf_op jit(solution)/shard_map/ppermute | solution.py:321
  169.2 5.6 %collective-permute-start.46 = (f32[16,512]{1,0:T(8,128)S(1)}, f32[16,512]{1,0:T(8,128)S(1)}, u32[]{:S(2)}, u32[]{:S(2)}) collective-permute-start(f32[16,512]{1,0:T(8,128)S(1)} %convert_add_fusion.1), channel_id=1, source_target_pairs={{0,1},{1,0},{2,3},{3,2},{4,5},{5,4},{6,7},{7,6},{8,9},{9,8},{10,11... | collective-permute-start | bytes 98312 | tf_op jit(solution)/shard_map/ppermute | solution.py:321
  169.3 17.3 %collective-permute-start.50 = (bf16[288,512]{1,0:T(8,128)(2,1)S(1)}, bf16[288,512]{1,0:T(8,128)(2,1)S(1)}, u32[]{:S(2)}, u32[]{:S(2)}) collective-permute-start(bf16[288,512]{1,0:T(8,128)(2,1)S(1)} %add_convert_fusion.1.refs_5_), channel_id=1, source_target_pairs={{0,12},{4,8},{8,4},{12,0},{16,28},{20,24},{24,20},{28,16},{1,13},{... | collective-permute-start | bytes 884744 | tf_op jit(solution)/shard_map/ppermute | solution.py:321
  171.1 15.5 %collective-permute-start.49 = (bf16[288,512]{1,0:T(8,128)(2,1)S(1)}, bf16[288,512]{1,0:T(8,128)(2,1)S(1)}, u32[]{:S(2)}, u32[]{:S(2)}) collective-permute-start(bf16[288,512]{1,0:T(8,128)(2,1)S(1)} %add_convert_fusion.1.refs_5_), channel_id=1, source_target_pairs={{0,8},{4,12},{8,0},{12,4},{16,24},{20,28},{24,16},{28,20},{1,9},{5... | collective-permute-start | bytes 884744 | tf_op jit(solution)/shard_map/ppermute | solution.py:321
  171.9 14.7 %collective-permute-start.48 = (bf16[288,512]{1,0:T(8,128)(2,1)S(1)}, bf16[288,512]{1,0:T(8,128)(2,1)S(1)}, u32[]{:S(2)}, u32[]{:S(2)}) collective-permute-start(bf16[288,512]{1,0:T(8,128)(2,1)S(1)} %add_convert_fusion.1.refs_5_), channel_id=1, source_target_pairs={{0,4},{4,0},{8,12},{12,8},{16,20},{20,16},{24,28},{28,24},{1,5},{5... | collective-permute-start | bytes 884744 | tf_op jit(solution)/shard_map/ppermute | solution.py:321
  172.9 8.4 %collective-permute-start.43 = (bf16[256,512]{1,0:T(8,128)(2,1)S(1)}, bf16[256,512]{1,0:T(8,128)(2,1)S(1)}, u32[]{:S(2)}, u32[]{:S(2)}) collective-permute-start(bf16[256,512]{1,0:T(8,128)(2,1)S(1)} %get-tuple-element.117), channel_id=1, source_target_pairs={{0,2},{1,3},{2,0},{3,1},{4,6},{5,7},{6,4},{7,5},{8,10},{9,11},{10,... | collective-permute-start | bytes 786440 | tf_op jit(solution)/shard_map/ppermute | solution.py:321
  174.8 6.8 %collective-permute-start.47 = (f32[16,512]{1,0:T(8,128)S(1)}, f32[16,512]{1,0:T(8,128)S(1)}, u32[]{:S(2)}, u32[]{:S(2)}) collective-permute-start(f32[16,512]{1,0:T(8,128)S(1)} %add.103), channel_id=1, source_target_pairs={{0,2},{1,3},{2,0},{3,1},{4,6},{5,7},{6,4},{7,5},{8,10},{9,11},{10,... | collective-permute-start | bytes 98312 | tf_op jit(solution)/shard_map/ppermute | solution.py:321
  181.3 2.9 %collective-permute-start.44 = (bf16[256,512]{1,0:T(8,128)(2,1)S(1)}, bf16[256,512]{1,0:T(8,128)(2,1)S(1)}, u32[]{:S(2)}, u32[]{:S(2)}) collective-permute-start(bf16[256,512]{1,0:T(8,128)(2,1)S(1)} %get-tuple-element.117), channel_id=1, source_target_pairs={{0,1},{1,0},{2,3},{3,2},{4,5},{5,4},{6,7},{7,6},{8,9},{9,8},{10,11... | collective-permute-start | bytes 786440 | tf_op jit(solution)/shard_map/ppermute | solution.py:321
  181.6 2.6 %collective-permute-start.45 = (bf16[256,512]{1,0:T(8,128)(2,1)S(1)}, bf16[256,512]{1,0:T(8,128)(2,1)S(1)}, u32[]{:S(2)}, u32[]{:S(2)}) collective-permute-start(bf16[256,512]{1,0:T(8,128)(2,1)S(1)} %collective-permute-done.43), channel_id=1, source_target_pairs={{0,1},{1,0},{2,3},{3,2},{4,5},{5,4},{6,7},{7,6},{8,9},{9,8},{10,11... | collective-permute-start | bytes 786440 | tf_op jit(solution)/shard_map/ppermute | solution.py:321
  (22 other events, 102.8 us)
